TPU v7x, 32 devices: a whole 2x2x4 slice. The times are simulated.
32 devices in a mesh: groups: 2 (over y), dom: 4 (over z), sub: 2 (over x), chip: 2 (over core).
Axes of the slice: x: 2, y: 2, z: 4, core: 2. Of those that a mesh axis runs over, the one named last changes fastest.
Arguments:
- field_prev: float32 [16, 16384], P(('groups', 'dom', 'sub')), parts along dimension 0, may hold values from -6 to 6
- field_now: float32 [16, 16384], P(('groups', 'dom', 'sub')), parts along dimension 0, may hold values from -6 to 6
- adjoint_now: float32 [16, 16384], P(('groups', 'dom', 'sub')), parts along dimension 0, may hold values from -6 to 6
- adjoint_next: float32 [16, 16384], P(('groups', 'dom', 'sub')), parts along dimension 0, may hold values from -6 to 6
- inv_mass: float32 [16, 16384], P(('groups', 'dom', 'sub')), parts along dimension 0, may hold values from 0.02 to 0.2
- metric: float32 [2048, 1536], P(('groups', 'dom', 'sub', 'chip')), parts along dimension 0, may hold values from 0.25 to 4
- connect: int32 [2048, 512], P(('groups', 'dom', 'sub', 'chip')), parts along dimension 0, may hold values from 0 to 16383
- surface: float32 [2048, 512], P(('groups', 'dom', 'sub', 'chip')), parts along dimension 0, may hold values from 0.5 to 4
- driver: int32 [2048], P(('groups', 'dom', 'sub', 'chip')), parts along dimension 0, may hold values from 0 to 31
- shared: int32 [16, 3, 2, 512], P(('groups', 'dom', 'sub')), parts along dimension 0, may hold values from 0 to 16384, as said below
- filter_taps: float32 [8, 2048], P(None, ('dom', 'sub', 'chip')), may hold values from -0.125 to 0.125
- signal: float32 [2, 2048], replicated, may hold values from -6 to 6
Outputs:
- field_out: float32 [16, 16384], P(('groups', 'dom', 'sub')), parts along dimension 0
- adjoint_out: float32 [16, 16384], P(('groups', 'dom', 'sub')), parts along dimension 0
- filter_grad: float32 [16, 2048], P('groups', ('dom', 'sub', 'chip')), parts along dimension 0
There are 2 independent parts, one for each index of `groups`. A program takes and returns all parts, laid end to end along the dimension named above; an argument that names none is the same for every part. Nothing has to cross between parts.
Inputs may be any that keep to these rules, and one draw needn't show every extreme that they name: `connect`: local node numbers of the element's own partition. A value below 8 names the driver on whose surface the element lies; 8 or more means none. shared[p, o, j, :] lists the nodes that partition p shares with partition (d + o - 1) * 2 + j, live entries first, then the value 16384 in every empty slot. The list of p toward q and the list of q toward p hold the same number of live entries and pair position by position. Slots toward a dom index outside the grid and toward p itself are empty. A list holds at most 512 live entries, and in every dom layer some pair holds exactly 512.
All inputs are finite; a program needn't handle non-finite values.
Results may differ from a plain program's by a relative error of at most 0.0001.
Values sent between devices are 32-bit elements; how exact they have to be, the bound alone decides.
No kernel may reach another device: no remote copies, remote signals or barrier semaphores. Data moves between devices by JAX's collectives and lax.ppermute only.
A program may use at most 128 MiB of HBM per device.

v0:
```python
import math

import jax
import jax.numpy as jnp
import numpy as np
from jax import lax
from jax.sharding import PartitionSpec as P

ELEM_NODES = 512
STEPS = 2


GLL_POINTS = (
    -1.0,
    -0.8717401485096066,
    -0.5917001814331423,
    -0.2092992179024789,
    0.2092992179024789,
    0.5917001814331423,
    0.8717401485096066,
    1.0,
)
GLL_WEIGHTS = (
    0.03571428571428571,
    0.21070422714350603,
    0.3411226924835044,
    0.4124587946587038,
    0.4124587946587038,
    0.3411226924835044,
    0.21070422714350603,
    0.03571428571428571,
)


def from_behind(value, axis, by):
    size = lax.axis_size(axis)
    pairs = [(i, i + by) for i in range(size) if 0 <= i + by < size]
    return lax.ppermute(value, axis, pairs)


def element_tables():
    points = np.array(GLL_POINTS)
    identity = np.eye(8)
    diffs = points[:, None] - points[None, :] + identity
    barycentric = 1.0 / np.prod(diffs, axis=1)
    derivative = barycentric[None, :] / barycentric[:, None] / diffs
    derivative = derivative * (1.0 - identity)
    derivative = derivative - identity * derivative.sum(axis=1)[:, None]
    along_x = np.kron(np.kron(derivative, identity), identity)
    along_y = np.kron(np.kron(identity, derivative), identity)
    along_z = np.kron(identity, np.kron(identity, derivative))
    stacked = np.concatenate([along_x.T, along_y.T, along_z.T], axis=1)
    quad = np.array(GLL_WEIGHTS)
    cube = np.kron(np.kron(quad, quad), quad)
    return (
        jnp.asarray(stacked, dtype=jnp.float32),
        jnp.asarray(np.concatenate([cube, cube, cube]), dtype=jnp.float32),
    )


def on_device(
    field_prev,
    field_now,
    adjoint_now,
    adjoint_next,
    inv_mass,
    metric,
    connect,
    surface,
    driver,
    shared,
    filter_taps,
    signal,
):
    stacked, weights = element_tables()
    nodes = field_now.shape[1]
    count = connect.shape[0]
    peers = shared.shape[2]
    capacity = shared.shape[3]
    drivers = filter_taps.shape[0]
    width = filter_taps.shape[1]
    start = lax.axis_index(("dom", "sub", "chip")) * width
    own_signal = lax.dynamic_slice_in_dim(signal, start, width, 1)
    drive = lax.psum(
        jnp.dot(
            filter_taps,
            own_signal.T,
            precision=lax.Precision.HIGHEST,
            preferred_element_type=jnp.float32,
        ),
        ("dom", "sub", "chip"),
    )
    onehot = (driver[:, None] == jnp.arange(drivers, dtype=jnp.int32)[None, :]).astype(jnp.float32)
    scaled_metric = metric * weights[None, :]
    links = shared.reshape(-1)
    scale = 1.0 / math.sqrt(ELEM_NODES * count * lax.axis_size(("dom", "sub", "chip")))
    previous = jnp.concatenate([field_prev, adjoint_next], axis=0)
    current = jnp.concatenate([field_now, adjoint_now], axis=0)
    columns = []
    for step in range(STEPS):
        element_vals = current[:, connect]
        products = jnp.sum(surface * element_vals[1], axis=1)
        columns.append(scale * jnp.sum(onehot * products[:, None], axis=0))
        grads = jnp.dot(
            element_vals.reshape(-1, ELEM_NODES),
            stacked,
            precision=lax.Precision.HIGHEST,
            preferred_element_type=jnp.float32,
        )
        flux = grads.reshape(2, count, -1) * scaled_metric[None]
        back = jnp.dot(
            flux.reshape(2 * count, -1),
            stacked.T,
            precision=lax.Precision.HIGHEST,
            preferred_element_type=jnp.float32,
        ).reshape(2, count, ELEM_NODES)
        amplitude = jnp.sum(onehot * drive[:, step][None, :], axis=1)
        residual = jnp.stack([amplitude[:, None] * surface - back[0], -back[1]])
        local = jax.ops.segment_sum(
            residual.reshape(2, -1).T, connect.reshape(-1), num_segments=nodes
        ).T
        padded = jnp.concatenate([local, jnp.zeros((2, 1), jnp.float32)], axis=1)
        sent = padded[:, links].reshape(2, 3, peers, capacity)
        mixed = lax.all_to_all(sent, "sub", split_axis=2, concat_axis=2, tiled=True)
        from_below = from_behind(mixed[:, 2], "dom", 1)
        from_above = from_behind(mixed[:, 0], "dom", -1)
        received = jnp.stack([from_below, mixed[:, 1], from_above], axis=1)
        summed = padded.at[:, links].add(received.reshape(2, -1))[:, :nodes]
        total = lax.psum(summed, "chip")
        advanced = 2.0 * current - previous + inv_mass * total
        previous = current
        current = advanced
    coefficients = jnp.stack(columns[::-1], axis=1)
    terms = jnp.dot(
        coefficients, signal, precision=lax.Precision.HIGHEST, preferred_element_type=jnp.float32
    )
    filter_grad = lax.psum_scatter(terms, ("dom", "sub", "chip"), scatter_dimension=1, tiled=True)
    return (current[0:1], current[1:2], filter_grad)


def solution(mesh):
    in_specs = (
        P(("groups", "dom", "sub"), None),
        P(("groups", "dom", "sub"), None),
        P(("groups", "dom", "sub"), None),
        P(("groups", "dom", "sub"), None),
        P(("groups", "dom", "sub"), None),
        P(("groups", "dom", "sub", "chip"), None),
        P(("groups", "dom", "sub", "chip"), None),
        P(("groups", "dom", "sub", "chip"), None),
        P(("groups", "dom", "sub", "chip")),
        P(("groups", "dom", "sub"), None, None, None),
        P(None, ("dom", "sub", "chip")),
        P(),
    )
    out_specs = (
        P(("groups", "dom", "sub"), None),
        P(("groups", "dom", "sub"), None),
        P("groups", ("dom", "sub", "chip")),
    )
    return jax.shard_map(
        on_device, mesh=mesh, in_specs=in_specs, out_specs=out_specs, check_vma=False
    )
```

profile of v0, /device:TPU:0, one launch (start us, length us, event | category | flops | bytes accessed | tf_op | source)
XLA Modules:
  0.0 960.6 jit_solution(5080239763584957078)
XLA Ops:
  7.2 0.7 copy-done
  7.9 0.8 convolution_bitcast_fusion
  8.7 34.9 %psum.21 = f32[8,2]{0,1:T(2,128)S(1)} all-reduce(f32[8,2]{0,1:T(2,128)S(1)} %convolution_bitcast_fusion), channel_id=1, replica_groups=mesh['groups'=2,'dom'=4,'sub'=2,'chip'=2] {'dom','sub','chip'}, use_global_device_ids=true, to_apply=%region_0.0 | all-reduce | flops 16 | bytes 128 | tf_op jit(solution)/shard_map/psum | solution.py:84
  43.6 0.5 slice_bitcast_fusion.6
  44.1 0.7 reshape.133
  44.9 0.6 copy-done.13
  45.5 0.6 broadcast_clamp_fusion.1
  46.1 0.9 fusion.4
  47.0 1.6 copy.93
  48.7 1.0 pad_maximum_fusion
  49.7 5.0 copy.71
  54.7 111.6 %gather_fusion = f32[32768,2]{1,0:T(8,128)} fusion(f32[2,16384]{0,1:T(8,128)} %copy.71, s32[32768]{0:T(1024)S(1)} %broadcast_clamp_fusion), kind=kCustom, calls=%fused_computation | custom fusion | bytes 655360 | tf_op jit(solution)/shard_map/gather | solution.py:101
  166.3 10.8 %copy.72 = f32[64,512,2]{1,0,2:T(8,128)} copy(f32[64,512,2]{2,1,0:T(8,128)} %bitcast.97) | data formatting | bytes 524288 | tf_op jit(solution)/shard_map/gather | solution.py:101
  177.1 1.0 broadcast_multiply_fusion
  178.2 2.8 convolution_multiply_fusion.1
  180.9 5.2 fusion.24
  186.2 0.1 copy.95
  186.4 0.1 copy.96
  186.5 0.9 maximum_bitcast_fusion
  187.4 8.9 copy.73
  196.3 177.9 %scatter_custom_fusion = f32[16384,2]{1,0:T(8,128)} fusion(s32[32768]{0:T(1024)} %bitcast.117, f32[32768,2]{1,0:T(8,128)} %copy.73, f32[]{:T(128)} %constant.16.clone.1), kind=kCustom, calls=%fused_computation.10 | custom fusion | flops 65536 | bytes 131584 | tf_op jit(solution)/shard_map/scatter-add | solution.py:119
  374.2 7.7 concatenate.16
  381.9 15.3 %gather_fusion.1 = f32[3072,2]{1,0:T(8,128)} fusion(f32[2,16385]{0,1:T(8,128)} %concatenate.16, s32[3072]{0:T(1024)} %broadcast_clamp_fusion.1), kind=kCustom, calls=%fused_computation.1 | custom fusion | bytes 61440 | tf_op jit(solution)/shard_map/gather | solution.py:123
  397.2 2.5 copy.74
  399.7 7.1 all_to_all.10
  406.8 1.3 collective-permute-start
  408.1 1.5 collective-permute-start.1
  409.6 4.0 collective-permute-done.1
  413.6 0.6 pad_maximum_fusion.1
  414.3 2.5 copy.89
  416.7 27.6 %scatter_fusion = f32[2,16385]{0,1:T(8,128)} fusion(f32[2,16385]{0,1:T(8,128)} %concatenate.16, s32[3072]{0:T(1024)} %bitcast.115, f32[3072,2]{1,0:T(8,128)} %bitcast.103), kind=kCustom, calls=%fused_computation.5 | custom fusion | flops 6144 | bytes 86016 | tf_op jit(solution)/shard_map/scatter-add | solution.py:128
  444.3 5.7 slice.89
  450.0 5.9 copy.91
  456.0 15.3 %all-reduce.5.cloned.1.call-done = f32[2,16384]{1,0:T(2,128)} async-done(((f32[2,16384]{1,0:T(2,128)}), f32[2,16384]{1,0:T(2,128)}) %all-reduce.5.cloned.1.call-update) | async-done | bytes 131088 | tf_op jit(solution)/shard_map/psum | solution.py:129
  471.3 1.9 fusion.13
  473.2 5.6 copy.80
  478.8 122.1 %gather_fusion.2 = f32[32768,2]{1,0:T(8,128)} fusion(f32[2,16384]{0,1:T(8,128)} %copy.80, s32[32768]{0:T(1024)} %copy-done.4), kind=kCustom, calls=%fused_computation.2 | custom fusion | bytes 655360 | tf_op jit(solution)/shard_map/gather | solution.py:101
  600.9 10.6 %copy.81 = f32[64,512,2]{1,0,2:T(8,128)} copy(f32[64,512,2]{2,1,0:T(8,128)} %bitcast.96) | data formatting | bytes 524288 | tf_op jit(solution)/shard_map/gather | solution.py:101
  611.5 2.8 convolution_multiply_fusion
  614.3 5.2 fusion.25
  619.6 0.1 fusion.8
  619.7 0.1 select_reduce_fusion.1
  619.8 0.1 fusion.10
  619.9 0.1 copy.97
  620.1 0.1 copy.98
  620.2 0.2 maximum_bitcast_fusion.1
  620.5 8.3 copy.82
  628.8 177.9 %scatter_custom_fusion.2 = f32[16384,2]{1,0:T(8,128)} fusion(s32[32768]{0:T(1024)} %bitcast.118, f32[32768,2]{1,0:T(8,128)} %copy.82, f32[]{:T(128)} %constant.16.clone.1), kind=kCustom, calls=%fused_computation.8 | custom fusion | flops 65536 | bytes 131584 | tf_op jit(solution)/shard_map/scatter-add | solution.py:119
  806.7 7.7 concatenate.17
  814.4 11.5 %gather_fusion.3 = f32[3072,2]{1,0:T(8,128)S(1)} fusion(f32[2,16385]{0,1:T(8,128)} %concatenate.17, s32[3072]{0:T(1024)S(1)} %copy-done.15), kind=kCustom, calls=%fused_computation.3 | custom fusion | bytes 61440 | tf_op jit(solution)/shard_map/gather | solution.py:123
  825.9 0.5 copy.83
  826.4 6.7 all_to_all.11
  833.1 3.4 collective-permute-start.2
  836.5 1.5 collective-permute-start.3
  838.0 4.0 collective-permute-done.3
  842.0 0.5 copy.90
  842.6 27.2 %scatter_fusion.1 = f32[2,16385]{0,1:T(8,128)} fusion(f32[2,16385]{0,1:T(8,128)} %concatenate.17, s32[3072]{0:T(1024)S(1)} %bitcast.116, f32[3072,2]{1,0:T(8,128)S(1)} %bitcast.102), kind=kCustom, calls=%fused_computation.7 | custom fusion | flops 6144 | bytes 86016 | tf_op jit(solution)/shard_map/scatter-add | solution.py:128
  869.8 5.7 slice.95
  875.5 6.0 copy.92
  881.6 0.9 fusion.14
  882.5 14.6 %all-reduce.7.cloned.1.call-done = f32[2,16384]{1,0:T(2,128)} async-done(((f32[2,16384]{1,0:T(2,128)}), f32[2,16384]{1,0:T(2,128)}) %all-reduce.7.cloned.1.call-update) | async-done | bytes 131088 | tf_op jit(solution)/shard_map/psum | solution.py:129
  897.1 1.2 multiply_add_fusion
  898.3 0.8 fusion.23
  899.1 55.0 %reduce-scatter.2.cloned.1.call-done = f32[8,128]{1,0:T(8,128)} async-done(((f32[8,2048]{1,0:T(8,128)}), f32[8,128]{1,0:T(8,128)}) %reduce-scatter.2.cloned.1.call-update) | async-done | bytes 4112 | tf_op jit(solution)/shard_map/reduce_scatter | solution.py:137
  (59 shorter events, 0.5 us)
Async XLA Ops:
  7.2 0.7 copy-start
  7.2 464.1 %all-reduce.5.cloned.1.call-start = ((), (), s32[]{:S(2)}) async-start(), calls=%async_computation.3 | async-start | bytes 262144 | tf_op jit(solution)/shard_map/psum | solution.py:129
  44.9 0.6 copy-start.13
  48.6 117.6 %copy-start.4 = (s32[32768]{0:T(1024)}, s32[32768]{0:T(1024)S(1)}, u32[]{:S(2)}) copy-start(s32[32768]{0:T(1024)S(1)} %broadcast_clamp_fusion) | copy-start | bytes 393220
  166.2 10.8 %copy-start.17 = (s32[64]{0:T(128)S(1)}, s32[64]{0:T(128)}, u32[]{:S(2)}) copy-start(s32[64]{0:T(128)} %param.22) | copy-start | bytes 772
  166.2 11.9 %copy-start.1 = (f32[512,1536,1]{1,0,2:T(8,128)S(1)}, f32[512,1536,1]{1,0,2:T(8,128)}, u32[]{:S(2)}) copy-start(f32[512,1536,1]{1,0,2:T(8,128)} %constant.55) | copy-start | bytes 9437188
  177.0 9.1 copy-start.5
  406.8 2.8 collective-permute-start
  408.1 5.5 collective-permute-start.1
  455.9 441.2 %all-reduce.7.cloned.1.call-start = ((), (), s32[]{:S(2)}) async-start(), calls=%async_computation.4 | async-start | bytes 262144 | tf_op jit(solution)/shard_map/psum | solution.py:129
  611.5 8.0 copy-start.2
  611.5 8.1 copy-start.3
  611.5 8.1 copy-start.6
  611.5 8.2 copy-start.16
  611.5 8.2 copy-start.18
  806.7 7.7 copy-start.15
  806.7 35.9 %copy-start.14 = (s32[3072,1]{0,1:T(1,128)S(1)}, s32[3072,1]{0,1:T(1,128)}, u32[]{:S(2)}) copy-start(s32[3072,1]{0,1:T(1,128)} %copy-done.13) | copy-start | bytes 36868
  833.1 4.9 collective-permute-start.2
  836.5 5.5 collective-permute-start.3
  875.5 21.6 %copy-start.7 = (f32[1,16384]{1,0:T(1,128)S(1)}, f32[1,16384]{1,0:T(1,128)}, u32[]{:S(2)}) copy-start(f32[1,16384]{1,0:T(1,128)} %param.16) | copy-start | bytes 196612
  875.5 21.6 %copy-start.8 = (f32[1,16384]{1,0:T(1,128)S(1)}, f32[1,16384]{1,0:T(1,128)}, u32[]{:S(2)}) copy-start(f32[1,16384]{1,0:T(1,128)} %param.15) | copy-start | bytes 196612
  875.5 21.6 %copy-start.9 = (f32[2,16384]{1,0:T(2,128)S(1)}, f32[2,16384]{1,0:T(2,128)}, u32[]{:S(2)}) copy-start(f32[2,16384]{1,0:T(2,128)} %all-reduce.5.cloned.1.call-done) | copy-start | bytes 393220
  875.5 21.6 %copy-start.10 = (f32[1,16384]{1,0:T(1,128)S(1)}, f32[1,16384]{1,0:T(1,128)}, u32[]{:S(2)}) copy-start(f32[1,16384]{1,0:T(1,128)} %param.17) | copy-start | bytes 196612
  875.5 21.6 %copy-start.11 = (f32[1,16384]{1,0:T(1,128)S(1)}, f32[1,16384]{1,0:T(1,128)}, u32[]{:S(2)}) copy-start(f32[1,16384]{1,0:T(1,128)} %param.14) | copy-start | bytes 196612
  875.5 21.6 %copy-start.12 = (f32[1,16384]{1,0:T(1,128)S(1)}, f32[1,16384]{1,0:T(1,128)}, u32[]{:S(2)}) copy-start(f32[1,16384]{1,0:T(1,128)} %param.18) | copy-start | bytes 196612
  881.5 72.6 %reduce-scatter.2.cloned.1.call-start = ((), (), s32[]{:S(2)}) async-start(), calls=%async_computation.5 | async-start | bytes 69632 | tf_op jit(solution)/shard_map/reduce_scatter | solution.py:137
Sparse Core Ops, SparseCore 0:
  456.0 15.2 all-reduce.4
  881.6 15.4 all-reduce.6
  901.0 53.0 reduce-scatter.1
where the time goes:
time: 965 us; the launch traced here: 961 us
  other arithmetic  420 us (44%)
  local copies, waits for them, and re-layouts  360 us (37%)
  waiting for transfers between devices  93 us (10%)
  blocking collectives  48.7 us (5%)
  matrix products  17.6 us (2%)
  between operations  14.1 us (1%)
    scatter-add x2, other arithmetic, on_device(): jax.ops.segment_sum(residual.reshape(2, -1).T, connect.reshape(-1), num_s...  356 us
    gather x4, local copies, waits for them, and re-layouts, on_device(): element_vals = current[:, connect]  255 us
    reduce_scatter x1, waiting for transfers between devices, on_device(): lax.psum_scatter(terms, ('dom', 'sub', 'chip'), scatter_dimension=1, tile...  55 us
    scatter-add x2, other arithmetic, on_device(): summed = padded.at[:, links].add(received.reshape(2, -1))[:, :nodes]  54.8 us
    psum x1, blocking collectives, on_device(): lax.psum(jnp.dot(filter_taps, own_signal.T, precision=lax.Precision.HIGHE...  34.9 us
    psum x2, waiting for transfers between devices, on_device(): total = lax.psum(summed, 'chip')  30 us
    gather x2, local copies, waits for them, and re-layouts, on_device(): sent = padded[:, links].reshape(2, 3, peers, capacity)  26.8 us
  transfers between devices with their start and end apart: 7, of which 5 were waited for; matrix products, arithmetic and copies ran while one was open for 0% of the time, Pallas kernels for 0%

commit v1 on v0

v1 whole, which is shorter than its diff:
```python
import functools
import math

import jax
import jax.numpy as jnp
import numpy as np
from jax import lax
from jax.experimental import pallas as pl
from jax.experimental.pallas import tpu as pltpu
from jax.sharding import PartitionSpec as P

NN = 512
LANES = 128
ROWS = 64
COLS = 256
BLOCK = 8
ALL = ("dom", "sub", "chip")

GLL_POINTS = (
    -1.0,
    -0.8717401485096066,
    -0.5917001814331423,
    -0.2092992179024789,
    0.2092992179024789,
    0.5917001814331423,
    0.8717401485096066,
    1.0,
)
GLL_WEIGHTS = (
    0.03571428571428571,
    0.21070422714350603,
    0.3411226924835044,
    0.4124587946587038,
    0.4124587946587038,
    0.3411226924835044,
    0.21070422714350603,
    0.03571428571428571,
)
BF = jnp.bfloat16
F32 = jnp.float32


def element_tables():
    points = np.array(GLL_POINTS)
    identity = np.eye(8)
    diffs = points[:, None] - points[None, :] + identity
    barycentric = 1.0 / np.prod(diffs, axis=1)
    derivative = barycentric[None, :] / barycentric[:, None] / diffs
    derivative = derivative * (1.0 - identity)
    derivative = derivative - identity * derivative.sum(axis=1)[:, None]
    along_x = np.kron(derivative, np.eye(64)).T
    along_y = np.kron(np.eye(4), np.kron(derivative, identity)).T
    along_z = np.kron(np.eye(32), derivative).T
    quad = np.array(GLL_WEIGHTS)
    cube = np.kron(np.kron(quad, quad), quad)

    def parts(table):
        table = table.astype(np.float32)
        high = table.astype(jnp.bfloat16)
        low = (table - high.astype(np.float32)).astype(jnp.bfloat16)
        return high, low

    forward = []
    backward = []
    for table in (along_x, along_y, along_z):
        forward += parts(table)
        backward += parts(table.T)
    return forward, backward, np.concatenate([cube] * 3).astype(np.float32)[None, :]


def halves(x):
    high = x.astype(BF)
    return high, (x - high.astype(F32)).astype(BF)


def mm(a, b):
    return jnp.dot(a, b, preferred_element_type=F32)


def times(x, high, low):
    xh, xl = halves(x)
    rows = x.shape[0]
    both = mm(jnp.concatenate([xh, xl], axis=0), high)
    return both[:rows] + both[rows:] + mm(xh, low)


def stack_halves(x):
    return jnp.concatenate([x[:, :256], x[:, 256:]], axis=0)


def unstack_halves(x):
    rows = x.shape[0] // 2
    return jnp.concatenate([x[:rows], x[rows:]], axis=1)


def split_index(index):
    row = (index >> 7) & (ROWS - 1)
    column = (index & (LANES - 1)) | ((index >> 13) << 7)
    return row, column


def column_hot(column):
    ids = lax.broadcasted_iota(jnp.int32, (COLS, NN), 0).astype(BF)
    return jnp.where(ids == column.astype(BF), BF(1), BF(0))


def fill_table(table_ref, fields):
    for k in range(2):
        field = fields[k]
        plane = jnp.concatenate([field[:ROWS], field[ROWS:]], axis=1)
        high, low = halves(plane)
        table_ref[k * ROWS : (k + 1) * ROWS] = high
        table_ref[(2 + k) * ROWS : (3 + k) * ROWS] = low


def look_up(table, index):
    row, column = split_index(index)
    found = mm(table, column_hot(column))
    found = found[: 2 * ROWS] + found[2 * ROWS :]
    mask = lax.broadcasted_iota(jnp.int32, (ROWS, NN), 0) == row
    return [
        jnp.sum(jnp.where(mask, found[k * ROWS : (k + 1) * ROWS], 0.0), axis=0, keepdims=True)
        for k in range(2)
    ]


def spread(indices, values):
    columns = []
    placed = []
    ids = lax.broadcasted_iota(jnp.int32, (ROWS, NN), 0).astype(BF)
    for index, pair in zip(indices, values):
        row, column = split_index(index)
        columns.append(column_hot(column))
        mask = ids == row.astype(BF)
        terms = [halves(v) for v in pair]
        placed.append(
            jnp.concatenate(
                [jnp.where(mask, terms[k][s], BF(0)) for s in range(2) for k in range(2)], axis=0
            )
        )
    left = jnp.concatenate(placed, axis=1) if len(placed) > 1 else placed[0]
    right = jnp.concatenate(columns, axis=1) if len(columns) > 1 else columns[0]
    return lax.dot_general(left, right, (((1,), (1,)), ((), ())), preferred_element_type=F32)


def to_fields(sums):
    sums = sums[: 2 * ROWS] + sums[2 * ROWS :]
    return [
        jnp.concatenate(
            [
                sums[k * ROWS : (k + 1) * ROWS, :LANES],
                sums[k * ROWS : (k + 1) * ROWS, LANES:],
            ],
            axis=0,
        )
        for k in range(2)
    ]


def gather_all(table_ref, connect_ref, vals_ref):
    count = connect_ref.shape[0]
    table = table_ref[...]

    def body(i, carry):
        for u in range(BLOCK):
            e = i * BLOCK + u
            pair = look_up(table, connect_ref[pl.ds(e, 1), :])
            for k in range(2):
                vals_ref[k, pl.ds(e, 1), :] = pair[k]
        return carry

    lax.fori_loop(0, count // BLOCK, body, 0)


def operator(vals_ref, metric_ref, weights_ref, forward, backward, back_ref):
    count = vals_ref.shape[1]
    vals = jnp.concatenate([vals_ref[0], vals_ref[1]], axis=0)
    stacked = stack_halves(vals)
    total = None
    for i in range(3):
        scale = metric_ref[:, i * NN : (i + 1) * NN] * weights_ref[:, i * NN : (i + 1) * NN]
        scale = jnp.concatenate([scale, scale], axis=0)
        fh, fl = forward[2 * i][...], forward[2 * i + 1][...]
        bh, bl = backward[2 * i][...], backward[2 * i + 1][...]
        if i == 0:
            part = times(times(vals, fh, fl) * scale, bh, bl)
        else:
            grads = times(stacked, fh, fl) * stack_halves(scale)
            part = unstack_halves(times(grads, bh, bl))
        total = part if total is None else total + part
    back_ref[0] = total[:count]
    back_ref[1] = total[count:]


def driver_hot(driver_ref):
    count = driver_ref.shape[1]
    return (lax.broadcasted_iota(jnp.int32, (8, count), 0) == driver_ref[...]).astype(F32)


def driver_sums(vals_ref, surface_ref, driver_ref):
    products = surface_ref[...] * vals_ref[1]
    products = sum(products[:, i * LANES : (i + 1) * LANES] for i in range(NN // LANES))
    return jnp.dot(
        driver_hot(driver_ref),
        products,
        precision=lax.Precision.HIGHEST,
        preferred_element_type=F32,
    )


def add_source(step, drive_ref, surface_ref, driver_ref, back_ref):
    terms = drive_ref[...]
    terms = jnp.sum(terms[:, 8 * step : 8 * step + 8, :], axis=0)
    drive = jnp.broadcast_to(jnp.sum(terms, axis=1, keepdims=True), (8, LANES))
    amplitude = lax.dot_general(
        driver_hot(driver_ref),
        drive,
        (((0,), (0,)), ((), ())),
        precision=lax.Precision.HIGHEST,
        preferred_element_type=F32,
    )
    amplitude = jnp.concatenate([amplitude] * (NN // LANES), axis=1)
    back_ref[0] = amplitude * surface_ref[...] - back_ref[0]
    back_ref[1] = -back_ref[1]


def scatter_all(res_ref, connect_ref, sums_ref):
    count = connect_ref.shape[0]
    sums_ref[...] = jnp.zeros_like(sums_ref)

    def body(i, carry):
        rows = [pl.ds(i * BLOCK + u, 1) for u in range(BLOCK)]
        sums_ref[...] += spread(
            [connect_ref[r, :] for r in rows],
            [[res_ref[k, r, :] for k in range(2)] for r in rows],
        )
        return carry

    lax.fori_loop(0, count // BLOCK, body, 0)


def fill_send(where_ref, table_ref, shared_ref, partial, send_ref, *, doms, peers):
    table = table_ref[...]
    send_ref[:, :8, :] = jnp.zeros((send_ref.shape[0], 8, LANES), F32)
    for q in range(send_ref.shape[0]):
        send_ref[q, 8:, :] = partial
    for o in range(3):
        dom = where_ref[0] + (o - 1)
        for j in range(peers):
            slot = o * peers + j
            pair = look_up(table, shared_ref[slot : slot + 1, :])

            @pl.when((dom >= 0) & (dom < doms))
            def _():
                for chip in range(2):
                    to = (dom * peers + j) * 2 + chip
                    for k in range(2):
                        for i in range(4):
                            send_ref[pl.ds(to, 1), 4 * k + i, :] = pair[k][
                                :, i * LANES : (i + 1) * LANES
                            ]


def received_sums(where_ref, shared_ref, recv_ref, *, doms, peers):
    indices = []
    values = []
    for o in range(3):
        dom = jnp.clip(where_ref[0] + (o - 1), 0, doms - 1)
        for j in range(peers):
            slot = o * peers + j
            start = (dom * peers + j) * 2
            both = recv_ref[start, :8, :] + recv_ref[start + 1, :8, :]
            indices.append(shared_ref[slot : slot + 1, :])
            values.append(
                [
                    jnp.concatenate([both[4 * k + i : 4 * k + i + 1] for i in range(4)], axis=1)
                    for k in range(2)
                ]
            )
    total = None
    for at in range(0, len(indices), BLOCK):
        part = spread(indices[at : at + BLOCK], values[at : at + BLOCK])
        total = part if total is None else total + part
    return to_fields(total)


def advance(current, previous, mass_ref, own_ref, other_ref, received):
    return [
        2.0 * current[k] - previous[k] + mass_ref[...] * (own_ref[k] + other_ref[k] + received[k])
        for k in range(2)
    ]


def first_kernel(now0, now1, connect, surface, driver, metric, weights, *refs):
    tables, (back, partial, vals, table) = refs[:12], refs[12:]
    fill_table(table, [now0[...], now1[...]])
    gather_all(table, connect, vals)
    partial[...] = driver_sums(vals, surface, driver)
    operator(vals, metric, weights, tables[:6], tables[6:], back)


def local_sums(where, res, connect, shared, partial, local, send, sums, table, sizes):
    scatter_all(res, connect, sums)
    fields = to_fields(sums[...])
    for k in range(2):
        local[k] = fields[k]
    fill_table(table, fields)
    fill_send(where, table, shared, partial, send, **sizes)


def second_kernel(
    where, back, partial, drive, connect, surface, driver, shared, local, send, res, sums, table, *, sizes
):
    for k in range(2):
        res[k] = back[k]
    add_source(0, drive, surface, driver, res)
    local_sums(where, res, connect, shared, partial[...], local, send, sums, table, sizes)


def third_kernel(
    where,
    now0,
    now1,
    prev0,
    prev1,
    mass,
    own,
    other,
    recv,
    drive,
    connect,
    surface,
    driver,
    shared,
    metric,
    weights,
    *refs,
    sizes,
):
    tables, (current, local, send, vals, res, sums, table) = refs[:12], refs[12:]
    received = received_sums(where, shared, recv, **sizes)
    fields = advance(
        [now0[...], now1[...]], [prev0[...], prev1[...]], mass, own, other, received
    )
    for k in range(2):
        current[k] = fields[k]
    fill_table(table, fields)
    gather_all(table, connect, vals)
    partial = driver_sums(vals, surface, driver)
    operator(vals, metric, weights, tables[:6], tables[6:], res)
    add_source(1, drive, surface, driver, res)
    local_sums(where, res, connect, shared, partial, local, send, sums, table, sizes)


def last_kernel(
    where, current, now0, now1, mass, own, other, recv_before, recv, shared, signal, out0, out1, grad, *, sizes, scale
):
    received = received_sums(where, shared, recv, **sizes)
    fields = advance(
        [current[0], current[1]], [now0[...], now1[...]], mass, own, other, received
    )
    out0[...] = fields[0]
    out1[...] = fields[1]

    def column(ref):
        return jnp.sum(jnp.sum(ref[:, 8:, :], axis=0), axis=1, keepdims=True) * scale

    grad[...] = column(recv) * signal[0:1, :] + column(recv_before) * signal[1:2, :]


VMEM = pl.BlockSpec(memory_space=pltpu.VMEM)
SMEM = pl.BlockSpec(memory_space=pltpu.SMEM)


def call(body, name, scalars, arrays, outs, scratch):
    return pl.pallas_call(
        body,
        out_shape=[jax.ShapeDtypeStruct(shape, F32) for shape in outs],
        in_specs=[SMEM] * len(scalars) + [VMEM] * len(arrays),
        out_specs=[VMEM] * len(outs),
        scratch_shapes=[pltpu.VMEM(shape, dtype) for shape, dtype in scratch],
        compiler_params=pltpu.CompilerParams(vmem_limit_bytes=56 << 20),
        name=name,
    )(*scalars, *arrays)


def on_device(
    field_prev,
    field_now,
    adjoint_now,
    adjoint_next,
    inv_mass,
    metric,
    connect,
    surface,
    driver,
    shared,
    filter_taps,
    signal,
):
    forward, backward, weights = element_tables()
    tables = [jnp.asarray(t) for t in forward + backward]
    count = connect.shape[0]
    peers = shared.shape[2]
    doms = lax.axis_size("dom")
    devices = lax.axis_size(ALL)
    width = filter_taps.shape[1]
    sizes = dict(doms=doms, peers=peers)
    where = lax.axis_index("dom").astype(jnp.int32).reshape(1)
    plane = (LANES, LANES)
    now0, now1, prev0, prev1, mass = (
        x.reshape(plane) for x in (field_now, adjoint_now, field_prev, adjoint_next, inv_mass)
    )
    links = shared.reshape(3 * peers, NN)
    driver_row = driver.reshape(1, count)
    own_signal = lax.dynamic_slice_in_dim(signal, lax.axis_index(ALL) * width, width, 1)
    terms = (own_signal[:, None, :] * filter_taps[None]).reshape(16, width)
    if width > LANES:
        terms = jnp.sum(terms, axis=1, keepdims=True)
    terms = jnp.pad(terms, ((0, 0), (0, LANES - terms.shape[1])))
    terms = jnp.broadcast_to(terms[None], (devices, 16, LANES))

    def trade(x):
        return lax.all_to_all(x, ALL, 0, 0, tiled=True)

    def swap(x):
        return lax.ppermute(x, "chip", [(0, 1), (1, 0)])

    drive = trade(terms)
    nodes = ((2,) + plane, F32)
    elements = ((2, count, NN), F32)
    sums = ((4 * ROWS, COLS), F32)
    table = ((4 * ROWS, COLS), BF)
    packet = (devices, 16, LANES)
    back, partial = call(
        first_kernel,
        "operator0",
        [],
        [now0, now1, connect, surface, driver_row, metric, jnp.asarray(weights)] + tables,
        [elements[0], (8, LANES)],
        [elements, table],
    )
    local, send = call(
        functools.partial(second_kernel, sizes=sizes),
        "assemble0",
        [where],
        [back, partial, drive, connect, surface, driver_row, links],
        [nodes[0], packet],
        [elements, sums, table],
    )
    other = swap(local)
    recv0 = trade(send)
    current, local, send = call(
        functools.partial(third_kernel, sizes=sizes),
        "step1",
        [where],
        [now0, now1, prev0, prev1, mass, local, other, recv0, drive, connect, surface, driver_row, links]
        + [metric, jnp.asarray(weights)]
        + tables,
        [nodes[0], nodes[0], packet],
        [elements, elements, sums, table],
    )
    other = swap(local)
    recv1 = trade(send)
    out0, out1, grad = call(
        functools.partial(
            last_kernel, sizes=sizes, scale=1.0 / math.sqrt(NN * count * devices)
        ),
        "finish",
        [where],
        [current, now0, now1, mass, local, other, recv0, recv1, links, own_signal],
        [plane, plane, (8, width)],
        [],
    )
    return out0.reshape(1, -1), out1.reshape(1, -1), grad


def solution(mesh):
    region = P(("groups", "dom", "sub"), None)
    element = P(("groups", "dom", "sub", "chip"), None)
    in_specs = (
        region,
        region,
        region,
        region,
        region,
        element,
        element,
        element,
        P(("groups", "dom", "sub", "chip")),
        P(("groups", "dom", "sub"), None, None, None),
        P(None, ALL),
        P(),
    )
    out_specs = (region, region, P("groups", ALL))
    return jax.shard_map(
        on_device, mesh=mesh, in_specs=in_specs, out_specs=out_specs, check_vma=False
    )
```

time: 965 us -> 80.2 us (0.08)
  other arithmetic: 420 us -> 0.01 us
  local copies, waits for them, and re-layouts: 360 us -> 4.46 us
  waiting for transfers between devices: 93 us -> 15 us
  blocking collectives: 48.7 us -> 0 us
  Pallas kernels: 0 us -> 41.4 us
  matrix products: 17.6 us -> 0 us
  between operations: 14.1 us -> 0.74 us
  starting transfers between devices: 7.77 us -> 18.1 us
    scatter-add x4 -> x0, other arithmetic: 411 us -> none  [the longest x2 356 us: on_device(): jax.ops.segment_sum(residual.reshape(2, -1).T, connect.reshape(-1), num_s...]
    gather x6 -> x0, local copies, waits for them, and re-layouts: 282 us -> none  [the longest x4 255 us: on_device(): element_vals = current[:, connect]]
    reduce_scatter x1 -> x0, waiting for transfers between devices: 55 us -> none  [on_device(): lax.psum_scatter(terms, ('dom', 'sub', 'chip'), scatter_dimension=1, tile...]
    pallas_call x0 -> x4, Pallas kernels: none -> 41.4 us  [call(): pl.pallas_call(body, out_shape=[jax.ShapeDtypeStruct(shape, F32) for shap...]
    psum x1 -> x0, blocking collectives: 34.9 us -> none  [on_device(): lax.psum(jnp.dot(filter_taps, own_signal.T, precision=lax.Precision.HIGHE...]
    psum x2 -> x0, waiting for transfers between devices: 30 us -> none  [on_device(): total = lax.psum(summed, 'chip')]
    concatenate x3 -> x0, local copies, waits for them, and re-layouts: 20.4 us -> none  [the longest x2 15.4 us: on_device(): padded = jnp.concatenate([local, jnp.zeros((2, 1), jnp.float32)], axis=1)]
    dot_general x6 -> x0, matrix products: 17.6 us -> none  [the longest x2 10.3 us: on_device(): jnp.dot(flux.reshape(2 * count, -1), stacked.T, precision=lax.Precision.H...]
  transfers between devices with their start and end apart: 7 -> 5, of which waited for: 5 -> 4; matrix products, arithmetic and copies ran while one was open for 0% -> 1% of each run, Pallas kernels for 0% -> 13%
where the time goes in v1:
time: 80.2 us; the launch traced here: 79.6 us
  Pallas kernels  41.4 us (52%)
  starting transfers between devices  18.1 us (23%)
  waiting for transfers between devices  15 us (19%)
  local copies, waits for them, and re-layouts  4.46 us (6%)
    pallas_call x4, Pallas kernels, call(): pl.pallas_call(body, out_shape=[jax.ShapeDtypeStruct(shape, F32) for shap...  41.4 us
    all_to_all x3, starting transfers between devices, trade(): return lax.all_to_all(x, ALL, 0, 0, tiled=True)  17.3 us
    all_to_all x3, waiting for transfers between devices, trade(): return lax.all_to_all(x, ALL, 0, 0, tiled=True)  12.9 us
    unnamed x22, local copies, waits for them, and re-layouts  3.2 us
    ppermute x2, waiting for transfers between devices, swap(): return lax.ppermute(x, 'chip', [(0, 1), (1, 0)])  2.05 us
  transfers between devices with their start and end apart: 5, of which 4 were waited for; matrix products, arithmetic and copies ran while one was open for 1% of the time, Pallas kernels for 13%

profile of v1, /device:TPU:0, one launch (start us, length us, event | category | flops | bytes accessed | tf_op | source)
XLA Modules:
  0.0 79.6 jit_solution(4059505932637143996)
XLA Ops:
  0.6 0.0 copy-start
  0.7 0.0 copy-start.10
  0.7 0.7 copy-done
  1.4 0.0 copy-done.10
  1.4 0.0 copy-start.9
  1.4 0.5 copy-done.9
  1.9 0.7 broadcast_in_dim.2
  2.6 0.0 copy-start.8
  2.6 7.5 %all-to-all-start = ((f32[16,16,128]{2,1,0:T(8,128)}), f32[16,16,128]{2,1,0:T(8,128)S(1)}, u32[]{:S(2)}, u32[]{:S(2)}) async-start(f32[16,16,128]{2,1,0:T(8,128)} %broadcast_in_dim.2), calls=%async_computation | async-start | bytes 262144 | tf_op jit(solution)/shard_map/all_to_all | solution.py:424
  10.1 0.0 copy-done.8
  10.1 0.6 reshape.61.shared
  10.7 10.3 %operator0.1 = (f32[2,64,512]{2,1,0:T(8,128)}, f32[8,128]{1,0:T(8,128)}) custom-call(f32[128,128]{1,0:T(8,128)} %bitcast.11, f32[128,128]{1,0:T(8,128)} %bitcast.14, s32[64,512]{1,0:T(8,128)} %connect.5, f32[64,512]{1,0:T(8,128)} %surface.5, s32[1,64]{1,0:T(1,128)} %bitcast.21, f32[64,1536]{1,0:T(8,128)} %metric.3, f32[1,1536]{1,0:T(1,128)} %constant.59.clone.weights, ...), custom_call_target="tpu_custom_call" | custom-call | tf_op jit(solution)/shard_map/operator0/pallas_call | solution.py:376
  21.0 0.0 all-to-all-done.drive
  21.0 0.0 copy-start.2
  21.0 0.6 copy-done.2
  21.7 9.7 %assemble0.1 = (f32[2,128,128]{2,1,0:T(8,128)}, f32[16,16,128]{2,1,0:T(8,128)}) custom-call(s32[1]{0:T(128)} %bitcast.where, f32[2,64,512]{2,1,0:T(8,128)} %get-tuple-element.13.back, f32[8,128]{1,0:T(8,128)} %get-tuple-element.14.partial, f32[16,16,128]{2,1,0:T(8,128)} %copy-done.2, s32[64,512]{1,0:T(8,128)} %connect.5, f32[64,512]{1,0:T(8,128)} %surface.5, ...), custom_call_target="tpu_custom_call" | custom-call | tf_op jit(solution)/shard_map/assemble0/pallas_call | solution.py:376
  31.3 0.0 copy-start.4
  31.3 6.1 %all-to-all-start.1 = ((f32[16,16,128]{2,1,0:T(8,128)}), f32[16,16,128]{2,1,0:T(8,128)S(1)}, u32[]{:S(2)}, u32[]{:S(2)}) async-start(f32[16,16,128]{2,1,0:T(8,128)} %get-tuple-element.16), calls=%async_computation.1 | async-start | bytes 262144 | tf_op jit(solution)/shard_map/all_to_all | solution.py:424
  37.5 0.0 copy-done.4
  37.5 0.5 collective-permute-start
  37.9 1.0 %collective-permute-done.other = f32[2,128,128]{2,1,0:T(8,128)S(1)} collective-permute-done((f32[2,128,128]{2,1,0:T(8,128)S(1)}, f32[2,128,128]{2,1,0:T(8,128)S(1)}, u32[]{:S(2)}, u32[]{:S(2)}) %collective-permute-start) | collective-permute-done | bytes 131104 | tf_op jit(solution)/shard_map/ppermute | solution.py:427
  38.9 0.0 copy-start.5
  38.9 6.5 %all-to-all-done.1.recv.recv_before = f32[16,16,128]{2,1,0:T(8,128)S(1)} async-done(((f32[16,16,128]{2,1,0:T(8,128)}), f32[16,16,128]{2,1,0:T(8,128)S(1)}, u32[]{:S(2)}, u32[]{:S(2)}) %all-to-all-start.1) | async-done | bytes 131104 | tf_op jit(solution)/shard_map/all_to_all | solution.py:424
  45.4 0.0 copy-start.1
  45.4 0.0 copy-done.5
  45.4 0.6 copy-done.1
  46.0 18.9 %step1.1 = (f32[2,128,128]{2,1,0:T(8,128)}, f32[2,128,128]{2,1,0:T(8,128)}, f32[16,16,128]{2,1,0:T(8,128)}) custom-call(s32[1]{0:T(128)} %bitcast.where, f32[128,128]{1,0:T(8,128)} %bitcast.12, f32[128,128]{1,0:T(8,128)} %bitcast.15, f32[128,128]{1,0:T(8,128)} %bitcast.19, f32[128,128]{1,0:T(8,128)} %bitcast.20, f32[128,128]{1,0:T(8,128)} %bitcast.17, ...), custom_call_target="tpu_custom_call" | custom-call | tf_op jit(solution)/shard_map/step1/pallas_call | solution.py:376
  64.9 0.0 copy-start.6
  64.9 3.7 %all-to-all-start.2 = ((f32[16,16,128]{2,1,0:T(8,128)}), f32[16,16,128]{2,1,0:T(8,128)S(1)}, u32[]{:S(2)}, u32[]{:S(2)}) async-start(f32[16,16,128]{2,1,0:T(8,128)} %get-tuple-element.19), calls=%async_computation.2 | async-start | bytes 262144 | tf_op jit(solution)/shard_map/all_to_all | solution.py:424
  68.6 0.0 copy-done.6
  68.6 0.4 collective-permute-start.1
  69.0 1.1 %collective-permute-done.1.other = f32[2,128,128]{2,1,0:T(8,128)S(1)} collective-permute-done((f32[2,128,128]{2,1,0:T(8,128)S(1)}, f32[2,128,128]{2,1,0:T(8,128)S(1)}, u32[]{:S(2)}, u32[]{:S(2)}) %collective-permute-start.1) | collective-permute-done | bytes 131104 | tf_op jit(solution)/shard_map/ppermute | solution.py:427
  70.0 0.0 copy-start.7
  70.0 6.5 %all-to-all-done.2.recv = f32[16,16,128]{2,1,0:T(8,128)S(1)} async-done(((f32[16,16,128]{2,1,0:T(8,128)}), f32[16,16,128]{2,1,0:T(8,128)S(1)}, u32[]{:S(2)}, u32[]{:S(2)}) %all-to-all-start.2) | async-done | bytes 131104 | tf_op jit(solution)/shard_map/all_to_all | solution.py:424
  76.5 0.0 copy-start.3
  76.5 0.0 copy-done.7
  76.5 0.7 copy-done.3
  77.2 2.5 %finish.1 = (f32[128,128]{1,0:T(8,128)}, f32[128,128]{1,0:T(8,128)}, f32[8,128]{1,0:T(8,128)}) custom-call(s32[1]{0:T(128)} %bitcast.where, f32[2,128,128]{2,1,0:T(8,128)} %get-tuple-element.17.current, f32[128,128]{1,0:T(8,128)} %bitcast.13, f32[128,128]{1,0:T(8,128)} %bitcast.16, f32[128,128]{1,0:T(8,128)} %bitcast.18, ...), custom_call_target="tpu_custom_call" | custom-call | tf_op jit(solution)/shard_map/finish/pallas_call | solution.py:376
  (2 shorter events, 0.0 us)
Async XLA Ops:
  0.6 0.7 copy-start
  0.7 0.7 copy-start.10
  1.4 0.5 copy-start.9
  2.6 7.5 %copy-start.8 = (s32[1,3,2,512]{3,2,1,0:T(2,128)S(1)}, s32[1,3,2,512]{3,2,1,0:T(2,128)}, u32[]{:S(2)}) copy-start(s32[1,3,2,512]{3,2,1,0:T(2,128)} %param.34) | copy-start | bytes 36868
  2.6 18.5 %all-to-all-start = ((f32[16,16,128]{2,1,0:T(8,128)}), f32[16,16,128]{2,1,0:T(8,128)S(1)}, u32[]{:S(2)}, u32[]{:S(2)}) async-start(f32[16,16,128]{2,1,0:T(8,128)} %broadcast_in_dim.2), calls=%async_computation | async-start | bytes 262144 | tf_op jit(solution)/shard_map/all_to_all | solution.py:424
  21.0 0.7 copy-start.2
  31.3 6.1 %copy-start.4 = (f32[2,128,128]{2,1,0:T(8,128)S(1)}, f32[2,128,128]{2,1,0:T(8,128)}, u32[]{:S(2)}) copy-start(f32[2,128,128]{2,1,0:T(8,128)} %get-tuple-element.15.own) | copy-start | bytes 393220
  31.3 14.1 %all-to-all-start.1 = ((f32[16,16,128]{2,1,0:T(8,128)}), f32[16,16,128]{2,1,0:T(8,128)S(1)}, u32[]{:S(2)}, u32[]{:S(2)}) async-start(f32[16,16,128]{2,1,0:T(8,128)} %get-tuple-element.16), calls=%async_computation.1 | async-start | bytes 262144 | tf_op jit(solution)/shard_map/all_to_all | solution.py:424
  37.5 1.5 %collective-permute-start = (f32[2,128,128]{2,1,0:T(8,128)S(1)}, f32[2,128,128]{2,1,0:T(8,128)S(1)}, u32[]{:S(2)}, u32[]{:S(2)}) collective-permute-start(f32[2,128,128]{2,1,0:T(8,128)S(1)} %copy-done.4), channel_id=1, source_target_pairs={{0,1},{1,0},{2,3},{3,2},{4,5},{5,4},{6,7},{7,6},{8,9},{9,8},{10,11... | collective-permute-start | bytes 393224 | tf_op jit(solution)/shard_map/ppermute | solution.py:427
  38.9 6.5 %copy-start.5 = (f32[2,128,128]{2,1,0:T(8,128)}, f32[2,128,128]{2,1,0:T(8,128)S(1)}, u32[]{:S(2)}) copy-start(f32[2,128,128]{2,1,0:T(8,128)S(1)} %collective-permute-done.other) | copy-start | bytes 393220
  45.4 0.6 copy-start.1
  64.9 3.7 %copy-start.6 = (f32[2,128,128]{2,1,0:T(8,128)S(1)}, f32[2,128,128]{2,1,0:T(8,128)}, u32[]{:S(2)}) copy-start(f32[2,128,128]{2,1,0:T(8,128)} %get-tuple-element.18.own) | copy-start | bytes 393220
  64.9 11.6 %all-to-all-start.2 = ((f32[16,16,128]{2,1,0:T(8,128)}), f32[16,16,128]{2,1,0:T(8,128)S(1)}, u32[]{:S(2)}, u32[]{:S(2)}) async-start(f32[16,16,128]{2,1,0:T(8,128)} %get-tuple-element.19), calls=%async_computation.2 | async-start | bytes 262144 | tf_op jit(solution)/shard_map/all_to_all | solution.py:424
  68.6 1.4 %collective-permute-start.1 = (f32[2,128,128]{2,1,0:T(8,128)S(1)}, f32[2,128,128]{2,1,0:T(8,128)S(1)}, u32[]{:S(2)}, u32[]{:S(2)}) collective-permute-start(f32[2,128,128]{2,1,0:T(8,128)S(1)} %copy-done.6), channel_id=1, source_target_pairs={{0,1},{1,0},{2,3},{3,2},{4,5},{5,4},{6,7},{7,6},{8,9},{9,8},{10,11... | collective-permute-start | bytes 393224 | tf_op jit(solution)/shard_map/ppermute | solution.py:427
  70.0 6.5 %copy-start.7 = (f32[2,128,128]{2,1,0:T(8,128)}, f32[2,128,128]{2,1,0:T(8,128)S(1)}, u32[]{:S(2)}) copy-start(f32[2,128,128]{2,1,0:T(8,128)S(1)} %collective-permute-done.1.other) | copy-start | bytes 393220
  76.5 0.7 copy-start.3

commit v2 on v1

--- a/solution.py
+++ b/solution.py
@@ -13,7 +13,8 @@
 LANES = 128
 ROWS = 64
 COLS = 256
-BLOCK = 8
+BLOCK = 64
+PACKET = 2 * NN + LANES
 ALL = ("dom", "sub", "chip")
 
 GLL_POINTS = (
@@ -169,7 +170,10 @@
                 vals_ref[k, pl.ds(e, 1), :] = pair[k]
         return carry
 
-    lax.fori_loop(0, count // BLOCK, body, 0)
+    if count == BLOCK:
+        body(0, 0)
+    else:
+        lax.fori_loop(0, count // BLOCK, body, 0)
 
 
 def operator(vals_ref, metric_ref, weights_ref, forward, backward, back_ref):
@@ -200,17 +204,26 @@
 def driver_sums(vals_ref, surface_ref, driver_ref):
     products = surface_ref[...] * vals_ref[1]
     products = sum(products[:, i * LANES : (i + 1) * LANES] for i in range(NN // LANES))
-    return jnp.dot(
-        driver_hot(driver_ref),
+    lanes = (((1,), (1,)), ((), ()))
+    per_element = lax.dot_general(
+        jnp.ones((8, LANES), F32),
         products,
+        lanes,
         precision=lax.Precision.HIGHEST,
         preferred_element_type=F32,
     )
+    count = driver_ref.shape[1]
+    hot = lax.broadcasted_iota(jnp.int32, (LANES, count), 0) == driver_ref[...]
+    hot = (hot & (lax.broadcasted_iota(jnp.int32, (LANES, count), 0) < 8)).astype(F32)
+    return lax.dot_general(
+        per_element, hot, lanes, precision=lax.Precision.HIGHEST, preferred_element_type=F32
+    )[:1]
 
 
 def add_source(step, drive_ref, surface_ref, driver_ref, back_ref):
-    terms = drive_ref[...]
-    terms = jnp.sum(terms[:, 8 * step : 8 * step + 8, :], axis=0)
+    terms = jnp.sum(drive_ref[...], axis=0)
+    half = lax.broadcasted_iota(jnp.int32, (8, LANES), 1) >> 6
+    terms = jnp.where(half == step, terms, 0.0)
     drive = jnp.broadcast_to(jnp.sum(terms, axis=1, keepdims=True), (8, LANES))
     amplitude = lax.dot_general(
         driver_hot(driver_ref),
@@ -226,14 +239,21 @@
 
 def scatter_all(res_ref, connect_ref, sums_ref):
     count = connect_ref.shape[0]
-    sums_ref[...] = jnp.zeros_like(sums_ref)
-
-    def body(i, carry):
+
+    def part(i):
         rows = [pl.ds(i * BLOCK + u, 1) for u in range(BLOCK)]
-        sums_ref[...] += spread(
+        return spread(
             [connect_ref[r, :] for r in rows],
             [[res_ref[k, r, :] for k in range(2)] for r in rows],
         )
+
+    if count == BLOCK:
+        sums_ref[...] = part(0)
+        return
+    sums_ref[...] = jnp.zeros_like(sums_ref)
+
+    def body(i, carry):
+        sums_ref[...] += part(i)
         return carry
 
     lax.fori_loop(0, count // BLOCK, body, 0)
@@ -241,24 +261,19 @@
 
 def fill_send(where_ref, table_ref, shared_ref, partial, send_ref, *, doms, peers):
     table = table_ref[...]
-    send_ref[:, :8, :] = jnp.zeros((send_ref.shape[0], 8, LANES), F32)
+    empty = jnp.concatenate([jnp.zeros((1, 2 * NN), F32), partial], axis=1)
     for q in range(send_ref.shape[0]):
-        send_ref[q, 8:, :] = partial
+        send_ref[q] = empty
     for o in range(3):
         dom = where_ref[0] + (o - 1)
         for j in range(peers):
-            slot = o * peers + j
-            pair = look_up(table, shared_ref[slot : slot + 1, :])
+            pair = look_up(table, shared_ref[o, j : j + 1, :])
+            values = jnp.concatenate(pair, axis=1)
 
             @pl.when((dom >= 0) & (dom < doms))
             def _():
                 for chip in range(2):
-                    to = (dom * peers + j) * 2 + chip
-                    for k in range(2):
-                        for i in range(4):
-                            send_ref[pl.ds(to, 1), 4 * k + i, :] = pair[k][
-                                :, i * LANES : (i + 1) * LANES
-                            ]
+                    send_ref[(dom * peers + j) * 2 + chip, :, : 2 * NN] = values
 
 
 def received_sums(where_ref, shared_ref, recv_ref, *, doms, peers):
@@ -267,19 +282,13 @@
     for o in range(3):
         dom = jnp.clip(where_ref[0] + (o - 1), 0, doms - 1)
         for j in range(peers):
-            slot = o * peers + j
             start = (dom * peers + j) * 2
-            both = recv_ref[start, :8, :] + recv_ref[start + 1, :8, :]
-            indices.append(shared_ref[slot : slot + 1, :])
-            values.append(
-                [
-                    jnp.concatenate([both[4 * k + i : 4 * k + i + 1] for i in range(4)], axis=1)
-                    for k in range(2)
-                ]
-            )
+            both = recv_ref[start] + recv_ref[start + 1]
+            indices.append(shared_ref[o, j : j + 1, :])
+            values.append([both[:, k * NN : (k + 1) * NN] for k in range(2)])
     total = None
-    for at in range(0, len(indices), BLOCK):
-        part = spread(indices[at : at + BLOCK], values[at : at + BLOCK])
+    for at in range(0, len(indices), 8):
+        part = spread(indices[at : at + 8], values[at : at + 8])
         total = part if total is None else total + part
     return to_fields(total)
 
@@ -289,6 +298,19 @@
         2.0 * current[k] - previous[k] + mass_ref[...] * (own_ref[k] + other_ref[k] + received[k])
         for k in range(2)
     ]
+
+
+def drive_kernel(taps, signal, send):
+    folded = []
+    for t in range(2):
+        products = taps[...] * signal[t : t + 1, :]
+        products = sum(
+            products[:, i * LANES : (i + 1) * LANES] for i in range(products.shape[1] // LANES)
+        )
+        folded.append(products[:, :64] + products[:, 64:])
+    terms = jnp.concatenate(folded, axis=1)
+    for q in range(send.shape[0]):
+        send[q] = terms
 
 
 def first_kernel(now0, now1, connect, surface, driver, metric, weights, *refs):
@@ -363,7 +385,10 @@
     out1[...] = fields[1]
 
     def column(ref):
-        return jnp.sum(jnp.sum(ref[:, 8:, :], axis=0), axis=1, keepdims=True) * scale
+        row = sum(ref[q, :, 2 * NN :] for q in range(ref.shape[0]))
+        ids = [lax.broadcasted_iota(jnp.int32, (8, LANES), axis) for axis in range(2)]
+        row = jnp.where(ids[0] == ids[1], jnp.broadcast_to(row, (8, LANES)), 0.0)
+        return jnp.sum(row, axis=1, keepdims=True) * scale
 
     grad[...] = column(recv) * signal[0:1, :] + column(recv_before) * signal[1:2, :]
 
@@ -411,33 +436,35 @@
     now0, now1, prev0, prev1, mass = (
         x.reshape(plane) for x in (field_now, adjoint_now, field_prev, adjoint_next, inv_mass)
     )
-    links = shared.reshape(3 * peers, NN)
+    links = shared.reshape(3, peers, NN)
     driver_row = driver.reshape(1, count)
     own_signal = lax.dynamic_slice_in_dim(signal, lax.axis_index(ALL) * width, width, 1)
-    terms = (own_signal[:, None, :] * filter_taps[None]).reshape(16, width)
-    if width > LANES:
-        terms = jnp.sum(terms, axis=1, keepdims=True)
-    terms = jnp.pad(terms, ((0, 0), (0, LANES - terms.shape[1])))
-    terms = jnp.broadcast_to(terms[None], (devices, 16, LANES))
-
     def trade(x):
         return lax.all_to_all(x, ALL, 0, 0, tiled=True)
 
     def swap(x):
         return lax.ppermute(x, "chip", [(0, 1), (1, 0)])
 
+    if width < LANES:
+        pad = ((0, 0), (0, LANES - width))
+        tap_block, signal_block = jnp.pad(filter_taps, pad), jnp.pad(own_signal, pad)
+    else:
+        tap_block, signal_block = filter_taps, own_signal
+    (terms,) = call(
+        drive_kernel, "drive", [], [tap_block, signal_block], [(devices, 8, LANES)], []
+    )
     drive = trade(terms)
     nodes = ((2,) + plane, F32)
     elements = ((2, count, NN), F32)
     sums = ((4 * ROWS, COLS), F32)
     table = ((4 * ROWS, COLS), BF)
-    packet = (devices, 16, LANES)
+    packet = (devices, 1, PACKET)
     back, partial = call(
         first_kernel,
         "operator0",
         [],
         [now0, now1, connect, surface, driver_row, metric, jnp.asarray(weights)] + tables,
-        [elements[0], (8, LANES)],
+        [elements[0], (1, LANES)],
         [elements, table],
     )
     local, send = call(

time: 80.2 us -> 82.2 us (1.025)
  Pallas kernels: 41.4 us -> 46.7 us
  waiting for transfers between devices: 15 us -> 13.1 us
  local copies, waits for them, and re-layouts: 4.46 us -> 3.18 us
    pallas_call x4 -> x5, Pallas kernels: 41.4 us -> 46.7 us  [call(): pl.pallas_call(body, out_shape=[jax.ShapeDtypeStruct(shape, F32) for shap...]
    all_to_all x3, waiting for transfers between devices: 12.9 us -> 11 us  [trade(): return lax.all_to_all(x, ALL, 0, 0, tiled=True)]
    unnamed x22 -> x16, local copies, waits for them, and re-layouts: 3.2 us -> 2.6 us
  transfers between devices with their start and end apart: 5 -> 5, of which waited for: 4 -> 4; matrix products, arithmetic and copies ran while one was open for 1% -> 0% of each run, Pallas kernels for 13% -> 12%
where the time goes in v2:
time: 82.2 us; the launch traced here: 81.7 us
  Pallas kernels  46.7 us (57%)
  starting transfers between devices  18 us (22%)
  waiting for transfers between devices  13.1 us (16%)
  local copies, waits for them, and re-layouts  3.18 us (4%)
    pallas_call x5, Pallas kernels, call(): pl.pallas_call(body, out_shape=[jax.ShapeDtypeStruct(shape, F32) for shap...  46.7 us
    all_to_all x3, starting transfers between devices, trade(): return lax.all_to_all(x, ALL, 0, 0, tiled=True)  17.3 us
    all_to_all x3, waiting for transfers between devices, trade(): return lax.all_to_all(x, ALL, 0, 0, tiled=True)  11 us
    unnamed x16, local copies, waits for them, and re-layouts  2.6 us
    ppermute x2, waiting for transfers between devices, swap(): return lax.ppermute(x, 'chip', [(0, 1), (1, 0)])  2.18 us
  transfers between devices with their start and end apart: 5, of which 4 were waited for; matrix products, arithmetic and copies ran while one was open for 0% of the time, Pallas kernels for 12%

profile of v2, /device:TPU:0, one launch (start us, length us, event | category | flops | bytes accessed | tf_op | source)
XLA Modules:
  0.0 81.7 jit_solution(9447950187384018982)
XLA Ops:
  0.6 0.0 copy-start
  0.7 0.7 copy-done
  1.4 0.6 constant_dynamic-slice_fusion.signal
  1.9 1.5 %drive.1 = f32[16,8,128]{2,1,0:T(8,128)} custom-call(f32[8,128]{1,0:T(8,128)} %taps.1, f32[2,128]{1,0:T(2,128)} %constant_dynamic-slice_fusion.signal), custom_call_target="tpu_custom_call" | custom-call | tf_op jit(solution)/shard_map/drive/pallas_call | solution.py:401
  3.4 7.4 %all-to-all-start = ((f32[16,8,128]{2,1,0:T(8,128)}), f32[16,8,128]{2,1,0:T(8,128)S(1)}, u32[]{:S(2)}, u32[]{:S(2)}) async-start(f32[16,8,128]{2,1,0:T(8,128)} %drive.1), calls=%async_computation | async-start | bytes 131072 | tf_op jit(solution)/shard_map/all_to_all | solution.py:443
  10.8 9.6 %operator0.1 = (f32[2,64,512]{2,1,0:T(8,128)}, f32[1,128]{1,0:T(1,128)}) custom-call(f32[128,128]{1,0:T(8,128)} %bitcast.10, f32[128,128]{1,0:T(8,128)} %bitcast.13, s32[64,512]{1,0:T(8,128)} %connect.5, f32[64,512]{1,0:T(8,128)} %surface.5, s32[1,64]{1,0:T(1,128)} %bitcast.23, f32[64,1536]{1,0:T(8,128)} %metric.3, f32[1,1536]{1,0:T(1,128)} %constant.59.clone.weights, ...), custom_call_target="tpu_custom_call" | custom-call | tf_op jit(solution)/shard_map/operator0/pallas_call | solution.py:401
  20.4 0.0 all-to-all-done.drive
  20.4 0.0 copy-start.2
  20.4 0.6 copy-done.2
  21.0 8.7 %assemble0.1 = (f32[2,128,128]{2,1,0:T(8,128)}, f32[16,1,1152]{2,1,0:T(1,128)}) custom-call(s32[1]{0:T(128)} %bitcast.where, f32[2,64,512]{2,1,0:T(8,128)} %get-tuple-element.13.back, f32[1,128]{1,0:T(1,128)} %get-tuple-element.14.partial, f32[16,8,128]{2,1,0:T(8,128)} %copy-done.2, s32[64,512]{1,0:T(8,128)} %connect.5, f32[64,512]{1,0:T(8,128)} %surface.5, ...), custom_call_target="tpu_custom_call" | custom-call | tf_op jit(solution)/shard_map/assemble0/pallas_call | solution.py:401
  29.8 0.0 copy-start.5
  29.8 6.3 %all-to-all-start.1 = ((f32[16,1,1152]{2,1,0:T(1,128)}), f32[16,1,1152]{2,1,0:T(1,128)S(1)}, u32[]{:S(2)}, u32[]{:S(2)}) async-start(f32[16,1,1152]{2,1,0:T(1,128)} %get-tuple-element.16), calls=%async_computation.1 | async-start | bytes 147456 | tf_op jit(solution)/shard_map/all_to_all | solution.py:443
  36.1 0.0 copy-done.5
  36.1 0.3 collective-permute-start
  36.4 1.1 %collective-permute-done.other = f32[2,128,128]{2,1,0:T(8,128)S(1)} collective-permute-done((f32[2,128,128]{2,1,0:T(8,128)S(1)}, f32[2,128,128]{2,1,0:T(8,128)S(1)}, u32[]{:S(2)}, u32[]{:S(2)}) %collective-permute-start) | collective-permute-done | bytes 131104 | tf_op jit(solution)/shard_map/ppermute | solution.py:446
  37.5 0.0 copy-start.6
  37.5 5.4 %all-to-all-done.1.recv.recv_before = f32[16,1,1152]{2,1,0:T(1,128)S(1)} async-done(((f32[16,1,1152]{2,1,0:T(1,128)}), f32[16,1,1152]{2,1,0:T(1,128)S(1)}, u32[]{:S(2)}, u32[]{:S(2)}) %all-to-all-start.1) | async-done | bytes 73760 | tf_op jit(solution)/shard_map/all_to_all | solution.py:443
  42.9 0.0 copy-start.1
  42.9 0.0 copy-done.6
  42.9 0.6 copy-done.1
  43.5 24.5 %step1.1 = (f32[2,128,128]{2,1,0:T(8,128)}, f32[2,128,128]{2,1,0:T(8,128)}, f32[16,1,1152]{2,1,0:T(1,128)}) custom-call(s32[1]{0:T(128)} %bitcast.where, f32[128,128]{1,0:T(8,128)} %bitcast.11, f32[128,128]{1,0:T(8,128)} %bitcast.14, f32[128,128]{1,0:T(8,128)} %bitcast.21, f32[128,128]{1,0:T(8,128)} %bitcast.22, f32[128,128]{1,0:T(8,128)} %bitcast.16, ...), custom_call_target="tpu_custom_call" | custom-call | tf_op jit(solution)/shard_map/step1/pallas_call | solution.py:401
  68.0 0.0 copy-start.4
  68.0 3.6 %all-to-all-start.2 = ((f32[16,1,1152]{2,1,0:T(1,128)}), f32[16,1,1152]{2,1,0:T(1,128)S(1)}, u32[]{:S(2)}, u32[]{:S(2)}) async-start(f32[16,1,1152]{2,1,0:T(1,128)} %get-tuple-element.19), calls=%async_computation.2 | async-start | bytes 147456 | tf_op jit(solution)/shard_map/all_to_all | solution.py:443
  71.7 0.0 copy-done.4
  71.7 0.4 collective-permute-start.1
  72.0 1.1 %collective-permute-done.1.other = f32[2,128,128]{2,1,0:T(8,128)S(1)} collective-permute-done((f32[2,128,128]{2,1,0:T(8,128)S(1)}, f32[2,128,128]{2,1,0:T(8,128)S(1)}, u32[]{:S(2)}, u32[]{:S(2)}) %collective-permute-start.1) | collective-permute-done | bytes 131104 | tf_op jit(solution)/shard_map/ppermute | solution.py:446
  73.1 0.0 copy-start.7
  73.1 5.5 %all-to-all-done.2.recv = f32[16,1,1152]{2,1,0:T(1,128)S(1)} async-done(((f32[16,1,1152]{2,1,0:T(1,128)}), f32[16,1,1152]{2,1,0:T(1,128)S(1)}, u32[]{:S(2)}, u32[]{:S(2)}) %all-to-all-start.2) | async-done | bytes 73760 | tf_op jit(solution)/shard_map/all_to_all | solution.py:443
  78.6 0.0 copy-start.3
  78.7 0.0 copy-done.7
  78.7 0.6 copy-done.3
  79.3 2.5 %finish.1 = (f32[128,128]{1,0:T(8,128)}, f32[128,128]{1,0:T(8,128)}, f32[8,128]{1,0:T(8,128)}) custom-call(s32[1]{0:T(128)} %bitcast.where, f32[2,128,128]{2,1,0:T(8,128)} %get-tuple-element.17.current, f32[128,128]{1,0:T(8,128)} %bitcast.12, f32[128,128]{1,0:T(8,128)} %bitcast.15, f32[128,128]{1,0:T(8,128)} %bitcast.17, ...), custom_call_target="tpu_custom_call" | custom-call | tf_op jit(solution)/shard_map/finish/pallas_call | solution.py:401
Async XLA Ops:
  0.6 0.7 copy-start
  3.4 17.0 %all-to-all-start = ((f32[16,8,128]{2,1,0:T(8,128)}), f32[16,8,128]{2,1,0:T(8,128)S(1)}, u32[]{:S(2)}, u32[]{:S(2)}) async-start(f32[16,8,128]{2,1,0:T(8,128)} %drive.1), calls=%async_computation | async-start | bytes 131072 | tf_op jit(solution)/shard_map/all_to_all | solution.py:443
  20.4 0.6 copy-start.2
  29.8 6.3 %copy-start.5 = (f32[2,128,128]{2,1,0:T(8,128)S(1)}, f32[2,128,128]{2,1,0:T(8,128)}, u32[]{:S(2)}) copy-start(f32[2,128,128]{2,1,0:T(8,128)} %get-tuple-element.15.own) | copy-start | bytes 393220
  29.8 13.2 %all-to-all-start.1 = ((f32[16,1,1152]{2,1,0:T(1,128)}), f32[16,1,1152]{2,1,0:T(1,128)S(1)}, u32[]{:S(2)}, u32[]{:S(2)}) async-start(f32[16,1,1152]{2,1,0:T(1,128)} %get-tuple-element.16), calls=%async_computation.1 | async-start | bytes 147456 | tf_op jit(solution)/shard_map/all_to_all | solution.py:443
  36.1 1.4 %collective-permute-start = (f32[2,128,128]{2,1,0:T(8,128)S(1)}, f32[2,128,128]{2,1,0:T(8,128)S(1)}, u32[]{:S(2)}, u32[]{:S(2)}) collective-permute-start(f32[2,128,128]{2,1,0:T(8,128)S(1)} %copy-done.5), channel_id=1, source_target_pairs={{0,1},{1,0},{2,3},{3,2},{4,5},{5,4},{6,7},{7,6},{8,9},{9,8},{10,11... | collective-permute-start | bytes 393224 | tf_op jit(solution)/shard_map/ppermute | solution.py:446
  37.5 5.4 %copy-start.6 = (f32[2,128,128]{2,1,0:T(8,128)}, f32[2,128,128]{2,1,0:T(8,128)S(1)}, u32[]{:S(2)}) copy-start(f32[2,128,128]{2,1,0:T(8,128)S(1)} %collective-permute-done.other) | copy-start | bytes 393220
  42.9 0.6 copy-start.1
  68.0 3.7 %copy-start.4 = (f32[2,128,128]{2,1,0:T(8,128)S(1)}, f32[2,128,128]{2,1,0:T(8,128)}, u32[]{:S(2)}) copy-start(f32[2,128,128]{2,1,0:T(8,128)} %get-tuple-element.18.own) | copy-start | bytes 393220
  68.0 10.6 %all-to-all-start.2 = ((f32[16,1,1152]{2,1,0:T(1,128)}), f32[16,1,1152]{2,1,0:T(1,128)S(1)}, u32[]{:S(2)}, u32[]{:S(2)}) async-start(f32[16,1,1152]{2,1,0:T(1,128)} %get-tuple-element.19), calls=%async_computation.2 | async-start | bytes 147456 | tf_op jit(solution)/shard_map/all_to_all | solution.py:443
  71.7 1.4 %collective-permute-start.1 = (f32[2,128,128]{2,1,0:T(8,128)S(1)}, f32[2,128,128]{2,1,0:T(8,128)S(1)}, u32[]{:S(2)}, u32[]{:S(2)}) collective-permute-start(f32[2,128,128]{2,1,0:T(8,128)S(1)} %copy-done.4), channel_id=1, source_target_pairs={{0,1},{1,0},{2,3},{3,2},{4,5},{5,4},{6,7},{7,6},{8,9},{9,8},{10,11... | collective-permute-start | bytes 393224 | tf_op jit(solution)/shard_map/ppermute | solution.py:446
  73.1 5.6 %copy-start.7 = (f32[2,128,128]{2,1,0:T(8,128)}, f32[2,128,128]{2,1,0:T(8,128)S(1)}, u32[]{:S(2)}) copy-start(f32[2,128,128]{2,1,0:T(8,128)S(1)} %collective-permute-done.1.other) | copy-start | bytes 393220
  78.6 0.6 copy-start.3

commit v3 on v2

--- a/solution.py
+++ b/solution.py
@@ -13,7 +13,7 @@
 LANES = 128
 ROWS = 64
 COLS = 256
-BLOCK = 64
+BLOCK = 32
 PACKET = 2 * NN + LANES
 ALL = ("dom", "sub", "chip")
 
@@ -61,12 +61,12 @@
         low = (table - high.astype(np.float32)).astype(jnp.bfloat16)
         return high, low
 
-    forward = []
-    backward = []
-    for table in (along_x, along_y, along_z):
-        forward += parts(table)
-        backward += parts(table.T)
-    return forward, backward, np.concatenate([cube] * 3).astype(np.float32)[None, :]
+    wide = list(parts(along_x)) + list(parts(along_x.T))
+    narrow = []
+    for table in (along_y, along_z, along_y.T, along_z.T):
+        narrow += parts(table)
+    weights = np.concatenate([cube] * 3).astype(np.float32)[None, :]
+    return np.stack(wide), np.stack(narrow), weights
 
 
 def halves(x):
@@ -176,21 +176,23 @@
         lax.fori_loop(0, count // BLOCK, body, 0)
 
 
-def operator(vals_ref, metric_ref, weights_ref, forward, backward, back_ref):
+def operator(vals_ref, metric, weights, wide, narrow, back_ref):
     count = vals_ref.shape[1]
     vals = jnp.concatenate([vals_ref[0], vals_ref[1]], axis=0)
     stacked = stack_halves(vals)
+    metric_ref, weights_ref = metric(), weights()
     total = None
-    for i in range(3):
+    for i in (1, 2, 0):
         scale = metric_ref[:, i * NN : (i + 1) * NN] * weights_ref[:, i * NN : (i + 1) * NN]
         scale = jnp.concatenate([scale, scale], axis=0)
-        fh, fl = forward[2 * i][...], forward[2 * i + 1][...]
-        bh, bl = backward[2 * i][...], backward[2 * i + 1][...]
         if i == 0:
-            part = times(times(vals, fh, fl) * scale, bh, bl)
+            table = wide()
+            part = times(times(vals, table[0], table[1]) * scale, table[2], table[3])
         else:
-            grads = times(stacked, fh, fl) * stack_halves(scale)
-            part = unstack_halves(times(grads, bh, bl))
+            table = narrow()
+            at = 2 * (i - 1)
+            grads = times(stacked, table[at], table[at + 1]) * stack_halves(scale)
+            part = unstack_halves(times(grads, table[at + 4], table[at + 5]))
         total = part if total is None else total + part
     back_ref[0] = total[:count]
     back_ref[1] = total[count:]
@@ -220,7 +222,7 @@
     )[:1]
 
 
-def add_source(step, drive_ref, surface_ref, driver_ref, back_ref):
+def residual(step, drive_ref, surface_ref, driver_ref, back_ref, res_ref):
     terms = jnp.sum(drive_ref[...], axis=0)
     half = lax.broadcasted_iota(jnp.int32, (8, LANES), 1) >> 6
     terms = jnp.where(half == step, terms, 0.0)
@@ -233,8 +235,8 @@
         preferred_element_type=F32,
     )
     amplitude = jnp.concatenate([amplitude] * (NN // LANES), axis=1)
-    back_ref[0] = amplitude * surface_ref[...] - back_ref[0]
-    back_ref[1] = -back_ref[1]
+    res_ref[0] = amplitude * surface_ref[...] - back_ref[0]
+    res_ref[1] = -back_ref[1]
 
 
 def scatter_all(res_ref, connect_ref, sums_ref):
@@ -259,28 +261,26 @@
     lax.fori_loop(0, count // BLOCK, body, 0)
 
 
-def fill_send(where_ref, table_ref, shared_ref, partial, send_ref, *, doms, peers):
+def fill_send(table_ref, shared_ref, partial, send_ref, *, doms, peers):
     table = table_ref[...]
     empty = jnp.concatenate([jnp.zeros((1, 2 * NN), F32), partial], axis=1)
     for q in range(send_ref.shape[0]):
         send_ref[q] = empty
-    for o in range(3):
-        dom = where_ref[0] + (o - 1)
-        for j in range(peers):
-            pair = look_up(table, shared_ref[o, j : j + 1, :])
-            values = jnp.concatenate(pair, axis=1)
-
-            @pl.when((dom >= 0) & (dom < doms))
-            def _():
-                for chip in range(2):
-                    send_ref[(dom * peers + j) * 2 + chip, :, : 2 * NN] = values
-
-
-def received_sums(where_ref, shared_ref, recv_ref, *, doms, peers):
+    slots = [(o, j) for o in (0, 2, 1) for j in range(peers)]
+    packets = [
+        jnp.concatenate(look_up(table, shared_ref[o, j : j + 1, :]), axis=1) for o, j in slots
+    ]
+    for (o, j), packet in zip(slots, packets):
+        dom = jnp.clip(lax.axis_index("dom") + (o - 1), 0, doms - 1)
+        for chip in range(2):
+            send_ref[(dom * peers + j) * 2 + chip, :, : 2 * NN] = packet
+
+
+def received_sums(shared_ref, recv_ref, *, doms, peers):
     indices = []
     values = []
     for o in range(3):
-        dom = jnp.clip(where_ref[0] + (o - 1), 0, doms - 1)
+        dom = jnp.clip(lax.axis_index("dom") + (o - 1), 0, doms - 1)
         for j in range(peers):
             start = (dom * peers + j) * 2
             both = recv_ref[start] + recv_ref[start + 1]
@@ -293,14 +293,15 @@
     return to_fields(total)
 
 
-def advance(current, previous, mass_ref, own_ref, other_ref, received):
+def advance(current, previous, mass, own, other, received):
     return [
-        2.0 * current[k] - previous[k] + mass_ref[...] * (own_ref[k] + other_ref[k] + received[k])
-        for k in range(2)
+        2.0 * current[k] - previous[k] + mass * (own[k] + other[k] + received[k]) for k in range(2)
     ]
 
 
-def drive_kernel(taps, signal, send):
+def drive_kernel(ins, outs, scratch):
+    taps, signal = (ref() for ref in ins)
+    (send,) = outs
     folded = []
     for t in range(2):
         products = taps[...] * signal[t : t + 1, :]
@@ -313,76 +314,69 @@
         send[q] = terms
 
 
-def first_kernel(now0, now1, connect, surface, driver, metric, weights, *refs):
-    tables, (back, partial, vals, table) = refs[:12], refs[12:]
-    fill_table(table, [now0[...], now1[...]])
-    gather_all(table, connect, vals)
-    partial[...] = driver_sums(vals, surface, driver)
-    operator(vals, metric, weights, tables[:6], tables[6:], back)
-
-
-def local_sums(where, res, connect, shared, partial, local, send, sums, table, sizes):
+def first_kernel(ins, outs, scratch):
+    connect, now0, now1, surface, driver, metric, weights, narrow, wide = ins
+    back, partial = outs
+    vals, table = scratch
+    fill_table(table, [now0()[...], now1()[...]])
+    gather_all(table, connect(), vals)
+    partial[...] = driver_sums(vals, surface(), driver())
+    operator(vals, metric, weights, wide, narrow, back)
+
+
+def local_sums(res, connect, shared, partial, local, send, sums, table, sizes):
     scatter_all(res, connect, sums)
     fields = to_fields(sums[...])
     for k in range(2):
         local[k] = fields[k]
+    local.flush()
     fill_table(table, fields)
-    fill_send(where, table, shared, partial, send, **sizes)
-
-
-def second_kernel(
-    where, back, partial, drive, connect, surface, driver, shared, local, send, res, sums, table, *, sizes
-):
-    for k in range(2):
-        res[k] = back[k]
-    add_source(0, drive, surface, driver, res)
-    local_sums(where, res, connect, shared, partial[...], local, send, sums, table, sizes)
-
-
-def third_kernel(
-    where,
-    now0,
-    now1,
-    prev0,
-    prev1,
-    mass,
-    own,
-    other,
-    recv,
-    drive,
-    connect,
-    surface,
-    driver,
-    shared,
-    metric,
-    weights,
-    *refs,
-    sizes,
-):
-    tables, (current, local, send, vals, res, sums, table) = refs[:12], refs[12:]
-    received = received_sums(where, shared, recv, **sizes)
+    fill_send(table, shared, partial, send, **sizes)
+
+
+def second_kernel(ins, outs, scratch, *, sizes):
+    drive, surface, driver, back, connect, partial, shared = ins
+    local, send = outs
+    res, sums, table = scratch
+    residual(0, drive(), surface(), driver(), back(), res)
+    local_sums(res, connect(), shared(), partial()[...], local, send, sums, table, sizes)
+
+
+def third_kernel(ins, outs, scratch, *, sizes):
+    recv, shared, now0, now1, prev0, prev1, mass, own, other = ins[:9]
+    connect, surface, driver, metric, weights, narrow, wide, drive = ins[9:]
+    current, local, send = outs
+    vals, back, res, sums, table = scratch
+    received = received_sums(shared(), recv(), **sizes)
     fields = advance(
-        [now0[...], now1[...]], [prev0[...], prev1[...]], mass, own, other, received
+        [now0()[...], now1()[...]],
+        [prev0()[...], prev1()[...]],
+        mass()[...],
+        own(),
+        other(),
+        received,
     )
     for k in range(2):
         current[k] = fields[k]
+    current.flush()
     fill_table(table, fields)
-    gather_all(table, connect, vals)
-    partial = driver_sums(vals, surface, driver)
-    operator(vals, metric, weights, tables[:6], tables[6:], res)
-    add_source(1, drive, surface, driver, res)
-    local_sums(where, res, connect, shared, partial, local, send, sums, table, sizes)
-
-
-def last_kernel(
-    where, current, now0, now1, mass, own, other, recv_before, recv, shared, signal, out0, out1, grad, *, sizes, scale
-):
-    received = received_sums(where, shared, recv, **sizes)
+    gather_all(table, connect(), vals)
+    partial = driver_sums(vals, surface(), driver())
+    operator(vals, metric, weights, wide, narrow, back)
+    residual(1, drive(), surface(), driver(), back, res)
+    local_sums(res, connect(), shared(), partial, local, send, sums, table, sizes)
+
+
+def last_kernel(ins, outs, scratch, *, sizes, scale):
+    recv, shared, current, now0, now1, mass, own, other, recv_before, signal = ins
+    out0, out1, grad = outs
+    received = received_sums(shared(), recv(), **sizes)
     fields = advance(
-        [current[0], current[1]], [now0[...], now1[...]], mass, own, other, received
-    )
-    out0[...] = fields[0]
-    out1[...] = fields[1]
+        current(), [now0()[...], now1()[...]], mass()[...], own(), other(), received
+    )
+    for out, field in zip((out0, out1), fields):
+        out[...] = field
+        out.flush()
 
     def column(ref):
         row = sum(ref[q, :, 2 * NN :] for q in range(ref.shape[0]))
@@ -390,23 +384,82 @@
         row = jnp.where(ids[0] == ids[1], jnp.broadcast_to(row, (8, LANES)), 0.0)
         return jnp.sum(row, axis=1, keepdims=True) * scale
 
-    grad[...] = column(recv) * signal[0:1, :] + column(recv_before) * signal[1:2, :]
-
-
-VMEM = pl.BlockSpec(memory_space=pltpu.VMEM)
-SMEM = pl.BlockSpec(memory_space=pltpu.SMEM)
-
-
-def call(body, name, scalars, arrays, outs, scratch):
+    window = signal()
+    grad[...] = column(recv()) * window[0:1, :] + column(recv_before()) * window[1:2, :]
+
+
+class Input:
+    def __init__(self, source, buffer, semaphore):
+        self.buffer = buffer
+        self.copy = pltpu.make_async_copy(source, buffer, semaphore)
+        self.waited = False
+        self.copy.start()
+
+    def __call__(self):
+        if not self.waited:
+            self.copy.wait()
+            self.waited = True
+        return self.buffer
+
+
+class Output:
+    def __init__(self, target, buffer, semaphore):
+        self.buffer = buffer
+        self.shape = buffer.shape
+        self.copy = pltpu.make_async_copy(buffer, target, semaphore)
+        self.sent = False
+
+    def __setitem__(self, index, value):
+        self.buffer[index] = value
+
+    def flush(self):
+        if not self.sent:
+            self.copy.start()
+            self.sent = True
+
+
+ANY = pl.BlockSpec(memory_space=pl.ANY)
+
+
+def call(body, name, arrays, outs, scratch, window=None):
+    n_in, n_out = len(arrays), len(outs)
+    shapes = [x.shape for x in arrays]
+    if window is not None:
+        shapes[-1] = (shapes[-1][0], window)
+
+    def kernel(*refs):
+        sources, refs = list(refs[:n_in]), refs[n_in:]
+        targets, refs = refs[:n_out], refs[n_out:]
+        in_buffers, refs = refs[:n_in], refs[n_in:]
+        out_buffers, refs = refs[:n_out], refs[n_out:]
+        own, (in_sems, out_sems) = refs[:-2], refs[-2:]
+        if window is not None:
+            start = pl.multiple_of(lax.axis_index(ALL) * window, LANES)
+            sources[-1] = sources[-1].at[:, pl.ds(start, window)]
+        ins = [Input(s, b, in_sems.at[i]) for i, (s, b) in enumerate(zip(sources, in_buffers))]
+        results = [
+            Output(t, b, out_sems.at[i]) for i, (t, b) in enumerate(zip(targets, out_buffers))
+        ]
+        body(ins, results, own)
+        for result in results:
+            result.flush()
+        for result in results:
+            result.copy.wait()
+        for value in ins:
+            value()
+
     return pl.pallas_call(
-        body,
+        kernel,
         out_shape=[jax.ShapeDtypeStruct(shape, F32) for shape in outs],
-        in_specs=[SMEM] * len(scalars) + [VMEM] * len(arrays),
-        out_specs=[VMEM] * len(outs),
-        scratch_shapes=[pltpu.VMEM(shape, dtype) for shape, dtype in scratch],
-        compiler_params=pltpu.CompilerParams(vmem_limit_bytes=56 << 20),
+        in_specs=[ANY] * n_in,
+        out_specs=[ANY] * n_out,
+        scratch_shapes=[pltpu.VMEM(shape, x.dtype) for shape, x in zip(shapes, arrays)]
+        + [pltpu.VMEM(shape, F32) for shape in outs]
+        + [pltpu.VMEM(shape, dtype) for shape, dtype in scratch]
+        + [pltpu.SemaphoreType.DMA((n_in,)), pltpu.SemaphoreType.DMA((n_out,))],
+        compiler_params=pltpu.CompilerParams(vmem_limit_bytes=64 << 20),
         name=name,
-    )(*scalars, *arrays)
+    )(*arrays)
 
 
 def on_device(
@@ -423,56 +476,52 @@
     filter_taps,
     signal,
 ):
-    forward, backward, weights = element_tables()
-    tables = [jnp.asarray(t) for t in forward + backward]
+    wide, narrow, weights = (jnp.asarray(t) for t in element_tables())
     count = connect.shape[0]
     peers = shared.shape[2]
     doms = lax.axis_size("dom")
     devices = lax.axis_size(ALL)
     width = filter_taps.shape[1]
     sizes = dict(doms=doms, peers=peers)
-    where = lax.axis_index("dom").astype(jnp.int32).reshape(1)
     plane = (LANES, LANES)
     now0, now1, prev0, prev1, mass = (
         x.reshape(plane) for x in (field_now, adjoint_now, field_prev, adjoint_next, inv_mass)
     )
     links = shared.reshape(3, peers, NN)
     driver_row = driver.reshape(1, count)
-    own_signal = lax.dynamic_slice_in_dim(signal, lax.axis_index(ALL) * width, width, 1)
+    if width % LANES == 0:
+        window, taps, samples = width, filter_taps, signal
+    else:
+        window = None
+        samples = lax.dynamic_slice_in_dim(signal, lax.axis_index(ALL) * width, width, 1)
+        pad = ((0, 0), (0, -width % LANES))
+        taps, samples = jnp.pad(filter_taps, pad), jnp.pad(samples, pad)
+
     def trade(x):
         return lax.all_to_all(x, ALL, 0, 0, tiled=True)
 
     def swap(x):
         return lax.ppermute(x, "chip", [(0, 1), (1, 0)])
 
-    if width < LANES:
-        pad = ((0, 0), (0, LANES - width))
-        tap_block, signal_block = jnp.pad(filter_taps, pad), jnp.pad(own_signal, pad)
-    else:
-        tap_block, signal_block = filter_taps, own_signal
-    (terms,) = call(
-        drive_kernel, "drive", [], [tap_block, signal_block], [(devices, 8, LANES)], []
-    )
-    drive = trade(terms)
-    nodes = ((2,) + plane, F32)
+    nodes = (2,) + plane
     elements = ((2, count, NN), F32)
     sums = ((4 * ROWS, COLS), F32)
     table = ((4 * ROWS, COLS), BF)
     packet = (devices, 1, PACKET)
+    (terms,) = call(drive_kernel, "drive", [taps, samples], [(devices, 8, LANES)], [], window)
+    drive = trade(terms)
     back, partial = call(
         first_kernel,
         "operator0",
-        [],
-        [now0, now1, connect, surface, driver_row, metric, jnp.asarray(weights)] + tables,
+        [connect, now0, now1, surface, driver_row, metric, weights, narrow, wide],
         [elements[0], (1, LANES)],
         [elements, table],
     )
     local, send = call(
         functools.partial(second_kernel, sizes=sizes),
         "assemble0",
-        [where],
-        [back, partial, drive, connect, surface, driver_row, links],
-        [nodes[0], packet],
+        [drive, surface, driver_row, back, connect, partial, links],
+        [nodes, packet],
         [elements, sums, table],
     )
     other = swap(local)
@@ -480,25 +529,22 @@
     current, local, send = call(
         functools.partial(third_kernel, sizes=sizes),
         "step1",
-        [where],
-        [now0, now1, prev0, prev1, mass, local, other, recv0, drive, connect, surface, driver_row, links]
-        + [metric, jnp.asarray(weights)]
-        + tables,
-        [nodes[0], nodes[0], packet],
-        [elements, elements, sums, table],
+        [recv0, links, now0, now1, prev0, prev1, mass, local, other]
+        + [connect, surface, driver_row, metric, weights, narrow, wide, drive],
+        [nodes, nodes, packet],
+        [elements, elements, elements, sums, table],
     )
     other = swap(local)
     recv1 = trade(send)
     out0, out1, grad = call(
-        functools.partial(
-            last_kernel, sizes=sizes, scale=1.0 / math.sqrt(NN * count * devices)
-        ),
+        functools.partial(last_kernel, sizes=sizes, scale=1.0 / math.sqrt(NN * count * devices)),
         "finish",
-        [where],
-        [current, now0, now1, mass, local, other, recv0, recv1, links, own_signal],
-        [plane, plane, (8, width)],
+        [recv1, links, current, now0, now1, mass, local, other, recv0, samples],
+        [plane, plane, (8, taps.shape[1])],
         [],
-    )
+        window,
+    )
+    grad = grad[:, :width]
     return out0.reshape(1, -1), out1.reshape(1, -1), grad
 
 

time: 82.2 us -> 68.8 us (0.84)
  Pallas kernels: 46.7 us -> 35.8 us
  local copies, waits for them, and re-layouts: 3.18 us -> 0 us
    pallas_call x5, Pallas kernels: 46.7 us -> 35.8 us  [call(): pl.pallas_call(kernel, out_shape=[jax.ShapeDtypeStruct(shape, F32) for sh...]
    unnamed x16 -> x0, local copies, waits for them, and re-layouts: 2.6 us -> none
  transfers between devices with their start and end apart: 5 -> 5, of which waited for: 4 -> 4; matrix products, arithmetic and copies ran while one was open for 0% -> 0% of each run, Pallas kernels for 12% -> 13%
where the time goes in v3:
time: 68.8 us; the launch traced here: 68.4 us
  Pallas kernels  35.8 us (52%)
  starting transfers between devices  18.2 us (26%)
  waiting for transfers between devices  13.4 us (19%)
  between operations  0.86 us (1%)
    pallas_call x5, Pallas kernels, call(): pl.pallas_call(kernel, out_shape=[jax.ShapeDtypeStruct(shape, F32) for sh...  35.8 us
    all_to_all x3, starting transfers between devices, trade(): return lax.all_to_all(x, ALL, 0, 0, tiled=True)  17.6 us
    all_to_all x3, waiting for transfers between devices, trade(): return lax.all_to_all(x, ALL, 0, 0, tiled=True)  10.6 us
    ppermute x2, waiting for transfers between devices, swap(): return lax.ppermute(x, 'chip', [(0, 1), (1, 0)])  2.86 us
  transfers between devices with their start and end apart: 5, of which 4 were waited for; matrix products, arithmetic and copies ran while one was open for 0% of the time, Pallas kernels for 13%

profile of v3, /device:TPU:0, one launch (start us, length us, event | category | flops | bytes accessed | tf_op | source)
XLA Modules:
  0.0 68.4 jit_solution(10947143737862862920)
XLA Ops:
  0.6 1.5 %drive.1 = f32[16,8,128]{2,1,0:T(8,128)} custom-call(f32[8,128]{1,0:T(8,128)} %refs_0_.2, f32[2,2048]{1,0:T(2,128)} %refs_9_.3), custom_call_target="tpu_custom_call" | custom-call | tf_op jit(solution)/shard_map/drive/pallas_call | solution.py:451
  2.1 7.4 %all-to-all-start = ((f32[16,8,128]{2,1,0:T(8,128)}), f32[16,8,128]{2,1,0:T(8,128)}, u32[]{:S(2)}, u32[]{:S(2)}) async-start(f32[16,8,128]{2,1,0:T(8,128)} %drive.1), calls=%async_computation | async-start | bytes 131072 | tf_op jit(solution)/shard_map/all_to_all | solution.py:501
  9.6 9.1 %operator0.1 = (f32[2,64,512]{2,1,0:T(8,128)}, f32[1,128]{1,0:T(1,128)}) custom-call(s32[64,512]{1,0:T(8,128)} %refs_9_.2, f32[128,128]{1,0:T(8,128)} %bitcast.9, f32[128,128]{1,0:T(8,128)} %bitcast.12, f32[64,512]{1,0:T(8,128)} %refs_10_.1, s32[1,64]{1,0:T(1,128)} %bitcast.22, f32[64,1536]{1,0:T(8,128)} %refs_12_.1, ...), custom_call_target="tpu_custom_call" | custom-call | tf_op jit(solution)/shard_map/operator0/pallas_call | solution.py:451
  18.6 0.0 all-to-all-done.refs_0_.refs_16_
  18.6 7.5 %assemble0.1 = (f32[2,128,128]{2,1,0:T(8,128)}, f32[16,1,1152]{2,1,0:T(1,128)}) custom-call(f32[16,8,128]{2,1,0:T(8,128)} %all-to-all-done.refs_0_.refs_16_, f32[64,512]{1,0:T(8,128)} %refs_10_.1, s32[1,64]{1,0:T(1,128)} %bitcast.23, f32[2,64,512]{2,1,0:T(8,128)} %get-tuple-element.13.refs_3_, s32[64,512]{1,0:T(8,128)} %refs_9_.2, ...), custom_call_target="tpu_custom_call" | custom-call | tf_op jit(solution)/shard_map/assemble0/pallas_call | solution.py:451
  26.1 6.0 %all-to-all-start.1 = ((f32[16,1,1152]{2,1,0:T(1,128)}), f32[16,1,1152]{2,1,0:T(1,128)}, u32[]{:S(2)}, u32[]{:S(2)}) async-start(f32[16,1,1152]{2,1,0:T(1,128)} %get-tuple-element.15), calls=%async_computation.1 | async-start | bytes 147456 | tf_op jit(solution)/shard_map/all_to_all | solution.py:501
  32.1 0.4 collective-permute-start
  32.5 1.3 %collective-permute-done.refs_8_ = f32[2,128,128]{2,1,0:T(8,128)} collective-permute-done((f32[2,128,128]{2,1,0:T(8,128)}, f32[2,128,128]{2,1,0:T(8,128)}, u32[]{:S(2)}, u32[]{:S(2)}) %collective-permute-start) | collective-permute-done | bytes 131104 | tf_op jit(solution)/shard_map/ppermute | solution.py:504
  33.9 5.3 %all-to-all-done.1.refs_0_.refs_8_ = f32[16,1,1152]{2,1,0:T(1,128)} async-done(((f32[16,1,1152]{2,1,0:T(1,128)}), f32[16,1,1152]{2,1,0:T(1,128)}, u32[]{:S(2)}, u32[]{:S(2)}) %all-to-all-start.1) | async-done | bytes 73760 | tf_op jit(solution)/shard_map/all_to_all | solution.py:501
  39.2 15.4 %step1.1 = (f32[2,128,128]{2,1,0:T(8,128)}, f32[2,128,128]{2,1,0:T(8,128)}, f32[16,1,1152]{2,1,0:T(1,128)}) custom-call(f32[16,1,1152]{2,1,0:T(1,128)} %all-to-all-done.1.refs_0_.refs_8_, s32[3,2,512]{2,1,0:T(2,128)} %bitcast.18, f32[128,128]{1,0:T(8,128)} %bitcast.10, f32[128,128]{1,0:T(8,128)} %bitcast.13, f32[128,128]{1,0:T(8,128)} %bitcast.20, ...), custom_call_target="tpu_custom_call" | custom-call | tf_op jit(solution)/shard_map/step1/pallas_call | solution.py:451
  54.6 4.2 %all-to-all-start.2 = ((f32[16,1,1152]{2,1,0:T(1,128)}), f32[16,1,1152]{2,1,0:T(1,128)}, u32[]{:S(2)}, u32[]{:S(2)}) async-start(f32[16,1,1152]{2,1,0:T(1,128)} %get-tuple-element.17), calls=%async_computation.2 | async-start | bytes 147456 | tf_op jit(solution)/shard_map/all_to_all | solution.py:501
  58.7 0.2 collective-permute-start.1
  59.0 1.5 %collective-permute-done.1.refs_7_ = f32[2,128,128]{2,1,0:T(8,128)} collective-permute-done((f32[2,128,128]{2,1,0:T(8,128)}, f32[2,128,128]{2,1,0:T(8,128)}, u32[]{:S(2)}, u32[]{:S(2)}) %collective-permute-start.1) | collective-permute-done | bytes 131104 | tf_op jit(solution)/shard_map/ppermute | solution.py:504
  60.5 5.3 %all-to-all-done.2.refs_0_ = f32[16,1,1152]{2,1,0:T(1,128)} async-done(((f32[16,1,1152]{2,1,0:T(1,128)}), f32[16,1,1152]{2,1,0:T(1,128)}, u32[]{:S(2)}, u32[]{:S(2)}) %all-to-all-start.2) | async-done | bytes 73760 | tf_op jit(solution)/shard_map/all_to_all | solution.py:501
  65.8 2.5 %finish.1 = (f32[128,128]{1,0:T(8,128)}, f32[128,128]{1,0:T(8,128)}, f32[8,128]{1,0:T(8,128)}) custom-call(f32[16,1,1152]{2,1,0:T(1,128)} %all-to-all-done.2.refs_0_, s32[3,2,512]{2,1,0:T(2,128)} %bitcast.19, f32[2,128,128]{2,1,0:T(8,128)} %get-tuple-element.18.refs_2_, f32[128,128]{1,0:T(8,128)} %bitcast.11, f32[128,128]{1,0:T(8,128)} %bitcast.14, ...), custom_call_target="tpu_custom_call" | custom-call | tf_op jit(solution)/shard_map/finish/pallas_call | solution.py:451
Async XLA Ops:
  2.1 16.5 %all-to-all-start = ((f32[16,8,128]{2,1,0:T(8,128)}), f32[16,8,128]{2,1,0:T(8,128)}, u32[]{:S(2)}, u32[]{:S(2)}) async-start(f32[16,8,128]{2,1,0:T(8,128)} %drive.1), calls=%async_computation | async-start | bytes 131072 | tf_op jit(solution)/shard_map/all_to_all | solution.py:501
  26.1 13.1 %all-to-all-start.1 = ((f32[16,1,1152]{2,1,0:T(1,128)}), f32[16,1,1152]{2,1,0:T(1,128)}, u32[]{:S(2)}, u32[]{:S(2)}) async-start(f32[16,1,1152]{2,1,0:T(1,128)} %get-tuple-element.15), calls=%async_computation.1 | async-start | bytes 147456 | tf_op jit(solution)/shard_map/all_to_all | solution.py:501
  32.1 1.8 %collective-permute-start = (f32[2,128,128]{2,1,0:T(8,128)}, f32[2,128,128]{2,1,0:T(8,128)}, u32[]{:S(2)}, u32[]{:S(2)}) collective-permute-start(f32[2,128,128]{2,1,0:T(8,128)} %get-tuple-element.16.refs_7_), channel_id=1, source_target_pairs={{0,1},{1,0},{2,3},{3,2},{4,5},{5,4},{6,7},{7,6},{8,9},{9,8},{10,11... | collective-permute-start | bytes 393224 | tf_op jit(solution)/shard_map/ppermute | solution.py:504
  54.6 11.2 %all-to-all-start.2 = ((f32[16,1,1152]{2,1,0:T(1,128)}), f32[16,1,1152]{2,1,0:T(1,128)}, u32[]{:S(2)}, u32[]{:S(2)}) async-start(f32[16,1,1152]{2,1,0:T(1,128)} %get-tuple-element.17), calls=%async_computation.2 | async-start | bytes 147456 | tf_op jit(solution)/shard_map/all_to_all | solution.py:501
  58.7 1.8 %collective-permute-start.1 = (f32[2,128,128]{2,1,0:T(8,128)}, f32[2,128,128]{2,1,0:T(8,128)}, u32[]{:S(2)}, u32[]{:S(2)}) collective-permute-start(f32[2,128,128]{2,1,0:T(8,128)} %get-tuple-element.19.refs_6_), channel_id=1, source_target_pairs={{0,1},{1,0},{2,3},{3,2},{4,5},{5,4},{6,7},{7,6},{8,9},{9,8},{10,11... | collective-permute-start | bytes 393224 | tf_op jit(solution)/shard_map/ppermute | solution.py:504

commit v4 on v3

--- a/solution.py
+++ b/solution.py
@@ -406,60 +406,87 @@
     def __init__(self, target, buffer, semaphore):
         self.buffer = buffer
         self.shape = buffer.shape
-        self.copy = pltpu.make_async_copy(buffer, target, semaphore)
+        self.copy = None if target is None else pltpu.make_async_copy(buffer, target, semaphore)
         self.sent = False
 
     def __setitem__(self, index, value):
         self.buffer[index] = value
 
     def flush(self):
-        if not self.sent:
+        if self.copy is not None and not self.sent:
             self.copy.start()
             self.sent = True
 
+    def wait(self):
+        if self.copy is not None:
+            self.copy.wait()
+
+
+class Held:
+    def __init__(self, value):
+        self.value = value
+
 
 ANY = pl.BlockSpec(memory_space=pl.ANY)
-
-
-def call(body, name, arrays, outs, scratch, window=None):
+VMEM = pl.BlockSpec(memory_space=pltpu.VMEM)
+
+
+def call(body, name, arrays, outs, scratch, window=None, held=()):
     n_in, n_out = len(arrays), len(outs)
-    shapes = [x.shape for x in arrays]
+    moved = [i for i, x in enumerate(arrays) if not isinstance(x, Held)]
+    sent = [i for i in range(n_out) if i not in held]
+    values = [
+        pltpu.with_memory_space_constraint(x.value, pltpu.VMEM)
+        if isinstance(x, Held)
+        else pltpu.with_memory_space_constraint(x, pltpu.HBM)
+        for x in arrays
+    ]
+    shapes = [x.shape for x in values]
     if window is not None:
         shapes[-1] = (shapes[-1][0], window)
 
     def kernel(*refs):
         sources, refs = list(refs[:n_in]), refs[n_in:]
         targets, refs = refs[:n_out], refs[n_out:]
-        in_buffers, refs = refs[:n_in], refs[n_in:]
-        out_buffers, refs = refs[:n_out], refs[n_out:]
+        in_buffers, refs = refs[: len(moved)], refs[len(moved) :]
+        out_buffers, refs = refs[: len(sent)], refs[len(sent) :]
         own, (in_sems, out_sems) = refs[:-2], refs[-2:]
         if window is not None:
             start = pl.multiple_of(lax.axis_index(ALL) * window, LANES)
             sources[-1] = sources[-1].at[:, pl.ds(start, window)]
-        ins = [Input(s, b, in_sems.at[i]) for i, (s, b) in enumerate(zip(sources, in_buffers))]
-        results = [
-            Output(t, b, out_sems.at[i]) for i, (t, b) in enumerate(zip(targets, out_buffers))
-        ]
+        ins = [functools.partial(lambda ref: ref, ref) for ref in sources]
+        for at, i in enumerate(moved):
+            ins[i] = Input(sources[i], in_buffers[at], in_sems.at[at])
+        results = [Output(None, ref, None) for ref in targets]
+        for at, i in enumerate(sent):
+            results[i] = Output(targets[i], out_buffers[at], out_sems.at[at])
         body(ins, results, own)
         for result in results:
             result.flush()
         for result in results:
-            result.copy.wait()
+            result.wait()
         for value in ins:
             value()
 
-    return pl.pallas_call(
+    results = pl.pallas_call(
         kernel,
-        out_shape=[jax.ShapeDtypeStruct(shape, F32) for shape in outs],
-        in_specs=[ANY] * n_in,
-        out_specs=[ANY] * n_out,
-        scratch_shapes=[pltpu.VMEM(shape, x.dtype) for shape, x in zip(shapes, arrays)]
-        + [pltpu.VMEM(shape, F32) for shape in outs]
+        out_shape=[
+            pltpu.VMEM(shape, F32) if i in held else jax.ShapeDtypeStruct(shape, F32)
+            for i, shape in enumerate(outs)
+        ],
+        in_specs=[VMEM if isinstance(x, Held) else ANY for x in arrays],
+        out_specs=[VMEM if i in held else ANY for i in range(n_out)],
+        scratch_shapes=[pltpu.VMEM(shapes[i], values[i].dtype) for i in moved]
+        + [pltpu.VMEM(outs[i], F32) for i in sent]
         + [pltpu.VMEM(shape, dtype) for shape, dtype in scratch]
-        + [pltpu.SemaphoreType.DMA((n_in,)), pltpu.SemaphoreType.DMA((n_out,))],
-        compiler_params=pltpu.CompilerParams(vmem_limit_bytes=64 << 20),
+        + [
+            pltpu.SemaphoreType.DMA((max(len(moved), 1),)),
+            pltpu.SemaphoreType.DMA((max(len(sent), 1),)),
+        ],
+        compiler_params=pltpu.CompilerParams(vmem_limit_bytes=40 << 20),
         name=name,
-    )(*arrays)
+    )(*values)
+    return [Held(x) if i in held else x for i, x in enumerate(results)]
 
 
 def on_device(
@@ -498,17 +525,17 @@
         taps, samples = jnp.pad(filter_taps, pad), jnp.pad(samples, pad)
 
     def trade(x):
-        return lax.all_to_all(x, ALL, 0, 0, tiled=True)
+        return Held(lax.all_to_all(x.value, ALL, 0, 0, tiled=True))
 
     def swap(x):
-        return lax.ppermute(x, "chip", [(0, 1), (1, 0)])
+        return Held(lax.ppermute(x.value, "chip", [(0, 1), (1, 0)]))
 
     nodes = (2,) + plane
     elements = ((2, count, NN), F32)
     sums = ((4 * ROWS, COLS), F32)
     table = ((4 * ROWS, COLS), BF)
     packet = (devices, 1, PACKET)
-    (terms,) = call(drive_kernel, "drive", [taps, samples], [(devices, 8, LANES)], [], window)
+    (terms,) = call(drive_kernel, "drive", [taps, samples], [(devices, 8, LANES)], [], window, (0,))
     drive = trade(terms)
     back, partial = call(
         first_kernel,
@@ -516,6 +543,7 @@
         [connect, now0, now1, surface, driver_row, metric, weights, narrow, wide],
         [elements[0], (1, LANES)],
         [elements, table],
+        held=(0, 1),
     )
     local, send = call(
         functools.partial(second_kernel, sizes=sizes),
@@ -523,6 +551,7 @@
         [drive, surface, driver_row, back, connect, partial, links],
         [nodes, packet],
         [elements, sums, table],
+        held=(0, 1),
     )
     other = swap(local)
     recv0 = trade(send)
@@ -533,6 +562,7 @@
         + [connect, surface, driver_row, metric, weights, narrow, wide, drive],
         [nodes, nodes, packet],
         [elements, elements, elements, sums, table],
+        held=(0, 1, 2),
     )
     other = swap(local)
     recv1 = trade(send)

time: 68.8 us -> 66.4 us (0.965)
  Pallas kernels: 35.8 us -> 34.1 us
    pallas_call x5, Pallas kernels: 35.8 us -> 34.1 us  [call(): pl.pallas_call(kernel, out_shape=[pltpu.VMEM(shape, F32) if i in held els...]
    ppermute x2, waiting for transfers between devices: 2.86 us -> 2.11 us  [swap(): return Held(lax.ppermute(x.value, 'chip', [(0, 1), (1, 0)]))]
where the time goes in v4:
time: 66.4 us; the launch traced here: 65.8 us
  Pallas kernels  34.1 us (51%)
  starting transfers between devices  17.7 us (27%)
  waiting for transfers between devices  13.2 us (20%)
  between operations  0.86 us (1%)
    pallas_call x5, Pallas kernels, call(): pl.pallas_call(kernel, out_shape=[pltpu.VMEM(shape, F32) if i in held els...  34.1 us
    all_to_all x3, starting transfers between devices, trade(): return Held(lax.all_to_all(x.value, ALL, 0, 0, tiled=True))  16.9 us
    all_to_all x3, waiting for transfers between devices, trade(): return Held(lax.all_to_all(x.value, ALL, 0, 0, tiled=True))  11.1 us
    ppermute x2, waiting for transfers between devices, swap(): return Held(lax.ppermute(x.value, 'chip', [(0, 1), (1, 0)]))  2.11 us
  transfers between devices with their start and end apart: 5, of which 4 were waited for; matrix products, arithmetic and copies ran while one was open for 0% of the time, Pallas kernels for 13%

profile of v4, /device:TPU:0, one launch (start us, length us, event | category | flops | bytes accessed | tf_op | source)
XLA Modules:
  0.0 65.8 jit_solution(7714936253871055845)
XLA Ops:
  0.6 1.5 %drive.1 = f32[16,8,128]{2,1,0:T(8,128)} custom-call(f32[8,128]{1,0:T(8,128)} %refs_0_.2, f32[2,2048]{1,0:T(2,128)} %refs_9_.3), custom_call_target="tpu_custom_call" | custom-call | tf_op jit(solution)/shard_map/drive/pallas_call | solution.py:471
  2.1 7.4 %all-to-all-start = ((f32[16,8,128]{2,1,0:T(8,128)}), f32[16,8,128]{2,1,0:T(8,128)S(1)}, u32[]{:S(2)}, u32[]{:S(2)}) async-start(f32[16,8,128]{2,1,0:T(8,128)} %drive.1), calls=%async_computation | async-start | bytes 131072 | tf_op jit(solution)/shard_map/all_to_all | solution.py:528
  9.5 8.4 %operator0.1 = (f32[2,64,512]{2,1,0:T(8,128)S(1)}, f32[1,128]{1,0:T(1,128)S(1)}) custom-call(s32[64,512]{1,0:T(8,128)} %refs_9_.2, f32[128,128]{1,0:T(8,128)} %bitcast.9, f32[128,128]{1,0:T(8,128)} %bitcast.12, f32[64,512]{1,0:T(8,128)} %refs_10_.1, s32[1,64]{1,0:T(1,128)} %bitcast.22, f32[64,1536]{1,0:T(8,128)} %refs_12_.1, ...), custom_call_target="tpu_custom_call" | custom-call | tf_op jit(solution)/shard_map/operator0/pallas_call | solution.py:471
  17.9 0.0 all-to-all-done.refs_0_.refs_16_
  17.9 7.3 %assemble0.1 = (f32[2,128,128]{2,1,0:T(8,128)S(1)}, f32[16,1,1152]{2,1,0:T(1,128)}) custom-call(f32[16,8,128]{2,1,0:T(8,128)S(1)} %all-to-all-done.refs_0_.refs_16_, f32[64,512]{1,0:T(8,128)} %refs_10_.1, s32[1,64]{1,0:T(1,128)} %bitcast.23, f32[2,64,512]{2,1,0:T(8,128)S(1)} %get-tuple-element.13.refs_3_, s32[64,512]{1,0:T(8,128)} %refs_9_.2, ...), custom_call_target="tpu_custom_call" | custom-call | tf_op jit(solution)/shard_map/assemble0/pallas_call | solution.py:471
  25.1 6.0 %all-to-all-start.1 = ((f32[16,1,1152]{2,1,0:T(1,128)}), f32[16,1,1152]{2,1,0:T(1,128)S(1)}, u32[]{:S(2)}, u32[]{:S(2)}) async-start(f32[16,1,1152]{2,1,0:T(1,128)} %get-tuple-element.15), calls=%async_computation.1 | async-start | bytes 147456 | tf_op jit(solution)/shard_map/all_to_all | solution.py:528
  31.2 0.5 collective-permute-start
  31.6 1.0 %collective-permute-done.refs_8_ = f32[2,128,128]{2,1,0:T(8,128)S(1)} collective-permute-done((f32[2,128,128]{2,1,0:T(8,128)S(1)}, f32[2,128,128]{2,1,0:T(8,128)S(1)}, u32[]{:S(2)}, u32[]{:S(2)}) %collective-permute-start) | collective-permute-done | bytes 131104 | tf_op jit(solution)/shard_map/ppermute | solution.py:531
  32.6 5.6 %all-to-all-done.1.refs_0_.refs_8_ = f32[16,1,1152]{2,1,0:T(1,128)S(1)} async-done(((f32[16,1,1152]{2,1,0:T(1,128)}), f32[16,1,1152]{2,1,0:T(1,128)S(1)}, u32[]{:S(2)}, u32[]{:S(2)}) %all-to-all-start.1) | async-done | bytes 73760 | tf_op jit(solution)/shard_map/all_to_all | solution.py:528
  38.2 14.9 %step1.1 = (f32[2,128,128]{2,1,0:T(8,128)S(1)}, f32[2,128,128]{2,1,0:T(8,128)S(1)}, f32[16,1,1152]{2,1,0:T(1,128)}) custom-call(f32[16,1,1152]{2,1,0:T(1,128)S(1)} %all-to-all-done.1.refs_0_.refs_8_, s32[3,2,512]{2,1,0:T(2,128)} %bitcast.18, f32[128,128]{1,0:T(8,128)} %bitcast.10, f32[128,128]{1,0:T(8,128)} %bitcast.13, f32[128,128]{1,0:T(8,128)} %bitcast.20, ...), custom_call_target="tpu_custom_call" | custom-call | tf_op jit(solution)/shard_map/step1/pallas_call | solution.py:471
  53.0 3.5 %all-to-all-start.2 = ((f32[16,1,1152]{2,1,0:T(1,128)}), f32[16,1,1152]{2,1,0:T(1,128)S(1)}, u32[]{:S(2)}, u32[]{:S(2)}) async-start(f32[16,1,1152]{2,1,0:T(1,128)} %get-tuple-element.17), calls=%async_computation.2 | async-start | bytes 147456 | tf_op jit(solution)/shard_map/all_to_all | solution.py:528
  56.6 0.3 collective-permute-start.1
  56.9 1.1 %collective-permute-done.1.refs_7_ = f32[2,128,128]{2,1,0:T(8,128)S(1)} collective-permute-done((f32[2,128,128]{2,1,0:T(8,128)S(1)}, f32[2,128,128]{2,1,0:T(8,128)S(1)}, u32[]{:S(2)}, u32[]{:S(2)}) %collective-permute-start.1) | collective-permute-done | bytes 131104 | tf_op jit(solution)/shard_map/ppermute | solution.py:531
  58.0 5.6 %all-to-all-done.2.refs_0_ = f32[16,1,1152]{2,1,0:T(1,128)S(1)} async-done(((f32[16,1,1152]{2,1,0:T(1,128)}), f32[16,1,1152]{2,1,0:T(1,128)S(1)}, u32[]{:S(2)}, u32[]{:S(2)}) %all-to-all-start.2) | async-done | bytes 73760 | tf_op jit(solution)/shard_map/all_to_all | solution.py:528
  63.5 2.1 %finish.1 = (f32[128,128]{1,0:T(8,128)}, f32[128,128]{1,0:T(8,128)}, f32[8,128]{1,0:T(8,128)}) custom-call(f32[16,1,1152]{2,1,0:T(1,128)S(1)} %all-to-all-done.2.refs_0_, s32[3,2,512]{2,1,0:T(2,128)} %bitcast.19, f32[2,128,128]{2,1,0:T(8,128)S(1)} %get-tuple-element.18.refs_2_, f32[128,128]{1,0:T(8,128)} %bitcast.11, f32[128,128]{1,0:T(8,128)} %bitcast.14, ...), custom_call_target="tpu_custom_call" | custom-call | tf_op jit(solution)/shard_map/finish/pallas_call | solution.py:471
Async XLA Ops:
  2.1 15.7 %all-to-all-start = ((f32[16,8,128]{2,1,0:T(8,128)}), f32[16,8,128]{2,1,0:T(8,128)S(1)}, u32[]{:S(2)}, u32[]{:S(2)}) async-start(f32[16,8,128]{2,1,0:T(8,128)} %drive.1), calls=%async_computation | async-start | bytes 131072 | tf_op jit(solution)/shard_map/all_to_all | solution.py:528
  25.1 13.0 %all-to-all-start.1 = ((f32[16,1,1152]{2,1,0:T(1,128)}), f32[16,1,1152]{2,1,0:T(1,128)S(1)}, u32[]{:S(2)}, u32[]{:S(2)}) async-start(f32[16,1,1152]{2,1,0:T(1,128)} %get-tuple-element.15), calls=%async_computation.1 | async-start | bytes 147456 | tf_op jit(solution)/shard_map/all_to_all | solution.py:528
  31.2 1.4 %collective-permute-start = (f32[2,128,128]{2,1,0:T(8,128)S(1)}, f32[2,128,128]{2,1,0:T(8,128)S(1)}, u32[]{:S(2)}, u32[]{:S(2)}) collective-permute-start(f32[2,128,128]{2,1,0:T(8,128)S(1)} %get-tuple-element.16.refs_7_), channel_id=1, source_target_pairs={{0,1},{1,0},{2,3},{3,2},{4,5},{5,4},{6,7},{7,6},{8,9},{9,8},{10,11... | collective-permute-start | bytes 393224 | tf_op jit(solution)/shard_map/ppermute | solution.py:531
  53.0 10.5 %all-to-all-start.2 = ((f32[16,1,1152]{2,1,0:T(1,128)}), f32[16,1,1152]{2,1,0:T(1,128)S(1)}, u32[]{:S(2)}, u32[]{:S(2)}) async-start(f32[16,1,1152]{2,1,0:T(1,128)} %get-tuple-element.17), calls=%async_computation.2 | async-start | bytes 147456 | tf_op jit(solution)/shard_map/all_to_all | solution.py:528
  56.6 1.4 %collective-permute-start.1 = (f32[2,128,128]{2,1,0:T(8,128)S(1)}, f32[2,128,128]{2,1,0:T(8,128)S(1)}, u32[]{:S(2)}, u32[]{:S(2)}) collective-permute-start(f32[2,128,128]{2,1,0:T(8,128)S(1)} %get-tuple-element.19.refs_6_), channel_id=1, source_target_pairs={{0,1},{1,0},{2,3},{3,2},{4,5},{5,4},{6,7},{7,6},{8,9},{9,8},{10,11... | collective-permute-start | bytes 393224 | tf_op jit(solution)/shard_map/ppermute | solution.py:531

commit v5 on v4

--- a/solution.py
+++ b/solution.py
@@ -293,14 +293,28 @@
     return to_fields(total)
 
 
-def advance(current, previous, mass, own, other, received):
-    return [
-        2.0 * current[k] - previous[k] + mass * (own[k] + other[k] + received[k]) for k in range(2)
-    ]
+def advance(base, mass, received):
+    return [base[k] + mass * received[k] for k in range(2)]
+
+
+def fill_base(base, current, previous, mass, own, other):
+    for k in range(2):
+        base[k] = 2.0 * current[k] - previous[k] + mass * (own[k] + other[k])
+
+
+def base_kernel(ins, outs, scratch):
+    own, other, mass, now0, now1, prev0, prev1 = (ref() for ref in ins[:7])
+    current, previous = [now0[...], now1[...]], [prev0[...], prev1[...]]
+    fill_base(outs[0], current, previous, mass[...], own, other)
+
+
+def last_base_kernel(ins, outs, scratch):
+    own, other, mass, current, now0, now1 = (ref() for ref in ins[:6])
+    fill_base(outs[0], current, [now0[...], now1[...]], mass[...], own, other)
 
 
 def drive_kernel(ins, outs, scratch):
-    taps, signal = (ref() for ref in ins)
+    taps, signal = ins[0](), ins[-1]()
     (send,) = outs
     folded = []
     for t in range(2):
@@ -315,7 +329,7 @@
 
 
 def first_kernel(ins, outs, scratch):
-    connect, now0, now1, surface, driver, metric, weights, narrow, wide = ins
+    connect, now0, now1, surface, driver, metric, weights, narrow, wide = ins[:9]
     back, partial = outs
     vals, table = scratch
     fill_table(table, [now0()[...], now1()[...]])
@@ -343,19 +357,11 @@
 
 
 def third_kernel(ins, outs, scratch, *, sizes):
-    recv, shared, now0, now1, prev0, prev1, mass, own, other = ins[:9]
-    connect, surface, driver, metric, weights, narrow, wide, drive = ins[9:]
+    recv, base, mass, shared, connect, surface, driver, metric, weights, narrow, wide, drive = ins
     current, local, send = outs
     vals, back, res, sums, table = scratch
     received = received_sums(shared(), recv(), **sizes)
-    fields = advance(
-        [now0()[...], now1()[...]],
-        [prev0()[...], prev1()[...]],
-        mass()[...],
-        own(),
-        other(),
-        received,
-    )
+    fields = advance(base(), mass()[...], received)
     for k in range(2):
         current[k] = fields[k]
     current.flush()
@@ -368,12 +374,10 @@
 
 
 def last_kernel(ins, outs, scratch, *, sizes, scale):
-    recv, shared, current, now0, now1, mass, own, other, recv_before, signal = ins
+    recv, base, mass, shared, recv_before, signal = ins
     out0, out1, grad = outs
     received = received_sums(shared(), recv(), **sizes)
-    fields = advance(
-        current(), [now0()[...], now1()[...]], mass()[...], own(), other(), received
-    )
+    fields = advance(base(), mass()[...], received)
     for out, field in zip((out0, out1), fields):
         out[...] = field
         out.flush()
@@ -431,9 +435,10 @@
 VMEM = pl.BlockSpec(memory_space=pltpu.VMEM)
 
 
-def call(body, name, arrays, outs, scratch, window=None, held=()):
+def call(body, name, arrays, outs, scratch, window=None, held=(), keep=()):
     n_in, n_out = len(arrays), len(outs)
-    moved = [i for i, x in enumerate(arrays) if not isinstance(x, Held)]
+    fetched = [i for i, x in enumerate(arrays) if not isinstance(x, Held)]
+    moved = [i for i in fetched if i not in keep]
     sent = [i for i in range(n_out) if i not in held]
     values = [
         pltpu.with_memory_space_constraint(x.value, pltpu.VMEM)
@@ -448,6 +453,7 @@
     def kernel(*refs):
         sources, refs = list(refs[:n_in]), refs[n_in:]
         targets, refs = refs[:n_out], refs[n_out:]
+        kept, refs = refs[: len(keep)], refs[len(keep) :]
         in_buffers, refs = refs[: len(moved)], refs[len(moved) :]
         out_buffers, refs = refs[: len(sent)], refs[len(sent) :]
         own, (in_sems, out_sems) = refs[:-2], refs[-2:]
@@ -455,8 +461,9 @@
             start = pl.multiple_of(lax.axis_index(ALL) * window, LANES)
             sources[-1] = sources[-1].at[:, pl.ds(start, window)]
         ins = [functools.partial(lambda ref: ref, ref) for ref in sources]
-        for at, i in enumerate(moved):
-            ins[i] = Input(sources[i], in_buffers[at], in_sems.at[at])
+        buffers = dict(zip(moved, in_buffers)) | dict(zip(keep, kept))
+        for at, i in enumerate(fetched):
+            ins[i] = Input(sources[i], buffers[i], in_sems.at[at])
         results = [Output(None, ref, None) for ref in targets]
         for at, i in enumerate(sent):
             results[i] = Output(targets[i], out_buffers[at], out_sems.at[at])
@@ -473,20 +480,21 @@
         out_shape=[
             pltpu.VMEM(shape, F32) if i in held else jax.ShapeDtypeStruct(shape, F32)
             for i, shape in enumerate(outs)
-        ],
+        ]
+        + [pltpu.VMEM(shapes[i], values[i].dtype) for i in keep],
         in_specs=[VMEM if isinstance(x, Held) else ANY for x in arrays],
-        out_specs=[VMEM if i in held else ANY for i in range(n_out)],
+        out_specs=[VMEM if i in held else ANY for i in range(n_out)] + [VMEM] * len(keep),
         scratch_shapes=[pltpu.VMEM(shapes[i], values[i].dtype) for i in moved]
         + [pltpu.VMEM(outs[i], F32) for i in sent]
         + [pltpu.VMEM(shape, dtype) for shape, dtype in scratch]
         + [
-            pltpu.SemaphoreType.DMA((max(len(moved), 1),)),
+            pltpu.SemaphoreType.DMA((max(len(fetched), 1),)),
             pltpu.SemaphoreType.DMA((max(len(sent), 1),)),
         ],
         compiler_params=pltpu.CompilerParams(vmem_limit_bytes=40 << 20),
         name=name,
     )(*values)
-    return [Held(x) if i in held else x for i, x in enumerate(results)]
+    return [Held(x) if i in held or i >= n_out else x for i, x in enumerate(results)]
 
 
 def on_device(
@@ -535,44 +543,71 @@
     sums = ((4 * ROWS, COLS), F32)
     table = ((4 * ROWS, COLS), BF)
     packet = (devices, 1, PACKET)
-    (terms,) = call(drive_kernel, "drive", [taps, samples], [(devices, 8, LANES)], [], window, (0,))
+    terms, connect0, now0_held, now1_held = call(
+        drive_kernel,
+        "drive",
+        [taps, connect, now0, now1, samples],
+        [(devices, 8, LANES)],
+        [],
+        window,
+        held=(0,),
+        keep=(1, 2, 3),
+    )
     drive = trade(terms)
-    back, partial = call(
+    back, partial, surface0, driver0, links0 = call(
         first_kernel,
         "operator0",
-        [connect, now0, now1, surface, driver_row, metric, weights, narrow, wide],
+        [connect0, now0_held, now1_held, surface, driver_row, metric, weights, narrow, wide, links],
         [elements[0], (1, LANES)],
         [elements, table],
         held=(0, 1),
+        keep=(3, 4, 9),
     )
     local, send = call(
         functools.partial(second_kernel, sizes=sizes),
         "assemble0",
-        [drive, surface, driver_row, back, connect, partial, links],
+        [drive, surface0, driver0, back, connect0, partial, links0],
         [nodes, packet],
         [elements, sums, table],
         held=(0, 1),
     )
     other = swap(local)
     recv0 = trade(send)
+    base, *rest = call(
+        base_kernel,
+        "base0",
+        [local, other, mass, now0, now1, prev0, prev1, links, connect],
+        [nodes],
+        [],
+        held=(0,),
+        keep=(2, 7, 8),
+    )
     current, local, send = call(
         functools.partial(third_kernel, sizes=sizes),
         "step1",
-        [recv0, links, now0, now1, prev0, prev1, mass, local, other]
-        + [connect, surface, driver_row, metric, weights, narrow, wide, drive],
+        [recv0, base, *rest, surface, driver_row, metric, weights, narrow, wide, drive],
         [nodes, nodes, packet],
         [elements, elements, elements, sums, table],
         held=(0, 1, 2),
     )
     other = swap(local)
     recv1 = trade(send)
+    base, mass1, links1, samples1 = call(
+        last_base_kernel,
+        "base1",
+        [local, other, mass, current, now0, now1, links, samples],
+        [nodes],
+        [],
+        window,
+        held=(0,),
+        keep=(2, 6, 7),
+    )
     out0, out1, grad = call(
         functools.partial(last_kernel, sizes=sizes, scale=1.0 / math.sqrt(NN * count * devices)),
         "finish",
-        [recv1, links, current, now0, now1, mass, local, other, recv0, samples],
+        [recv1, base, mass1, links1, recv0, samples1],
         [plane, plane, (8, taps.shape[1])],
         [],
-        window,
     )
     grad = grad[:, :width]
     return out0.reshape(1, -1), out1.reshape(1, -1), grad

time: 66.4 us -> 62.8 us (0.946)
  waiting for transfers between devices: 13.2 us -> 11.1 us
  Pallas kernels: 34.1 us -> 32.8 us
    all_to_all x3, waiting for transfers between devices: 11.1 us -> 8.96 us  [trade(): return Held(lax.all_to_all(x.value, ALL, 0, 0, tiled=True))]
    pallas_call x5 -> x7, Pallas kernels: 34.1 us -> 32.8 us  [call(): pl.pallas_call(kernel, out_shape=[pltpu.VMEM(shape, F32) if i in held els...]
  transfers between devices with their start and end apart: 5 -> 5, of which waited for: 4 -> 4; matrix products, arithmetic and copies ran while one was open for 0% -> 0% of each run, Pallas kernels for 13% -> 15%
where the time goes in v5:
time: 62.8 us; the launch traced here: 62.4 us
  Pallas kernels  32.8 us (52%)
  starting transfers between devices  17.7 us (28%)
  waiting for transfers between devices  11.1 us (18%)
  between operations  0.87 us (1%)
    pallas_call x7, Pallas kernels, call(): pl.pallas_call(kernel, out_shape=[pltpu.VMEM(shape, F32) if i in held els...  32.8 us
    all_to_all x3, starting transfers between devices, trade(): return Held(lax.all_to_all(x.value, ALL, 0, 0, tiled=True))  16.9 us
    all_to_all x3, waiting for transfers between devices, trade(): return Held(lax.all_to_all(x.value, ALL, 0, 0, tiled=True))  8.96 us
    ppermute x2, waiting for transfers between devices, swap(): return Held(lax.ppermute(x.value, 'chip', [(0, 1), (1, 0)]))  2.11 us
  transfers between devices with their start and end apart: 5, of which 4 were waited for; matrix products, arithmetic and copies ran while one was open for 0% of the time, Pallas kernels for 15%

profile of v5, /device:TPU:0, one launch (start us, length us, event | category | flops | bytes accessed | tf_op | source)
XLA Modules:
  0.0 62.4 jit_solution(8086942753903402291)
XLA Ops:
  0.6 1.7 %drive.1 = (f32[16,8,128]{2,1,0:T(8,128)}, s32[64,512]{1,0:T(8,128)S(1)}, f32[128,128]{1,0:T(8,128)S(1)}, f32[128,128]{1,0:T(8,128)S(1)}) custom-call(f32[8,128]{1,0:T(8,128)} %refs_0_.1, s32[64,512]{1,0:T(8,128)} %refs_8_.3, f32[128,128]{1,0:T(8,128)} %bitcast.9, f32[128,128]{1,0:T(8,128)} %bitcast.12, f32[2,2048]{1,0:T(2,128)} %refs_7_.4), custom_call_target="tpu_custom_call" | custom-call | tf_op jit(solution)/shard_map/drive/pallas_call | solution.py:478
  2.3 7.4 %all-to-all-start = ((f32[16,8,128]{2,1,0:T(8,128)}), f32[16,8,128]{2,1,0:T(8,128)S(1)}, u32[]{:S(2)}, u32[]{:S(2)}) async-start(f32[16,8,128]{2,1,0:T(8,128)} %get-tuple-element.28), calls=%async_computation | async-start | bytes 131072 | tf_op jit(solution)/shard_map/all_to_all | solution.py:536
  9.7 7.4 %operator0.1 = (f32[2,64,512]{2,1,0:T(8,128)S(1)}, f32[1,128]{1,0:T(1,128)S(1)}, f32[64,512]{1,0:T(8,128)S(1)}, s32[1,64]{1,0:T(1,128)S(1)}, s32[3,2,512]{2,1,0:T(2,128)S(1)}) custom-call(s32[64,512]{1,0:T(8,128)S(1)} %get-tuple-element.29.refs_0_.refs_4_, f32[128,128]{1,0:T(8,128)S(1)} %get-tuple-element.30.refs_1_, ...), custom_call_target="tpu_custom_call" | custom-call | tf_op jit(solution)/shard_map/operator0/pallas_call | solution.py:478
  17.1 0.0 all-to-all-done.refs_0_.refs_11_
  17.1 6.3 %assemble0.1 = (f32[2,128,128]{2,1,0:T(8,128)S(1)}, f32[16,1,1152]{2,1,0:T(1,128)}) custom-call(f32[16,8,128]{2,1,0:T(8,128)S(1)} %all-to-all-done.refs_0_.refs_11_, f32[64,512]{1,0:T(8,128)S(1)} %get-tuple-element.32.refs_1_, s32[1,64]{1,0:T(1,128)S(1)} %get-tuple-element.33.refs_2_, f32[2,64,512]{2,1,0:T(8,128)S(1)} %get-tuple-element.34.refs_3_, ...), custom_call_target="tpu_custom_call" | custom-call | tf_op jit(solution)/shard_map/assemble0/pallas_call | solution.py:478
  23.4 6.0 %all-to-all-start.1 = ((f32[16,1,1152]{2,1,0:T(1,128)}), f32[16,1,1152]{2,1,0:T(1,128)S(1)}, u32[]{:S(2)}, u32[]{:S(2)}) async-start(f32[16,1,1152]{2,1,0:T(1,128)} %get-tuple-element.37), calls=%async_computation.1 | async-start | bytes 147456 | tf_op jit(solution)/shard_map/all_to_all | solution.py:536
  29.4 0.5 collective-permute-start
  29.9 1.0 %collective-permute-done.refs_1_ = f32[2,128,128]{2,1,0:T(8,128)S(1)} collective-permute-done((f32[2,128,128]{2,1,0:T(8,128)S(1)}, f32[2,128,128]{2,1,0:T(8,128)S(1)}, u32[]{:S(2)}, u32[]{:S(2)}) %collective-permute-start) | collective-permute-done | bytes 131104 | tf_op jit(solution)/shard_map/ppermute | solution.py:539
  30.9 1.2 %base0.1 = (f32[2,128,128]{2,1,0:T(8,128)S(1)}, f32[128,128]{1,0:T(8,128)S(1)}, s32[3,2,512]{2,1,0:T(2,128)S(1)}, s32[64,512]{1,0:T(8,128)S(1)}) custom-call(f32[2,128,128]{2,1,0:T(8,128)S(1)} %get-tuple-element.38.refs_0_, f32[2,128,128]{2,1,0:T(8,128)S(1)} %collective-permute-done.refs_1_, f32[128,128]{1,0:T(8,128)} %bitcast.15, f32[128,128]{1,0:T(8,128)} %bitcast.10, ...), custom_call_target="tpu_custom_call" | custom-call | tf_op jit(solution)/shard_map/base0/pallas_call | solution.py:478
  32.1 4.4 %all-to-all-done.1.refs_0_.refs_4_ = f32[16,1,1152]{2,1,0:T(1,128)S(1)} async-done(((f32[16,1,1152]{2,1,0:T(1,128)}), f32[16,1,1152]{2,1,0:T(1,128)S(1)}, u32[]{:S(2)}, u32[]{:S(2)}) %all-to-all-start.1) | async-done | bytes 73760 | tf_op jit(solution)/shard_map/all_to_all | solution.py:536
  36.4 14.0 %step1.1 = (f32[2,128,128]{2,1,0:T(8,128)S(1)}, f32[2,128,128]{2,1,0:T(8,128)S(1)}, f32[16,1,1152]{2,1,0:T(1,128)}) custom-call(f32[16,1,1152]{2,1,0:T(1,128)S(1)} %all-to-all-done.1.refs_0_.refs_4_, f32[2,128,128]{2,1,0:T(8,128)S(1)} %get-tuple-element.39.refs_1_, f32[128,128]{1,0:T(8,128)S(1)} %get-tuple-element.40.refs_2_, ...), custom_call_target="tpu_custom_call" | custom-call | tf_op jit(solution)/shard_map/step1/pallas_call | solution.py:478
  50.5 3.5 %all-to-all-start.2 = ((f32[16,1,1152]{2,1,0:T(1,128)}), f32[16,1,1152]{2,1,0:T(1,128)S(1)}, u32[]{:S(2)}, u32[]{:S(2)}) async-start(f32[16,1,1152]{2,1,0:T(1,128)} %get-tuple-element.43), calls=%async_computation.2 | async-start | bytes 147456 | tf_op jit(solution)/shard_map/all_to_all | solution.py:536
  54.0 0.3 collective-permute-start.1
  54.3 1.1 %collective-permute-done.1.refs_1_ = f32[2,128,128]{2,1,0:T(8,128)S(1)} collective-permute-done((f32[2,128,128]{2,1,0:T(8,128)S(1)}, f32[2,128,128]{2,1,0:T(8,128)S(1)}, u32[]{:S(2)}, u32[]{:S(2)}) %collective-permute-start.1) | collective-permute-done | bytes 131104 | tf_op jit(solution)/shard_map/ppermute | solution.py:539
  55.4 1.0 %base1.1 = (f32[2,128,128]{2,1,0:T(8,128)S(1)}, f32[128,128]{1,0:T(8,128)S(1)}, s32[3,2,512]{2,1,0:T(2,128)S(1)}, f32[2,128]{1,0:T(2,128)S(1)}) custom-call(f32[2,128,128]{2,1,0:T(8,128)S(1)} %get-tuple-element.44.refs_0_, f32[2,128,128]{2,1,0:T(8,128)S(1)} %collective-permute-done.1.refs_1_, f32[128,128]{1,0:T(8,128)} %bitcast.16, ...), custom_call_target="tpu_custom_call" | custom-call | tf_op jit(solution)/shard_map/base1/pallas_call | solution.py:478
  56.4 4.6 %all-to-all-done.2.refs_0_ = f32[16,1,1152]{2,1,0:T(1,128)S(1)} async-done(((f32[16,1,1152]{2,1,0:T(1,128)}), f32[16,1,1152]{2,1,0:T(1,128)S(1)}, u32[]{:S(2)}, u32[]{:S(2)}) %all-to-all-start.2) | async-done | bytes 73760 | tf_op jit(solution)/shard_map/all_to_all | solution.py:536
  61.0 1.3 %finish.1 = (f32[128,128]{1,0:T(8,128)}, f32[128,128]{1,0:T(8,128)}, f32[8,128]{1,0:T(8,128)}) custom-call(f32[16,1,1152]{2,1,0:T(1,128)S(1)} %all-to-all-done.2.refs_0_, f32[2,128,128]{2,1,0:T(8,128)S(1)} %get-tuple-element.46.refs_1_, f32[128,128]{1,0:T(8,128)S(1)} %get-tuple-element.47.refs_2_, s32[3,2,512]{2,1,0:T(2,128)S(1)} %get-tuple-element.48.refs_3_, ...), custom_call_target="tpu_custom_call" | custom-call | tf_op jit(solution)/shard_map/finish/pallas_call | solution.py:478
Async XLA Ops:
  2.3 14.8 %all-to-all-start = ((f32[16,8,128]{2,1,0:T(8,128)}), f32[16,8,128]{2,1,0:T(8,128)S(1)}, u32[]{:S(2)}, u32[]{:S(2)}) async-start(f32[16,8,128]{2,1,0:T(8,128)} %get-tuple-element.28), calls=%async_computation | async-start | bytes 131072 | tf_op jit(solution)/shard_map/all_to_all | solution.py:536
  23.4 13.0 %all-to-all-start.1 = ((f32[16,1,1152]{2,1,0:T(1,128)}), f32[16,1,1152]{2,1,0:T(1,128)S(1)}, u32[]{:S(2)}, u32[]{:S(2)}) async-start(f32[16,1,1152]{2,1,0:T(1,128)} %get-tuple-element.37), calls=%async_computation.1 | async-start | bytes 147456 | tf_op jit(solution)/shard_map/all_to_all | solution.py:536
  29.4 1.4 %collective-permute-start = (f32[2,128,128]{2,1,0:T(8,128)S(1)}, f32[2,128,128]{2,1,0:T(8,128)S(1)}, u32[]{:S(2)}, u32[]{:S(2)}) collective-permute-start(f32[2,128,128]{2,1,0:T(8,128)S(1)} %get-tuple-element.38.refs_0_), channel_id=1, source_target_pairs={{0,1},{1,0},{2,3},{3,2},{4,5},{5,4},{6,7},{7,6},{8,9},{9,8},{10,11... | collective-permute-start | bytes 393224 | tf_op jit(solution)/shard_map/ppermute | solution.py:539
  50.5 10.5 %all-to-all-start.2 = ((f32[16,1,1152]{2,1,0:T(1,128)}), f32[16,1,1152]{2,1,0:T(1,128)S(1)}, u32[]{:S(2)}, u32[]{:S(2)}) async-start(f32[16,1,1152]{2,1,0:T(1,128)} %get-tuple-element.43), calls=%async_computation.2 | async-start | bytes 147456 | tf_op jit(solution)/shard_map/all_to_all | solution.py:536
  54.0 1.4 %collective-permute-start.1 = (f32[2,128,128]{2,1,0:T(8,128)S(1)}, f32[2,128,128]{2,1,0:T(8,128)S(1)}, u32[]{:S(2)}, u32[]{:S(2)}) collective-permute-start(f32[2,128,128]{2,1,0:T(8,128)S(1)} %get-tuple-element.44.refs_0_), channel_id=1, source_target_pairs={{0,1},{1,0},{2,3},{3,2},{4,5},{5,4},{6,7},{7,6},{8,9},{9,8},{10,11... | collective-permute-start | bytes 393224 | tf_op jit(solution)/shard_map/ppermute | solution.py:539

commit v6 on v5

--- a/solution.py
+++ b/solution.py
@@ -62,11 +62,10 @@
         return high, low
 
     wide = list(parts(along_x)) + list(parts(along_x.T))
-    narrow = []
-    for table in (along_y, along_z, along_y.T, along_z.T):
-        narrow += parts(table)
+    forward = parts(np.concatenate([along_y, along_z], axis=1))
+    backward = parts(np.concatenate([along_y.T, along_z.T], axis=0))
     weights = np.concatenate([cube] * 3).astype(np.float32)[None, :]
-    return np.stack(wide), np.stack(narrow), weights
+    return np.stack(wide), np.stack(forward), np.stack(backward), weights
 
 
 def halves(x):
@@ -176,65 +175,45 @@
         lax.fori_loop(0, count // BLOCK, body, 0)
 
 
-def operator(vals_ref, metric, weights, wide, narrow, back_ref):
+def operator(vals_ref, metric, weights, narrow, narrow_back, wide, back_ref):
     count = vals_ref.shape[1]
     vals = jnp.concatenate([vals_ref[0], vals_ref[1]], axis=0)
-    stacked = stack_halves(vals)
-    metric_ref, weights_ref = metric(), weights()
-    total = None
-    for i in (1, 2, 0):
-        scale = metric_ref[:, i * NN : (i + 1) * NN] * weights_ref[:, i * NN : (i + 1) * NN]
-        scale = jnp.concatenate([scale, scale], axis=0)
-        if i == 0:
-            table = wide()
-            part = times(times(vals, table[0], table[1]) * scale, table[2], table[3])
-        else:
-            table = narrow()
-            at = 2 * (i - 1)
-            grads = times(stacked, table[at], table[at + 1]) * stack_halves(scale)
-            part = unstack_halves(times(grads, table[at + 4], table[at + 5]))
-        total = part if total is None else total + part
+    scale = metric()[...] * weights()[...]
+    scale = jnp.concatenate([scale, scale], axis=0)
+    along = [scale[:, i * NN : (i + 1) * NN] for i in range(3)]
+    table = narrow()
+    grads = times(stack_halves(vals), table[0], table[1])
+    grads = grads * jnp.concatenate([stack_halves(x) for x in along[1:]], axis=1)
+    table = narrow_back()
+    total = unstack_halves(times(grads, table[0], table[1]))
+    table = wide()
+    total += times(times(vals, table[0], table[1]) * along[0], table[2], table[3])
     back_ref[0] = total[:count]
     back_ref[1] = total[count:]
 
 
 def driver_hot(driver_ref):
     count = driver_ref.shape[1]
-    return (lax.broadcasted_iota(jnp.int32, (8, count), 0) == driver_ref[...]).astype(F32)
-
-
-def driver_sums(vals_ref, surface_ref, driver_ref):
+    ids = lax.broadcasted_iota(jnp.int32, (LANES, count), 0)
+    return ((ids == driver_ref[...]) & (ids < 8)).astype(F32).T
+
+
+def driver_sums(vals_ref, surface_ref, hot):
     products = surface_ref[...] * vals_ref[1]
     products = sum(products[:, i * LANES : (i + 1) * LANES] for i in range(NN // LANES))
-    lanes = (((1,), (1,)), ((), ()))
-    per_element = lax.dot_general(
-        jnp.ones((8, LANES), F32),
-        products,
-        lanes,
-        precision=lax.Precision.HIGHEST,
-        preferred_element_type=F32,
-    )
-    count = driver_ref.shape[1]
-    hot = lax.broadcasted_iota(jnp.int32, (LANES, count), 0) == driver_ref[...]
-    hot = (hot & (lax.broadcasted_iota(jnp.int32, (LANES, count), 0) < 8)).astype(F32)
-    return lax.dot_general(
-        per_element, hot, lanes, precision=lax.Precision.HIGHEST, preferred_element_type=F32
-    )[:1]
-
-
-def residual(step, drive_ref, surface_ref, driver_ref, back_ref, res_ref):
+    return jnp.sum(hot * jnp.sum(products, axis=1, keepdims=True), axis=0, keepdims=True)
+
+
+def amplitudes(step, drive_ref, hot):
     terms = jnp.sum(drive_ref[...], axis=0)
     half = lax.broadcasted_iota(jnp.int32, (8, LANES), 1) >> 6
-    terms = jnp.where(half == step, terms, 0.0)
-    drive = jnp.broadcast_to(jnp.sum(terms, axis=1, keepdims=True), (8, LANES))
-    amplitude = lax.dot_general(
-        driver_hot(driver_ref),
-        drive,
-        (((0,), (0,)), ((), ())),
-        precision=lax.Precision.HIGHEST,
-        preferred_element_type=F32,
-    )
-    amplitude = jnp.concatenate([amplitude] * (NN // LANES), axis=1)
+    drive = jnp.sum(jnp.where(half == step, terms, 0.0), axis=1, keepdims=True)
+    ids = [lax.broadcasted_iota(jnp.int32, (8, LANES), axis) for axis in range(2)]
+    row = jnp.sum(jnp.where(ids[0] == ids[1], drive, 0.0), axis=0, keepdims=True)
+    return jnp.sum(hot * row, axis=1, keepdims=True)
+
+
+def residual(amplitude, surface_ref, back_ref, res_ref):
     res_ref[0] = amplitude * surface_ref[...] - back_ref[0]
     res_ref[1] = -back_ref[1]
 
@@ -329,13 +308,13 @@
 
 
 def first_kernel(ins, outs, scratch):
-    connect, now0, now1, surface, driver, metric, weights, narrow, wide = ins[:9]
+    connect, now0, now1, surface, driver, metric, weights, narrow, narrow_back, wide = ins[:10]
     back, partial = outs
     vals, table = scratch
     fill_table(table, [now0()[...], now1()[...]])
     gather_all(table, connect(), vals)
-    partial[...] = driver_sums(vals, surface(), driver())
-    operator(vals, metric, weights, wide, narrow, back)
+    partial[...] = driver_sums(vals, surface(), driver_hot(driver()))
+    operator(vals, metric, weights, narrow, narrow_back, wide, back)
 
 
 def local_sums(res, connect, shared, partial, local, send, sums, table, sizes):
@@ -352,12 +331,12 @@
     drive, surface, driver, back, connect, partial, shared = ins
     local, send = outs
     res, sums, table = scratch
-    residual(0, drive(), surface(), driver(), back(), res)
+    residual(amplitudes(0, drive(), driver_hot(driver())), surface(), back(), res)
     local_sums(res, connect(), shared(), partial()[...], local, send, sums, table, sizes)
 
 
 def third_kernel(ins, outs, scratch, *, sizes):
-    recv, base, mass, shared, connect, surface, driver, metric, weights, narrow, wide, drive = ins
+    recv, base, mass, shared, connect, surface, driver, metric, weights, narrow, narrow_back, wide, drive = ins
     current, local, send = outs
     vals, back, res, sums, table = scratch
     received = received_sums(shared(), recv(), **sizes)
@@ -366,10 +345,12 @@
         current[k] = fields[k]
     current.flush()
     fill_table(table, fields)
+    hot = driver_hot(driver())
+    amplitude = amplitudes(1, drive(), hot)
     gather_all(table, connect(), vals)
-    partial = driver_sums(vals, surface(), driver())
-    operator(vals, metric, weights, wide, narrow, back)
-    residual(1, drive(), surface(), driver(), back, res)
+    partial = driver_sums(vals, surface(), hot)
+    operator(vals, metric, weights, narrow, narrow_back, wide, back)
+    residual(amplitude, surface(), back, res)
     local_sums(res, connect(), shared(), partial, local, send, sums, table, sizes)
 
 
@@ -511,7 +492,7 @@
     filter_taps,
     signal,
 ):
-    wide, narrow, weights = (jnp.asarray(t) for t in element_tables())
+    wide, narrow, narrow_back, weights = (jnp.asarray(t) for t in element_tables())
     count = connect.shape[0]
     peers = shared.shape[2]
     doms = lax.axis_size("dom")
@@ -557,11 +538,11 @@
     back, partial, surface0, driver0, links0 = call(
         first_kernel,
         "operator0",
-        [connect0, now0_held, now1_held, surface, driver_row, metric, weights, narrow, wide, links],
+        [connect0, now0_held, now1_held, surface, driver_row, metric, weights, narrow, narrow_back, wide, links],
         [elements[0], (1, LANES)],
         [elements, table],
         held=(0, 1),
-        keep=(3, 4, 9),
+        keep=(3, 4, 10),
     )
     local, send = call(
         functools.partial(second_kernel, sizes=sizes),
@@ -576,16 +557,17 @@
     base, *rest = call(
         base_kernel,
         "base0",
-        [local, other, mass, now0, now1, prev0, prev1, links, connect],
+        [local, other, mass, now0, now1, prev0, prev1, links, connect, surface, driver_row]
+        + [metric, weights, narrow, narrow_back],
         [nodes],
         [],
         held=(0,),
-        keep=(2, 7, 8),
+        keep=(2, 7, 8, 9, 10, 11, 12, 13, 14),
     )
     current, local, send = call(
         functools.partial(third_kernel, sizes=sizes),
         "step1",
-        [recv0, base, *rest, surface, driver_row, metric, weights, narrow, wide, drive],
+        [recv0, base, *rest, wide, drive],
         [nodes, nodes, packet],
         [elements, elements, elements, sums, table],
         held=(0, 1, 2),

time: 62.8 us -> 62.3 us (level)
  waiting for transfers between devices: 11.1 us -> 10.4 us
  transfers between devices with their start and end apart: 5 -> 5, of which waited for: 4 -> 4; matrix products, arithmetic and copies ran while one was open for 0% -> 0% of each run, Pallas kernels for 15% -> 16%
where the time goes in v6:
time: 62.3 us; the launch traced here: 61.9 us
  Pallas kernels  32.9 us (53%)
  starting transfers between devices  17.7 us (28%)
  waiting for transfers between devices  10.4 us (17%)
  between operations  0.87 us (1%)
    pallas_call x7, Pallas kernels, call(): pl.pallas_call(kernel, out_shape=[pltpu.VMEM(shape, F32) if i in held els...  32.9 us
    all_to_all x3, starting transfers between devices, trade(): return Held(lax.all_to_all(x.value, ALL, 0, 0, tiled=True))  16.9 us
    all_to_all x3, waiting for transfers between devices, trade(): return Held(lax.all_to_all(x.value, ALL, 0, 0, tiled=True))  8.34 us
    ppermute x2, waiting for transfers between devices, swap(): return Held(lax.ppermute(x.value, 'chip', [(0, 1), (1, 0)]))  2.11 us
  transfers between devices with their start and end apart: 5, of which 4 were waited for; matrix products, arithmetic and copies ran while one was open for 0% of the time, Pallas kernels for 16%

profile of v6, /device:TPU:0, one launch (start us, length us, event | category | flops | bytes accessed | tf_op | source)
XLA Modules:
  0.0 61.9 jit_solution(10562041532056827776)
XLA Ops:
  0.6 1.7 %drive.1 = (f32[16,8,128]{2,1,0:T(8,128)}, s32[64,512]{1,0:T(8,128)S(1)}, f32[128,128]{1,0:T(8,128)S(1)}, f32[128,128]{1,0:T(8,128)S(1)}) custom-call(f32[8,128]{1,0:T(8,128)} %refs_0_.1, s32[64,512]{1,0:T(8,128)} %refs_8_.2, f32[128,128]{1,0:T(8,128)} %bitcast.9, f32[128,128]{1,0:T(8,128)} %bitcast.12, f32[2,2048]{1,0:T(2,128)} %refs_7_.2), custom_call_target="tpu_custom_call" | custom-call | tf_op jit(solution)/shard_map/drive/pallas_call | solution.py:459
  2.3 7.4 %all-to-all-start = ((f32[16,8,128]{2,1,0:T(8,128)}), f32[16,8,128]{2,1,0:T(8,128)S(1)}, u32[]{:S(2)}, u32[]{:S(2)}) async-start(f32[16,8,128]{2,1,0:T(8,128)} %get-tuple-element.34), calls=%async_computation | async-start | bytes 131072 | tf_op jit(solution)/shard_map/all_to_all | solution.py:517
  9.7 7.4 %operator0.1 = (f32[2,64,512]{2,1,0:T(8,128)S(1)}, f32[1,128]{1,0:T(1,128)S(1)}, f32[64,512]{1,0:T(8,128)S(1)}, s32[1,64]{1,0:T(1,128)S(1)}, s32[3,2,512]{2,1,0:T(2,128)S(1)}) custom-call(s32[64,512]{1,0:T(8,128)S(1)} %get-tuple-element.35.refs_0_.refs_4_, f32[128,128]{1,0:T(8,128)S(1)} %get-tuple-element.36.refs_1_, ...), custom_call_target="tpu_custom_call" | custom-call | tf_op jit(solution)/shard_map/operator0/pallas_call | solution.py:459
  17.1 0.0 all-to-all-done.refs_0_.refs_12_
  17.1 6.2 %assemble0.1 = (f32[2,128,128]{2,1,0:T(8,128)S(1)}, f32[16,1,1152]{2,1,0:T(1,128)}) custom-call(f32[16,8,128]{2,1,0:T(8,128)S(1)} %all-to-all-done.refs_0_.refs_12_, f32[64,512]{1,0:T(8,128)S(1)} %get-tuple-element.38.refs_1_, s32[1,64]{1,0:T(1,128)S(1)} %get-tuple-element.39.refs_2_, f32[2,64,512]{2,1,0:T(8,128)S(1)} %get-tuple-element.40.refs_3_, ...), custom_call_target="tpu_custom_call" | custom-call | tf_op jit(solution)/shard_map/assemble0/pallas_call | solution.py:459
  23.3 6.0 %all-to-all-start.1 = ((f32[16,1,1152]{2,1,0:T(1,128)}), f32[16,1,1152]{2,1,0:T(1,128)S(1)}, u32[]{:S(2)}, u32[]{:S(2)}) async-start(f32[16,1,1152]{2,1,0:T(1,128)} %get-tuple-element.43), calls=%async_computation.1 | async-start | bytes 147456 | tf_op jit(solution)/shard_map/all_to_all | solution.py:517
  29.3 0.5 collective-permute-start
  29.8 1.0 %collective-permute-done.refs_1_ = f32[2,128,128]{2,1,0:T(8,128)S(1)} collective-permute-done((f32[2,128,128]{2,1,0:T(8,128)S(1)}, f32[2,128,128]{2,1,0:T(8,128)S(1)}, u32[]{:S(2)}, u32[]{:S(2)}) %collective-permute-start) | collective-permute-done | bytes 131104 | tf_op jit(solution)/shard_map/ppermute | solution.py:520
  30.8 1.8 %base0.1 = (f32[2,128,128]{2,1,0:T(8,128)S(1)}, f32[128,128]{1,0:T(8,128)S(1)}, s32[3,2,512]{2,1,0:T(2,128)S(1)}, s32[64,512]{1,0:T(8,128)S(1)}, f32[64,512]{1,0...) custom-call(f32[2,128,128]{2,1,0:T(8,128)S(1)} %get-tuple-element.44, ...), custom_call_target="tpu_custom_call" | custom-call | tf_op jit(solution)/shard_map/base0/pallas_call | solution.py:459
  32.6 3.8 %all-to-all-done.1.refs_0_.refs_4_ = f32[16,1,1152]{2,1,0:T(1,128)S(1)} async-done(((f32[16,1,1152]{2,1,0:T(1,128)}), f32[16,1,1152]{2,1,0:T(1,128)S(1)}, u32[]{:S(2)}, u32[]{:S(2)}) %all-to-all-start.1) | async-done | bytes 73760 | tf_op jit(solution)/shard_map/all_to_all | solution.py:517
  36.3 13.6 %step1.1 = (f32[2,128,128]{2,1,0:T(8,128)S(1)}, f32[2,128,128]{2,1,0:T(8,128)S(1)}, f32[16,1,1152]{2,1,0:T(1,128)}) custom-call(f32[16,1,1152]{2,1,0:T(1,128)S(1)} %all-to-all-done.1.refs_0_.refs_4_, f32[2,128,128]{2,1,0:T(8,128)S(1)} %get-tuple-element.45.refs_1_, f32[128,128]{1,0:T(8,128)S(1)} %get-tuple-element.46.refs_2_, ...), custom_call_target="tpu_custom_call" | custom-call | tf_op jit(solution)/shard_map/step1/pallas_call | solution.py:459
  49.9 3.5 %all-to-all-start.2 = ((f32[16,1,1152]{2,1,0:T(1,128)}), f32[16,1,1152]{2,1,0:T(1,128)S(1)}, u32[]{:S(2)}, u32[]{:S(2)}) async-start(f32[16,1,1152]{2,1,0:T(1,128)} %get-tuple-element.55), calls=%async_computation.2 | async-start | bytes 147456 | tf_op jit(solution)/shard_map/all_to_all | solution.py:517
  53.4 0.3 collective-permute-start.1
  53.7 1.1 %collective-permute-done.1.refs_1_ = f32[2,128,128]{2,1,0:T(8,128)S(1)} collective-permute-done((f32[2,128,128]{2,1,0:T(8,128)S(1)}, f32[2,128,128]{2,1,0:T(8,128)S(1)}, u32[]{:S(2)}, u32[]{:S(2)}) %collective-permute-start.1) | collective-permute-done | bytes 131104 | tf_op jit(solution)/shard_map/ppermute | solution.py:520
  54.8 1.0 %base1.1 = (f32[2,128,128]{2,1,0:T(8,128)S(1)}, f32[128,128]{1,0:T(8,128)S(1)}, s32[3,2,512]{2,1,0:T(2,128)S(1)}, f32[2,128]{1,0:T(2,128)S(1)}) custom-call(f32[2,128,128]{2,1,0:T(8,128)S(1)} %get-tuple-element.56.refs_0_, f32[2,128,128]{2,1,0:T(8,128)S(1)} %collective-permute-done.1.refs_1_, f32[128,128]{1,0:T(8,128)} %bitcast.16, ...), custom_call_target="tpu_custom_call" | custom-call | tf_op jit(solution)/shard_map/base1/pallas_call | solution.py:459
  55.8 4.6 %all-to-all-done.2.refs_0_ = f32[16,1,1152]{2,1,0:T(1,128)S(1)} async-done(((f32[16,1,1152]{2,1,0:T(1,128)}), f32[16,1,1152]{2,1,0:T(1,128)S(1)}, u32[]{:S(2)}, u32[]{:S(2)}) %all-to-all-start.2) | async-done | bytes 73760 | tf_op jit(solution)/shard_map/all_to_all | solution.py:517
  60.4 1.3 %finish.1 = (f32[128,128]{1,0:T(8,128)}, f32[128,128]{1,0:T(8,128)}, f32[8,128]{1,0:T(8,128)}) custom-call(f32[16,1,1152]{2,1,0:T(1,128)S(1)} %all-to-all-done.2.refs_0_, f32[2,128,128]{2,1,0:T(8,128)S(1)} %get-tuple-element.58.refs_1_, f32[128,128]{1,0:T(8,128)S(1)} %get-tuple-element.59.refs_2_, s32[3,2,512]{2,1,0:T(2,128)S(1)} %get-tuple-element.60.refs_3_, ...), custom_call_target="tpu_custom_call" | custom-call | tf_op jit(solution)/shard_map/finish/pallas_call | solution.py:459
Async XLA Ops:
  2.3 14.8 %all-to-all-start = ((f32[16,8,128]{2,1,0:T(8,128)}), f32[16,8,128]{2,1,0:T(8,128)S(1)}, u32[]{:S(2)}, u32[]{:S(2)}) async-start(f32[16,8,128]{2,1,0:T(8,128)} %get-tuple-element.34), calls=%async_computation | async-start | bytes 131072 | tf_op jit(solution)/shard_map/all_to_all | solution.py:517
  23.3 13.0 %all-to-all-start.1 = ((f32[16,1,1152]{2,1,0:T(1,128)}), f32[16,1,1152]{2,1,0:T(1,128)S(1)}, u32[]{:S(2)}, u32[]{:S(2)}) async-start(f32[16,1,1152]{2,1,0:T(1,128)} %get-tuple-element.43), calls=%async_computation.1 | async-start | bytes 147456 | tf_op jit(solution)/shard_map/all_to_all | solution.py:517
  29.3 1.4 %collective-permute-start = (f32[2,128,128]{2,1,0:T(8,128)S(1)}, f32[2,128,128]{2,1,0:T(8,128)S(1)}, u32[]{:S(2)}, u32[]{:S(2)}) collective-permute-start(f32[2,128,128]{2,1,0:T(8,128)S(1)} %get-tuple-element.44.refs_0_), channel_id=1, source_target_pairs={{0,1},{1,0},{2,3},{3,2},{4,5},{5,4},{6,7},{7,6},{8,9},{9,8},{10,11... | collective-permute-start | bytes 393224 | tf_op jit(solution)/shard_map/ppermute | solution.py:520
  49.9 10.5 %all-to-all-start.2 = ((f32[16,1,1152]{2,1,0:T(1,128)}), f32[16,1,1152]{2,1,0:T(1,128)S(1)}, u32[]{:S(2)}, u32[]{:S(2)}) async-start(f32[16,1,1152]{2,1,0:T(1,128)} %get-tuple-element.55), calls=%async_computation.2 | async-start | bytes 147456 | tf_op jit(solution)/shard_map/all_to_all | solution.py:517
  53.4 1.4 %collective-permute-start.1 = (f32[2,128,128]{2,1,0:T(8,128)S(1)}, f32[2,128,128]{2,1,0:T(8,128)S(1)}, u32[]{:S(2)}, u32[]{:S(2)}) collective-permute-start(f32[2,128,128]{2,1,0:T(8,128)S(1)} %get-tuple-element.56.refs_0_), channel_id=1, source_target_pairs={{0,1},{1,0},{2,3},{3,2},{4,5},{5,4},{6,7},{7,6},{8,9},{9,8},{10,11... | collective-permute-start | bytes 393224 | tf_op jit(solution)/shard_map/ppermute | solution.py:520

commit v7 on v6

--- a/solution.py
+++ b/solution.py
@@ -157,22 +157,42 @@
     ]
 
 
-def gather_all(table_ref, connect_ref, vals_ref):
+def gather_all(table_ref, connect_ref, vals_ref, row):
     count = connect_ref.shape[0]
     table = table_ref[...]
-
-    def body(i, carry):
-        for u in range(BLOCK):
-            e = i * BLOCK + u
+    last = count - 8
+    passes = 2
+    assert last % passes == 0
+    block, rows = last // passes, LANES // passes
+    blocks = range(NN // LANES)
+    links = [connect_ref[last:, i * LANES : (i + 1) * LANES] for i in blocks]
+
+    def body(i, found):
+        found = list(found)
+        done = 0
+        for u in range(block):
+            e = i * block + u
             pair = look_up(table, connect_ref[pl.ds(e, 1), :])
             for k in range(2):
                 vals_ref[k, pl.ds(e, 1), :] = pair[k]
-        return carry
-
-    if count == BLOCK:
-        body(0, 0)
-    else:
-        lax.fori_loop(0, count // BLOCK, body, 0)
+            upto = rows * (u + 1) // block
+            for h in range(done, upto):
+                node_row = i * rows + h
+                for k in range(2):
+                    values = jnp.broadcast_to(row(k, node_row), (8, LANES))
+                    for n in blocks:
+                        picked = jnp.take_along_axis(
+                            values, links[n] & (LANES - 1), axis=1, mode="promise_in_bounds"
+                        )
+                        at = 2 * n + k
+                        found[at] = jnp.where((links[n] >> 7) == node_row, picked, found[at])
+            done = upto
+        return tuple(found)
+
+    found = lax.fori_loop(0, passes, body, (jnp.zeros((8, LANES), F32),) * (2 * len(blocks)))
+    for n in blocks:
+        for k in range(2):
+            vals_ref[k, last:, n * LANES : (n + 1) * LANES] = found[2 * n + k]
 
 
 def operator(vals_ref, metric, weights, narrow, narrow_back, wide, back_ref):
@@ -312,7 +332,8 @@
     back, partial = outs
     vals, table = scratch
     fill_table(table, [now0()[...], now1()[...]])
-    gather_all(table, connect(), vals)
+    now = (now0(), now1())
+    gather_all(table, connect(), vals, lambda k, r: now[k][pl.ds(r, 1), :])
     partial[...] = driver_sums(vals, surface(), driver_hot(driver()))
     operator(vals, metric, weights, narrow, narrow_back, wide, back)
 
@@ -347,7 +368,7 @@
     fill_table(table, fields)
     hot = driver_hot(driver())
     amplitude = amplitudes(1, drive(), hot)
-    gather_all(table, connect(), vals)
+    gather_all(table, connect(), vals, lambda k, r: current.buffer[k, pl.ds(r, 1), :])
     partial = driver_sums(vals, surface(), hot)
     operator(vals, metric, weights, narrow, narrow_back, wide, back)
     residual(amplitude, surface(), back, res)

time: 62.3 us -> 61.8 us (level)
  no operation moved by 1% of the time
where the time goes in v7:
time: 61.8 us; the launch traced here: 61.4 us
  Pallas kernels  32.4 us (52%)
  starting transfers between devices  17.7 us (29%)
  waiting for transfers between devices  10.4 us (17%)
  between operations  0.87 us (1%)
    pallas_call x7, Pallas kernels, call(): pl.pallas_call(kernel, out_shape=[pltpu.VMEM(shape, F32) if i in held els...  32.4 us
    all_to_all x3, starting transfers between devices, trade(): return Held(lax.all_to_all(x.value, ALL, 0, 0, tiled=True))  16.9 us
    all_to_all x3, waiting for transfers between devices, trade(): return Held(lax.all_to_all(x.value, ALL, 0, 0, tiled=True))  8.34 us
    ppermute x2, waiting for transfers between devices, swap(): return Held(lax.ppermute(x.value, 'chip', [(0, 1), (1, 0)]))  2.11 us
  transfers between devices with their start and end apart: 5, of which 4 were waited for; matrix products, arithmetic and copies ran while one was open for 0% of the time, Pallas kernels for 16%

profile of v7, /device:TPU:0, one launch (start us, length us, event | category | flops | bytes accessed | tf_op | source)
XLA Modules:
  0.0 61.4 jit_solution(1108467237992275370)
XLA Ops:
  0.6 1.7 %drive.1 = (f32[16,8,128]{2,1,0:T(8,128)}, s32[64,512]{1,0:T(8,128)S(1)}, f32[128,128]{1,0:T(8,128)S(1)}, f32[128,128]{1,0:T(8,128)S(1)}) custom-call(f32[8,128]{1,0:T(8,128)} %refs_0_.1, s32[64,512]{1,0:T(8,128)} %refs_8_.2, f32[128,128]{1,0:T(8,128)} %bitcast.9, f32[128,128]{1,0:T(8,128)} %bitcast.12, f32[2,2048]{1,0:T(2,128)} %refs_7_.2), custom_call_target="tpu_custom_call" | custom-call | tf_op jit(solution)/shard_map/drive/pallas_call | solution.py:480
  2.3 7.4 %all-to-all-start = ((f32[16,8,128]{2,1,0:T(8,128)}), f32[16,8,128]{2,1,0:T(8,128)S(1)}, u32[]{:S(2)}, u32[]{:S(2)}) async-start(f32[16,8,128]{2,1,0:T(8,128)} %get-tuple-element.34), calls=%async_computation | async-start | bytes 131072 | tf_op jit(solution)/shard_map/all_to_all | solution.py:538
  9.7 7.1 %operator0.1 = (f32[2,64,512]{2,1,0:T(8,128)S(1)}, f32[1,128]{1,0:T(1,128)S(1)}, f32[64,512]{1,0:T(8,128)S(1)}, s32[1,64]{1,0:T(1,128)S(1)}, s32[3,2,512]{2,1,0:T(2,128)S(1)}) custom-call(s32[64,512]{1,0:T(8,128)S(1)} %get-tuple-element.35.refs_0_.refs_4_, f32[128,128]{1,0:T(8,128)S(1)} %get-tuple-element.36.refs_1_, ...), custom_call_target="tpu_custom_call" | custom-call | tf_op jit(solution)/shard_map/operator0/pallas_call | solution.py:480
  16.8 0.0 all-to-all-done.refs_0_.refs_12_
  16.8 6.2 %assemble0.1 = (f32[2,128,128]{2,1,0:T(8,128)S(1)}, f32[16,1,1152]{2,1,0:T(1,128)}) custom-call(f32[16,8,128]{2,1,0:T(8,128)S(1)} %all-to-all-done.refs_0_.refs_12_, f32[64,512]{1,0:T(8,128)S(1)} %get-tuple-element.38.refs_1_, s32[1,64]{1,0:T(1,128)S(1)} %get-tuple-element.39.refs_2_, f32[2,64,512]{2,1,0:T(8,128)S(1)} %get-tuple-element.40.refs_3_, ...), custom_call_target="tpu_custom_call" | custom-call | tf_op jit(solution)/shard_map/assemble0/pallas_call | solution.py:480
  23.1 6.0 %all-to-all-start.1 = ((f32[16,1,1152]{2,1,0:T(1,128)}), f32[16,1,1152]{2,1,0:T(1,128)S(1)}, u32[]{:S(2)}, u32[]{:S(2)}) async-start(f32[16,1,1152]{2,1,0:T(1,128)} %get-tuple-element.43), calls=%async_computation.1 | async-start | bytes 147456 | tf_op jit(solution)/shard_map/all_to_all | solution.py:538
  29.1 0.5 collective-permute-start
  29.6 1.0 %collective-permute-done.refs_1_ = f32[2,128,128]{2,1,0:T(8,128)S(1)} collective-permute-done((f32[2,128,128]{2,1,0:T(8,128)S(1)}, f32[2,128,128]{2,1,0:T(8,128)S(1)}, u32[]{:S(2)}, u32[]{:S(2)}) %collective-permute-start) | collective-permute-done | bytes 131104 | tf_op jit(solution)/shard_map/ppermute | solution.py:541
  30.5 1.8 %base0.1 = (f32[2,128,128]{2,1,0:T(8,128)S(1)}, f32[128,128]{1,0:T(8,128)S(1)}, s32[3,2,512]{2,1,0:T(2,128)S(1)}, s32[64,512]{1,0:T(8,128)S(1)}, f32[64,512]{1,0...) custom-call(f32[2,128,128]{2,1,0:T(8,128)S(1)} %get-tuple-element.44, ...), custom_call_target="tpu_custom_call" | custom-call | tf_op jit(solution)/shard_map/base0/pallas_call | solution.py:480
  32.3 3.8 %all-to-all-done.1.refs_0_.refs_4_ = f32[16,1,1152]{2,1,0:T(1,128)S(1)} async-done(((f32[16,1,1152]{2,1,0:T(1,128)}), f32[16,1,1152]{2,1,0:T(1,128)S(1)}, u32[]{:S(2)}, u32[]{:S(2)}) %all-to-all-start.1) | async-done | bytes 73760 | tf_op jit(solution)/shard_map/all_to_all | solution.py:538
  36.1 13.3 %step1.1 = (f32[2,128,128]{2,1,0:T(8,128)S(1)}, f32[2,128,128]{2,1,0:T(8,128)S(1)}, f32[16,1,1152]{2,1,0:T(1,128)}) custom-call(f32[16,1,1152]{2,1,0:T(1,128)S(1)} %all-to-all-done.1.refs_0_.refs_4_, f32[2,128,128]{2,1,0:T(8,128)S(1)} %get-tuple-element.45.refs_1_, f32[128,128]{1,0:T(8,128)S(1)} %get-tuple-element.46.refs_2_, ...), custom_call_target="tpu_custom_call" | custom-call | tf_op jit(solution)/shard_map/step1/pallas_call | solution.py:480
  49.5 3.5 %all-to-all-start.2 = ((f32[16,1,1152]{2,1,0:T(1,128)}), f32[16,1,1152]{2,1,0:T(1,128)S(1)}, u32[]{:S(2)}, u32[]{:S(2)}) async-start(f32[16,1,1152]{2,1,0:T(1,128)} %get-tuple-element.55), calls=%async_computation.2 | async-start | bytes 147456 | tf_op jit(solution)/shard_map/all_to_all | solution.py:538
  53.0 0.3 collective-permute-start.1
  53.3 1.1 %collective-permute-done.1.refs_1_ = f32[2,128,128]{2,1,0:T(8,128)S(1)} collective-permute-done((f32[2,128,128]{2,1,0:T(8,128)S(1)}, f32[2,128,128]{2,1,0:T(8,128)S(1)}, u32[]{:S(2)}, u32[]{:S(2)}) %collective-permute-start.1) | collective-permute-done | bytes 131104 | tf_op jit(solution)/shard_map/ppermute | solution.py:541
  54.4 1.0 %base1.1 = (f32[2,128,128]{2,1,0:T(8,128)S(1)}, f32[128,128]{1,0:T(8,128)S(1)}, s32[3,2,512]{2,1,0:T(2,128)S(1)}, f32[2,128]{1,0:T(2,128)S(1)}) custom-call(f32[2,128,128]{2,1,0:T(8,128)S(1)} %get-tuple-element.56.refs_0_, f32[2,128,128]{2,1,0:T(8,128)S(1)} %collective-permute-done.1.refs_1_, f32[128,128]{1,0:T(8,128)} %bitcast.16, ...), custom_call_target="tpu_custom_call" | custom-call | tf_op jit(solution)/shard_map/base1/pallas_call | solution.py:480
  55.4 4.6 %all-to-all-done.2.refs_0_ = f32[16,1,1152]{2,1,0:T(1,128)S(1)} async-done(((f32[16,1,1152]{2,1,0:T(1,128)}), f32[16,1,1152]{2,1,0:T(1,128)S(1)}, u32[]{:S(2)}, u32[]{:S(2)}) %all-to-all-start.2) | async-done | bytes 73760 | tf_op jit(solution)/shard_map/all_to_all | solution.py:538
  60.0 1.3 %finish.1 = (f32[128,128]{1,0:T(8,128)}, f32[128,128]{1,0:T(8,128)}, f32[8,128]{1,0:T(8,128)}) custom-call(f32[16,1,1152]{2,1,0:T(1,128)S(1)} %all-to-all-done.2.refs_0_, f32[2,128,128]{2,1,0:T(8,128)S(1)} %get-tuple-element.58.refs_1_, f32[128,128]{1,0:T(8,128)S(1)} %get-tuple-element.59.refs_2_, s32[3,2,512]{2,1,0:T(2,128)S(1)} %get-tuple-element.60.refs_3_, ...), custom_call_target="tpu_custom_call" | custom-call | tf_op jit(solution)/shard_map/finish/pallas_call | solution.py:480
Async XLA Ops:
  2.3 14.5 %all-to-all-start = ((f32[16,8,128]{2,1,0:T(8,128)}), f32[16,8,128]{2,1,0:T(8,128)S(1)}, u32[]{:S(2)}, u32[]{:S(2)}) async-start(f32[16,8,128]{2,1,0:T(8,128)} %get-tuple-element.34), calls=%async_computation | async-start | bytes 131072 | tf_op jit(solution)/shard_map/all_to_all | solution.py:538
  23.1 13.0 %all-to-all-start.1 = ((f32[16,1,1152]{2,1,0:T(1,128)}), f32[16,1,1152]{2,1,0:T(1,128)S(1)}, u32[]{:S(2)}, u32[]{:S(2)}) async-start(f32[16,1,1152]{2,1,0:T(1,128)} %get-tuple-element.43), calls=%async_computation.1 | async-start | bytes 147456 | tf_op jit(solution)/shard_map/all_to_all | solution.py:538
  29.1 1.4 %collective-permute-start = (f32[2,128,128]{2,1,0:T(8,128)S(1)}, f32[2,128,128]{2,1,0:T(8,128)S(1)}, u32[]{:S(2)}, u32[]{:S(2)}) collective-permute-start(f32[2,128,128]{2,1,0:T(8,128)S(1)} %get-tuple-element.44.refs_0_), channel_id=1, source_target_pairs={{0,1},{1,0},{2,3},{3,2},{4,5},{5,4},{6,7},{7,6},{8,9},{9,8},{10,11... | collective-permute-start | bytes 393224 | tf_op jit(solution)/shard_map/ppermute | solution.py:541
  49.5 10.5 %all-to-all-start.2 = ((f32[16,1,1152]{2,1,0:T(1,128)}), f32[16,1,1152]{2,1,0:T(1,128)S(1)}, u32[]{:S(2)}, u32[]{:S(2)}) async-start(f32[16,1,1152]{2,1,0:T(1,128)} %get-tuple-element.55), calls=%async_computation.2 | async-start | bytes 147456 | tf_op jit(solution)/shard_map/all_to_all | solution.py:538
  53.0 1.4 %collective-permute-start.1 = (f32[2,128,128]{2,1,0:T(8,128)S(1)}, f32[2,128,128]{2,1,0:T(8,128)S(1)}, u32[]{:S(2)}, u32[]{:S(2)}) collective-permute-start(f32[2,128,128]{2,1,0:T(8,128)S(1)} %get-tuple-element.56.refs_0_), channel_id=1, source_target_pairs={{0,1},{1,0},{2,3},{3,2},{4,5},{5,4},{6,7},{7,6},{8,9},{9,8},{10,11... | collective-permute-start | bytes 393224 | tf_op jit(solution)/shard_map/ppermute | solution.py:541

commit v8 on v7

--- a/solution.py
+++ b/solution.py
@@ -113,9 +113,12 @@
         table_ref[(2 + k) * ROWS : (3 + k) * ROWS] = low
 
 
-def look_up(table, index):
+def look_up_columns(table, index):
     row, column = split_index(index)
-    found = mm(table, column_hot(column))
+    return mm(table, column_hot(column)), row
+
+
+def pick_rows(found, row):
     found = found[: 2 * ROWS] + found[2 * ROWS :]
     mask = lax.broadcasted_iota(jnp.int32, (ROWS, NN), 0) == row
     return [
@@ -167,14 +170,21 @@
     blocks = range(NN // LANES)
     links = [connect_ref[last:, i * LANES : (i + 1) * LANES] for i in blocks]
 
+    def store(e, columns):
+        pair = pick_rows(*columns)
+        for k in range(2):
+            vals_ref[k, pl.ds(e, 1), :] = pair[k]
+
     def body(i, found):
         found = list(found)
         done = 0
+        columns = None
         for u in range(block):
             e = i * block + u
-            pair = look_up(table, connect_ref[pl.ds(e, 1), :])
-            for k in range(2):
-                vals_ref[k, pl.ds(e, 1), :] = pair[k]
+            before = columns
+            columns = look_up_columns(table, connect_ref[pl.ds(e, 1), :])
+            if before is not None:
+                store(e - 1, before)
             upto = rows * (u + 1) // block
             for h in range(done, upto):
                 node_row = i * rows + h
@@ -187,6 +197,7 @@
                         at = 2 * n + k
                         found[at] = jnp.where((links[n] >> 7) == node_row, picked, found[at])
             done = upto
+        store(i * block + block - 1, columns)
         return tuple(found)
 
     found = lax.fori_loop(0, passes, body, (jnp.zeros((8, LANES), F32),) * (2 * len(blocks)))
@@ -201,13 +212,13 @@
     scale = metric()[...] * weights()[...]
     scale = jnp.concatenate([scale, scale], axis=0)
     along = [scale[:, i * NN : (i + 1) * NN] for i in range(3)]
-    table = narrow()
-    grads = times(stack_halves(vals), table[0], table[1])
+    split, across, table = narrow(), narrow_back(), wide()
+    grads = times(stack_halves(vals), split[0], split[1])
+    along_x = times(vals, table[0], table[1])
     grads = grads * jnp.concatenate([stack_halves(x) for x in along[1:]], axis=1)
-    table = narrow_back()
-    total = unstack_halves(times(grads, table[0], table[1]))
-    table = wide()
-    total += times(times(vals, table[0], table[1]) * along[0], table[2], table[3])
+    along_x = along_x * along[0]
+    total = unstack_halves(times(grads, across[0], across[1]))
+    total += times(along_x, table[2], table[3])
     back_ref[0] = total[:count]
     back_ref[1] = total[count:]
 
@@ -266,9 +277,8 @@
     for q in range(send_ref.shape[0]):
         send_ref[q] = empty
     slots = [(o, j) for o in (0, 2, 1) for j in range(peers)]
-    packets = [
-        jnp.concatenate(look_up(table, shared_ref[o, j : j + 1, :]), axis=1) for o, j in slots
-    ]
+    columns = [look_up_columns(table, shared_ref[o, j : j + 1, :]) for o, j in slots]
+    packets = [jnp.concatenate(pick_rows(*found), axis=1) for found in columns]
     for (o, j), packet in zip(slots, packets):
         dom = jnp.clip(lax.axis_index("dom") + (o - 1), 0, doms - 1)
         for chip in range(2):

time: 61.8 us -> 60.4 us (0.977)
  Pallas kernels: 32.4 us -> 31 us
    pallas_call x7, Pallas kernels: 32.4 us -> 31 us  [call(): pl.pallas_call(kernel, out_shape=[pltpu.VMEM(shape, F32) if i in held els...]
  transfers between devices with their start and end apart: 5 -> 5, of which waited for: 4 -> 5; matrix products, arithmetic and copies ran while one was open for 0% -> 0% of each run, Pallas kernels for 16% -> 15%
where the time goes in v8:
time: 60.4 us; the launch traced here: 60 us
  Pallas kernels  31 us (51%)
  starting transfers between devices  17.1 us (28%)
  waiting for transfers between devices  11 us (18%)
  between operations  0.87 us (1%)
    pallas_call x7, Pallas kernels, call(): pl.pallas_call(kernel, out_shape=[pltpu.VMEM(shape, F32) if i in held els...  31 us
    all_to_all x3, starting transfers between devices, trade(): return Held(lax.all_to_all(x.value, ALL, 0, 0, tiled=True))  16.3 us
    all_to_all x3, waiting for transfers between devices, trade(): return Held(lax.all_to_all(x.value, ALL, 0, 0, tiled=True))  8.91 us
    ppermute x2, waiting for transfers between devices, swap(): return Held(lax.ppermute(x.value, 'chip', [(0, 1), (1, 0)]))  2.11 us
  transfers between devices with their start and end apart: 5, of which 5 were waited for; matrix products, arithmetic and copies ran while one was open for 0% of the time, Pallas kernels for 15%

profile of v8, /device:TPU:0, one launch (start us, length us, event | category | flops | bytes accessed | tf_op | source)
XLA Modules:
  0.0 60.0 jit_solution(16027117635922123099)
XLA Ops:
  0.6 1.7 %drive.1 = (f32[16,8,128]{2,1,0:T(8,128)}, s32[64,512]{1,0:T(8,128)S(1)}, f32[128,128]{1,0:T(8,128)S(1)}, f32[128,128]{1,0:T(8,128)S(1)}) custom-call(f32[8,128]{1,0:T(8,128)} %refs_0_.1, s32[64,512]{1,0:T(8,128)} %refs_8_.2, f32[128,128]{1,0:T(8,128)} %bitcast.9, f32[128,128]{1,0:T(8,128)} %bitcast.12, f32[2,2048]{1,0:T(2,128)} %refs_7_.2), custom_call_target="tpu_custom_call" | custom-call | tf_op jit(solution)/shard_map/drive/pallas_call | solution.py:490
  2.3 7.4 %all-to-all-start = ((f32[16,8,128]{2,1,0:T(8,128)}), f32[16,8,128]{2,1,0:T(8,128)S(1)}, u32[]{:S(2)}, u32[]{:S(2)}) async-start(f32[16,8,128]{2,1,0:T(8,128)} %get-tuple-element.34), calls=%async_computation | async-start | bytes 131072 | tf_op jit(solution)/shard_map/all_to_all | solution.py:548
  9.7 6.3 %operator0.1 = (f32[2,64,512]{2,1,0:T(8,128)S(1)}, f32[1,128]{1,0:T(1,128)S(1)}, f32[64,512]{1,0:T(8,128)S(1)}, s32[1,64]{1,0:T(1,128)S(1)}, s32[3,2,512]{2,1,0:T(2,128)S(1)}) custom-call(s32[64,512]{1,0:T(8,128)S(1)} %get-tuple-element.35.refs_0_.refs_4_, f32[128,128]{1,0:T(8,128)S(1)} %get-tuple-element.36.refs_1_, ...), custom_call_target="tpu_custom_call" | custom-call | tf_op jit(solution)/shard_map/operator0/pallas_call | solution.py:490
  16.0 0.6 all-to-all-done.refs_0_.refs_12_
  16.6 6.2 %assemble0.1 = (f32[2,128,128]{2,1,0:T(8,128)S(1)}, f32[16,1,1152]{2,1,0:T(1,128)}) custom-call(f32[16,8,128]{2,1,0:T(8,128)S(1)} %all-to-all-done.refs_0_.refs_12_, f32[64,512]{1,0:T(8,128)S(1)} %get-tuple-element.38.refs_1_, s32[1,64]{1,0:T(1,128)S(1)} %get-tuple-element.39.refs_2_, f32[2,64,512]{2,1,0:T(8,128)S(1)} %get-tuple-element.40.refs_3_, ...), custom_call_target="tpu_custom_call" | custom-call | tf_op jit(solution)/shard_map/assemble0/pallas_call | solution.py:490
  22.8 5.5 %all-to-all-start.1 = ((f32[16,1,1152]{2,1,0:T(1,128)}), f32[16,1,1152]{2,1,0:T(1,128)S(1)}, u32[]{:S(2)}, u32[]{:S(2)}) async-start(f32[16,1,1152]{2,1,0:T(1,128)} %get-tuple-element.43), calls=%async_computation.1 | async-start | bytes 147456 | tf_op jit(solution)/shard_map/all_to_all | solution.py:548
  28.3 0.5 collective-permute-start
  28.7 1.0 %collective-permute-done.refs_1_ = f32[2,128,128]{2,1,0:T(8,128)S(1)} collective-permute-done((f32[2,128,128]{2,1,0:T(8,128)S(1)}, f32[2,128,128]{2,1,0:T(8,128)S(1)}, u32[]{:S(2)}, u32[]{:S(2)}) %collective-permute-start) | collective-permute-done | bytes 131104 | tf_op jit(solution)/shard_map/ppermute | solution.py:551
  29.7 1.8 %base0.1 = (f32[2,128,128]{2,1,0:T(8,128)S(1)}, f32[128,128]{1,0:T(8,128)S(1)}, s32[3,2,512]{2,1,0:T(2,128)S(1)}, s32[64,512]{1,0:T(8,128)S(1)}, f32[64,512]{1,0...) custom-call(f32[2,128,128]{2,1,0:T(8,128)S(1)} %get-tuple-element.44, ...), custom_call_target="tpu_custom_call" | custom-call | tf_op jit(solution)/shard_map/base0/pallas_call | solution.py:490
  31.5 3.8 %all-to-all-done.1.refs_0_.refs_4_ = f32[16,1,1152]{2,1,0:T(1,128)S(1)} async-done(((f32[16,1,1152]{2,1,0:T(1,128)}), f32[16,1,1152]{2,1,0:T(1,128)S(1)}, u32[]{:S(2)}, u32[]{:S(2)}) %all-to-all-start.1) | async-done | bytes 73760 | tf_op jit(solution)/shard_map/all_to_all | solution.py:548
  35.3 12.8 %step1.1 = (f32[2,128,128]{2,1,0:T(8,128)S(1)}, f32[2,128,128]{2,1,0:T(8,128)S(1)}, f32[16,1,1152]{2,1,0:T(1,128)}) custom-call(f32[16,1,1152]{2,1,0:T(1,128)S(1)} %all-to-all-done.1.refs_0_.refs_4_, f32[2,128,128]{2,1,0:T(8,128)S(1)} %get-tuple-element.45.refs_1_, f32[128,128]{1,0:T(8,128)S(1)} %get-tuple-element.46.refs_2_, ...), custom_call_target="tpu_custom_call" | custom-call | tf_op jit(solution)/shard_map/step1/pallas_call | solution.py:490
  48.1 3.5 %all-to-all-start.2 = ((f32[16,1,1152]{2,1,0:T(1,128)}), f32[16,1,1152]{2,1,0:T(1,128)S(1)}, u32[]{:S(2)}, u32[]{:S(2)}) async-start(f32[16,1,1152]{2,1,0:T(1,128)} %get-tuple-element.55), calls=%async_computation.2 | async-start | bytes 147456 | tf_op jit(solution)/shard_map/all_to_all | solution.py:548
  51.6 0.3 collective-permute-start.1
  51.9 1.1 %collective-permute-done.1.refs_1_ = f32[2,128,128]{2,1,0:T(8,128)S(1)} collective-permute-done((f32[2,128,128]{2,1,0:T(8,128)S(1)}, f32[2,128,128]{2,1,0:T(8,128)S(1)}, u32[]{:S(2)}, u32[]{:S(2)}) %collective-permute-start.1) | collective-permute-done | bytes 131104 | tf_op jit(solution)/shard_map/ppermute | solution.py:551
  53.0 1.0 %base1.1 = (f32[2,128,128]{2,1,0:T(8,128)S(1)}, f32[128,128]{1,0:T(8,128)S(1)}, s32[3,2,512]{2,1,0:T(2,128)S(1)}, f32[2,128]{1,0:T(2,128)S(1)}) custom-call(f32[2,128,128]{2,1,0:T(8,128)S(1)} %get-tuple-element.56.refs_0_, f32[2,128,128]{2,1,0:T(8,128)S(1)} %collective-permute-done.1.refs_1_, f32[128,128]{1,0:T(8,128)} %bitcast.16, ...), custom_call_target="tpu_custom_call" | custom-call | tf_op jit(solution)/shard_map/base1/pallas_call | solution.py:490
  54.0 4.6 %all-to-all-done.2.refs_0_ = f32[16,1,1152]{2,1,0:T(1,128)S(1)} async-done(((f32[16,1,1152]{2,1,0:T(1,128)}), f32[16,1,1152]{2,1,0:T(1,128)S(1)}, u32[]{:S(2)}, u32[]{:S(2)}) %all-to-all-start.2) | async-done | bytes 73760 | tf_op jit(solution)/shard_map/all_to_all | solution.py:548
  58.5 1.3 %finish.1 = (f32[128,128]{1,0:T(8,128)}, f32[128,128]{1,0:T(8,128)}, f32[8,128]{1,0:T(8,128)}) custom-call(f32[16,1,1152]{2,1,0:T(1,128)S(1)} %all-to-all-done.2.refs_0_, f32[2,128,128]{2,1,0:T(8,128)S(1)} %get-tuple-element.58.refs_1_, f32[128,128]{1,0:T(8,128)S(1)} %get-tuple-element.59.refs_2_, s32[3,2,512]{2,1,0:T(2,128)S(1)} %get-tuple-element.60.refs_3_, ...), custom_call_target="tpu_custom_call" | custom-call | tf_op jit(solution)/shard_map/finish/pallas_call | solution.py:490
Async XLA Ops:
  2.3 14.3 %all-to-all-start = ((f32[16,8,128]{2,1,0:T(8,128)}), f32[16,8,128]{2,1,0:T(8,128)S(1)}, u32[]{:S(2)}, u32[]{:S(2)}) async-start(f32[16,8,128]{2,1,0:T(8,128)} %get-tuple-element.34), calls=%async_computation | async-start | bytes 131072 | tf_op jit(solution)/shard_map/all_to_all | solution.py:548
  22.8 12.5 %all-to-all-start.1 = ((f32[16,1,1152]{2,1,0:T(1,128)}), f32[16,1,1152]{2,1,0:T(1,128)S(1)}, u32[]{:S(2)}, u32[]{:S(2)}) async-start(f32[16,1,1152]{2,1,0:T(1,128)} %get-tuple-element.43), calls=%async_computation.1 | async-start | bytes 147456 | tf_op jit(solution)/shard_map/all_to_all | solution.py:548
  28.3 1.4 %collective-permute-start = (f32[2,128,128]{2,1,0:T(8,128)S(1)}, f32[2,128,128]{2,1,0:T(8,128)S(1)}, u32[]{:S(2)}, u32[]{:S(2)}) collective-permute-start(f32[2,128,128]{2,1,0:T(8,128)S(1)} %get-tuple-element.44.refs_0_), channel_id=1, source_target_pairs={{0,1},{1,0},{2,3},{3,2},{4,5},{5,4},{6,7},{7,6},{8,9},{9,8},{10,11... | collective-permute-start | bytes 393224 | tf_op jit(solution)/shard_map/ppermute | solution.py:551
  48.1 10.5 %all-to-all-start.2 = ((f32[16,1,1152]{2,1,0:T(1,128)}), f32[16,1,1152]{2,1,0:T(1,128)S(1)}, u32[]{:S(2)}, u32[]{:S(2)}) async-start(f32[16,1,1152]{2,1,0:T(1,128)} %get-tuple-element.55), calls=%async_computation.2 | async-start | bytes 147456 | tf_op jit(solution)/shard_map/all_to_all | solution.py:548
  51.6 1.4 %collective-permute-start.1 = (f32[2,128,128]{2,1,0:T(8,128)S(1)}, f32[2,128,128]{2,1,0:T(8,128)S(1)}, u32[]{:S(2)}, u32[]{:S(2)}) collective-permute-start(f32[2,128,128]{2,1,0:T(8,128)S(1)} %get-tuple-element.56.refs_0_), channel_id=1, source_target_pairs={{0,1},{1,0},{2,3},{3,2},{4,5},{5,4},{6,7},{7,6},{8,9},{9,8},{10,11... | collective-permute-start | bytes 393224 | tf_op jit(solution)/shard_map/ppermute | solution.py:551

commit v9 on v8

--- a/solution.py
+++ b/solution.py
@@ -344,8 +344,8 @@
     fill_table(table, [now0()[...], now1()[...]])
     now = (now0(), now1())
     gather_all(table, connect(), vals, lambda k, r: now[k][pl.ds(r, 1), :])
+    operator(vals, metric, weights, narrow, narrow_back, wide, back)
     partial[...] = driver_sums(vals, surface(), driver_hot(driver()))
-    operator(vals, metric, weights, narrow, narrow_back, wide, back)
 
 
 def local_sums(res, connect, shared, partial, local, send, sums, table, sizes):
@@ -379,8 +379,8 @@
     hot = driver_hot(driver())
     amplitude = amplitudes(1, drive(), hot)
     gather_all(table, connect(), vals, lambda k, r: current.buffer[k, pl.ds(r, 1), :])
+    operator(vals, metric, weights, narrow, narrow_back, wide, back)
     partial = driver_sums(vals, surface(), hot)
-    operator(vals, metric, weights, narrow, narrow_back, wide, back)
     residual(amplitude, surface(), back, res)
     local_sums(res, connect(), shared(), partial, local, send, sums, table, sizes)
 

time: 60.4 us -> 60.4 us (level)
  no operation moved by 1% of the time
where the time goes in v9:
time: 60.4 us; the launch traced here: 60 us
  Pallas kernels  31 us (51%)
  starting transfers between devices  17.1 us (28%)
  waiting for transfers between devices  11 us (18%)
  between operations  0.87 us (1%)
    pallas_call x7, Pallas kernels, call(): pl.pallas_call(kernel, out_shape=[pltpu.VMEM(shape, F32) if i in held els...  31 us
    all_to_all x3, starting transfers between devices, trade(): return Held(lax.all_to_all(x.value, ALL, 0, 0, tiled=True))  16.4 us
    all_to_all x3, waiting for transfers between devices, trade(): return Held(lax.all_to_all(x.value, ALL, 0, 0, tiled=True))  8.91 us
    ppermute x2, waiting for transfers between devices, swap(): return Held(lax.ppermute(x.value, 'chip', [(0, 1), (1, 0)]))  2.11 us
  transfers between devices with their start and end apart: 5, of which 5 were waited for; matrix products, arithmetic and copies ran while one was open for 0% of the time, Pallas kernels for 15%

profile of v9, /device:TPU:0, one launch (start us, length us, event | category | flops | bytes accessed | tf_op | source)
XLA Modules:
  0.0 60.0 jit_solution(3123590152815976115)
XLA Ops:
  0.6 1.7 %drive.1 = (f32[16,8,128]{2,1,0:T(8,128)}, s32[64,512]{1,0:T(8,128)S(1)}, f32[128,128]{1,0:T(8,128)S(1)}, f32[128,128]{1,0:T(8,128)S(1)}) custom-call(f32[8,128]{1,0:T(8,128)} %refs_0_.1, s32[64,512]{1,0:T(8,128)} %refs_8_.2, f32[128,128]{1,0:T(8,128)} %bitcast.9, f32[128,128]{1,0:T(8,128)} %bitcast.12, f32[2,2048]{1,0:T(2,128)} %refs_7_.2), custom_call_target="tpu_custom_call" | custom-call | tf_op jit(solution)/shard_map/drive/pallas_call | solution.py:490
  2.3 7.4 %all-to-all-start = ((f32[16,8,128]{2,1,0:T(8,128)}), f32[16,8,128]{2,1,0:T(8,128)S(1)}, u32[]{:S(2)}, u32[]{:S(2)}) async-start(f32[16,8,128]{2,1,0:T(8,128)} %get-tuple-element.34), calls=%async_computation | async-start | bytes 131072 | tf_op jit(solution)/shard_map/all_to_all | solution.py:548
  9.7 6.3 %operator0.1 = (f32[2,64,512]{2,1,0:T(8,128)S(1)}, f32[1,128]{1,0:T(1,128)S(1)}, f32[64,512]{1,0:T(8,128)S(1)}, s32[1,64]{1,0:T(1,128)S(1)}, s32[3,2,512]{2,1,0:T(2,128)S(1)}) custom-call(s32[64,512]{1,0:T(8,128)S(1)} %get-tuple-element.35.refs_0_.refs_4_, f32[128,128]{1,0:T(8,128)S(1)} %get-tuple-element.36.refs_1_, ...), custom_call_target="tpu_custom_call" | custom-call | tf_op jit(solution)/shard_map/operator0/pallas_call | solution.py:490
  16.0 0.6 all-to-all-done.refs_0_.refs_12_
  16.6 6.2 %assemble0.1 = (f32[2,128,128]{2,1,0:T(8,128)S(1)}, f32[16,1,1152]{2,1,0:T(1,128)}) custom-call(f32[16,8,128]{2,1,0:T(8,128)S(1)} %all-to-all-done.refs_0_.refs_12_, f32[64,512]{1,0:T(8,128)S(1)} %get-tuple-element.38.refs_1_, s32[1,64]{1,0:T(1,128)S(1)} %get-tuple-element.39.refs_2_, f32[2,64,512]{2,1,0:T(8,128)S(1)} %get-tuple-element.40.refs_3_, ...), custom_call_target="tpu_custom_call" | custom-call | tf_op jit(solution)/shard_map/assemble0/pallas_call | solution.py:490
  22.8 5.5 %all-to-all-start.1 = ((f32[16,1,1152]{2,1,0:T(1,128)}), f32[16,1,1152]{2,1,0:T(1,128)S(1)}, u32[]{:S(2)}, u32[]{:S(2)}) async-start(f32[16,1,1152]{2,1,0:T(1,128)} %get-tuple-element.43), calls=%async_computation.1 | async-start | bytes 147456 | tf_op jit(solution)/shard_map/all_to_all | solution.py:548
  28.3 0.5 collective-permute-start
  28.7 1.0 %collective-permute-done.refs_1_ = f32[2,128,128]{2,1,0:T(8,128)S(1)} collective-permute-done((f32[2,128,128]{2,1,0:T(8,128)S(1)}, f32[2,128,128]{2,1,0:T(8,128)S(1)}, u32[]{:S(2)}, u32[]{:S(2)}) %collective-permute-start) | collective-permute-done | bytes 131104 | tf_op jit(solution)/shard_map/ppermute | solution.py:551
  29.7 1.8 %base0.1 = (f32[2,128,128]{2,1,0:T(8,128)S(1)}, f32[128,128]{1,0:T(8,128)S(1)}, s32[3,2,512]{2,1,0:T(2,128)S(1)}, s32[64,512]{1,0:T(8,128)S(1)}, f32[64,512]{1,0...) custom-call(f32[2,128,128]{2,1,0:T(8,128)S(1)} %get-tuple-element.44, ...), custom_call_target="tpu_custom_call" | custom-call | tf_op jit(solution)/shard_map/base0/pallas_call | solution.py:490
  31.5 3.8 %all-to-all-done.1.refs_0_.refs_4_ = f32[16,1,1152]{2,1,0:T(1,128)S(1)} async-done(((f32[16,1,1152]{2,1,0:T(1,128)}), f32[16,1,1152]{2,1,0:T(1,128)S(1)}, u32[]{:S(2)}, u32[]{:S(2)}) %all-to-all-start.1) | async-done | bytes 73760 | tf_op jit(solution)/shard_map/all_to_all | solution.py:548
  35.3 12.7 %step1.1 = (f32[2,128,128]{2,1,0:T(8,128)S(1)}, f32[2,128,128]{2,1,0:T(8,128)S(1)}, f32[16,1,1152]{2,1,0:T(1,128)}) custom-call(f32[16,1,1152]{2,1,0:T(1,128)S(1)} %all-to-all-done.1.refs_0_.refs_4_, f32[2,128,128]{2,1,0:T(8,128)S(1)} %get-tuple-element.45.refs_1_, f32[128,128]{1,0:T(8,128)S(1)} %get-tuple-element.46.refs_2_, ...), custom_call_target="tpu_custom_call" | custom-call | tf_op jit(solution)/shard_map/step1/pallas_call | solution.py:490
  48.0 3.5 %all-to-all-start.2 = ((f32[16,1,1152]{2,1,0:T(1,128)}), f32[16,1,1152]{2,1,0:T(1,128)S(1)}, u32[]{:S(2)}, u32[]{:S(2)}) async-start(f32[16,1,1152]{2,1,0:T(1,128)} %get-tuple-element.55), calls=%async_computation.2 | async-start | bytes 147456 | tf_op jit(solution)/shard_map/all_to_all | solution.py:548
  51.5 0.3 collective-permute-start.1
  51.8 1.1 %collective-permute-done.1.refs_1_ = f32[2,128,128]{2,1,0:T(8,128)S(1)} collective-permute-done((f32[2,128,128]{2,1,0:T(8,128)S(1)}, f32[2,128,128]{2,1,0:T(8,128)S(1)}, u32[]{:S(2)}, u32[]{:S(2)}) %collective-permute-start.1) | collective-permute-done | bytes 131104 | tf_op jit(solution)/shard_map/ppermute | solution.py:551
  53.0 1.0 %base1.1 = (f32[2,128,128]{2,1,0:T(8,128)S(1)}, f32[128,128]{1,0:T(8,128)S(1)}, s32[3,2,512]{2,1,0:T(2,128)S(1)}, f32[2,128]{1,0:T(2,128)S(1)}) custom-call(f32[2,128,128]{2,1,0:T(8,128)S(1)} %get-tuple-element.56.refs_0_, f32[2,128,128]{2,1,0:T(8,128)S(1)} %collective-permute-done.1.refs_1_, f32[128,128]{1,0:T(8,128)} %bitcast.16, ...), custom_call_target="tpu_custom_call" | custom-call | tf_op jit(solution)/shard_map/base1/pallas_call | solution.py:490
  54.0 4.6 %all-to-all-done.2.refs_0_ = f32[16,1,1152]{2,1,0:T(1,128)S(1)} async-done(((f32[16,1,1152]{2,1,0:T(1,128)}), f32[16,1,1152]{2,1,0:T(1,128)S(1)}, u32[]{:S(2)}, u32[]{:S(2)}) %all-to-all-start.2) | async-done | bytes 73760 | tf_op jit(solution)/shard_map/all_to_all | solution.py:548
  58.5 1.3 %finish.1 = (f32[128,128]{1,0:T(8,128)}, f32[128,128]{1,0:T(8,128)}, f32[8,128]{1,0:T(8,128)}) custom-call(f32[16,1,1152]{2,1,0:T(1,128)S(1)} %all-to-all-done.2.refs_0_, f32[2,128,128]{2,1,0:T(8,128)S(1)} %get-tuple-element.58.refs_1_, f32[128,128]{1,0:T(8,128)S(1)} %get-tuple-element.59.refs_2_, s32[3,2,512]{2,1,0:T(2,128)S(1)} %get-tuple-element.60.refs_3_, ...), custom_call_target="tpu_custom_call" | custom-call | tf_op jit(solution)/shard_map/finish/pallas_call | solution.py:490
Async XLA Ops:
  2.3 14.3 %all-to-all-start = ((f32[16,8,128]{2,1,0:T(8,128)}), f32[16,8,128]{2,1,0:T(8,128)S(1)}, u32[]{:S(2)}, u32[]{:S(2)}) async-start(f32[16,8,128]{2,1,0:T(8,128)} %get-tuple-element.34), calls=%async_computation | async-start | bytes 131072 | tf_op jit(solution)/shard_map/all_to_all | solution.py:548
  22.8 12.5 %all-to-all-start.1 = ((f32[16,1,1152]{2,1,0:T(1,128)}), f32[16,1,1152]{2,1,0:T(1,128)S(1)}, u32[]{:S(2)}, u32[]{:S(2)}) async-start(f32[16,1,1152]{2,1,0:T(1,128)} %get-tuple-element.43), calls=%async_computation.1 | async-start | bytes 147456 | tf_op jit(solution)/shard_map/all_to_all | solution.py:548
  28.3 1.4 %collective-permute-start = (f32[2,128,128]{2,1,0:T(8,128)S(1)}, f32[2,128,128]{2,1,0:T(8,128)S(1)}, u32[]{:S(2)}, u32[]{:S(2)}) collective-permute-start(f32[2,128,128]{2,1,0:T(8,128)S(1)} %get-tuple-element.44.refs_0_), channel_id=1, source_target_pairs={{0,1},{1,0},{2,3},{3,2},{4,5},{5,4},{6,7},{7,6},{8,9},{9,8},{10,11... | collective-permute-start | bytes 393224 | tf_op jit(solution)/shard_map/ppermute | solution.py:551
  48.0 10.5 %all-to-all-start.2 = ((f32[16,1,1152]{2,1,0:T(1,128)}), f32[16,1,1152]{2,1,0:T(1,128)S(1)}, u32[]{:S(2)}, u32[]{:S(2)}) async-start(f32[16,1,1152]{2,1,0:T(1,128)} %get-tuple-element.55), calls=%async_computation.2 | async-start | bytes 147456 | tf_op jit(solution)/shard_map/all_to_all | solution.py:548
  51.5 1.4 %collective-permute-start.1 = (f32[2,128,128]{2,1,0:T(8,128)S(1)}, f32[2,128,128]{2,1,0:T(8,128)S(1)}, u32[]{:S(2)}, u32[]{:S(2)}) collective-permute-start(f32[2,128,128]{2,1,0:T(8,128)S(1)} %get-tuple-element.56.refs_0_), channel_id=1, source_target_pairs={{0,1},{1,0},{2,3},{3,2},{4,5},{5,4},{6,7},{7,6},{8,9},{9,8},{10,11... | collective-permute-start | bytes 393224 | tf_op jit(solution)/shard_map/ppermute | solution.py:551
